TPU v7x, 32 devices: a whole 2x2x4 slice. The times are simulated.
32 devices in a mesh: gx: 4 (over z), gy: 8 (over y, x, core).
Axes of the slice: x: 2, y: 2, z: 4, core: 2. Of those that a mesh axis runs over, the one named last changes fastest.
Arguments:
- fields: float32 [6, 128, 256, 128], P(None, 'gx', 'gy'), may hold values from -6 to 6
- eps_background: float32 [128, 256, 128], P('gx', 'gy'), may hold values from 1 to 4
- target: float32 [256, 256], replicated, may hold values from 1 to 10
- widths: float32 [4096], P(('gx', 'gy')), may hold values from 0.2 to 1
- intersection: float32 [4096, 16], P(('gx', 'gy')), may hold values from 0.1 to 1
- pillar_tile: int32 [4096, 1], P(('gx', 'gy')), may hold values from 0 to 31; in each aligned block of 128 rows (0 to 127, 128 to 255, ...) at most 8 rows name the same one
- anchors: int32 [4096, 2], P(('gx', 'gy')), may hold values from 0 to 28
Outputs:
- final_fields: float32 [6, 128, 256, 128], P(None, 'gx', 'gy')
- focal_power: float32 [256, 256], P(('gx', 'gy'))
- grad_widths: float32 [4096], P(('gx', 'gy'))
Inputs may be any that keep to these rules, and one draw needn't show every extreme that they name: `pillar_tile`: in the pillars of one device (aligned blocks of 128), no tile is named by more than 8 pillars, a bound that some block reaches. Tile t is the one at gx index t div (256 div 32) and gy index t mod (256 div 32).
All inputs are finite; a program needn't handle non-finite values.
Results may differ from a plain program's by a relative error of at most 0.00016.
Values sent between devices are 32-bit elements; how exact they have to be, the bound alone decides.
No kernel may reach another device: no remote copies, remote signals or barrier semaphores. Data moves between devices by JAX's collectives and lax.ppermute only.
A program may use at most 128 MiB of HBM per device.

v0:
```python
import math

import jax
import jax.numpy as jnp
from jax import lax
from jax.sharding import PartitionSpec as P

TILE = 32
P_DEV = 128
NT = 4
ZP = 4
U = 256
V = 256
ZM = 64


COURANT = 0.5
ANGULAR_STEP = 0.9
DELTA_EPS = 4.0


def passed_along(shard, axis, by):
    count = lax.axis_size(axis)
    pairs = [(i, i + by) for i in range(count) if 0 <= i + by < count]
    return lax.ppermute(shard, axis, pairs)


def plus_diff(field, rim_layer, axis):
    extended = jnp.concatenate([field, rim_layer], axis=axis)
    return lax.slice_in_dim(extended, 1, extended.shape[axis], axis=axis) - field


def minus_diff(field, rim_layer, axis):
    extended = jnp.concatenate([rim_layer, field], axis=axis)
    return field - lax.slice_in_dim(extended, 0, field.shape[axis], axis=axis)


def leap_step(fields_now, inv_eps, sources):
    elec_x, elec_y, elec_z, magn_x, magn_y, magn_z = fields_now
    z_blank = jnp.zeros_like(elec_x[:, :, :1])
    rim_east = passed_along(jnp.stack([elec_y[:1], elec_z[:1]]), "gx", -1)
    rim_north = passed_along(jnp.stack([elec_x[:, :1], elec_z[:, :1]]), "gy", -1)
    curl_x = plus_diff(elec_z, rim_north[1], 1) - plus_diff(elec_y, z_blank, 2)
    curl_y = plus_diff(elec_x, z_blank, 2) - plus_diff(elec_z, rim_east[1], 0)
    curl_z = plus_diff(elec_y, rim_east[0], 0) - plus_diff(elec_x, rim_north[0], 1)
    magn_x = magn_x - COURANT * curl_x
    magn_y = magn_y - COURANT * curl_y
    magn_z = magn_z - COURANT * curl_z
    rim_west = passed_along(jnp.stack([magn_y[-1:], magn_z[-1:]]), "gx", 1)
    rim_south = passed_along(jnp.stack([magn_x[:, -1:], magn_z[:, -1:]]), "gy", 1)
    curl_x = minus_diff(magn_z, rim_south[1], 1) - minus_diff(magn_y, z_blank, 2)
    curl_y = minus_diff(magn_x, z_blank, 2) - minus_diff(magn_z, rim_west[1], 0)
    curl_z = minus_diff(magn_y, rim_west[0], 0) - minus_diff(magn_x, rim_south[0], 1)
    elec_x = elec_x + COURANT * (curl_x - sources[0]) * inv_eps
    elec_y = elec_y + COURANT * (curl_y - sources[1]) * inv_eps
    elec_z = elec_z + COURANT * curl_z * inv_eps
    return (elec_x, elec_y, elec_z, magn_x, magn_y, magn_z)


def kernel_table(count_out, count_in, offset, length):
    focal_pos = (jnp.arange(count_out, dtype=jnp.float32) + 0.5) / count_out - 0.5
    cell_pos = (
        offset.astype(jnp.float32) + jnp.arange(length, dtype=jnp.float32) + 0.5
    ) / count_in - 0.5
    phase = math.pi * count_out * (focal_pos[:, None] - cell_pos[None, :]) ** 2
    return (jnp.cos(phase), jnp.sin(phase))


def contract(pattern, first_op, second_op):
    return jnp.einsum(pattern, first_op, second_op, precision=lax.Precision.HIGHEST)


def project_forward(mon_re, mon_im, table_x, table_y, norm_scale):
    x_re, x_im = table_x
    y_re, y_im = table_y
    part_re = contract("ux,cxy->cuy", x_re, mon_re) - contract("ux,cxy->cuy", x_im, mon_im)
    part_im = contract("ux,cxy->cuy", x_re, mon_im) + contract("ux,cxy->cuy", x_im, mon_re)
    far_re = contract("cuy,vy->cuv", part_re, y_re) - contract("cuy,vy->cuv", part_im, y_im)
    far_im = contract("cuy,vy->cuv", part_re, y_im) + contract("cuy,vy->cuv", part_im, y_re)
    return norm_scale * jnp.stack([far_re, far_im])


def project_back(weighted, table_x, table_y, norm_scale):
    x_re, x_im = table_x
    y_re, y_im = table_y
    w_re = weighted[0]
    w_im = weighted[1]
    half_re = contract("cuv,vy->cuy", w_re, y_re) - contract("cuv,vy->cuy", w_im, y_im)
    half_im = contract("cuv,vy->cuy", w_re, y_im) + contract("cuv,vy->cuy", w_im, y_re)
    back_re = contract("ux,cuy->cxy", x_re, half_re) - contract("ux,cuy->cxy", x_im, half_im)
    back_im = contract("ux,cuy->cxy", x_re, half_im) + contract("ux,cuy->cxy", x_im, half_re)
    return (2.0 * norm_scale * back_re, 2.0 * norm_scale * back_im)


def shards(fields, eps_background, target, widths, intersection, pillar_tile, anchors):
    span_x = lax.axis_size("gx")
    span_y = lax.axis_size("gy")
    devices = span_x * span_y
    place_x = lax.axis_index("gx")
    place_y = lax.axis_index("gy")
    linear = place_x * span_y + place_y
    offsets = jnp.arange(16, dtype=jnp.int32)
    capacity = 2 * max(1, P_DEV // devices)
    target_tile = pillar_tile[:, 0]
    onehot = (target_tile[:, None] == jnp.arange(devices, dtype=jnp.int32)[None, :]).astype(
        jnp.int32
    )
    earlier = jnp.cumsum(onehot, axis=0) - onehot
    order_in = jnp.sum(earlier * onehot, axis=1)
    slot_ids = target_tile * capacity + order_in
    packed = (
        jnp.zeros((devices * capacity, 16), jnp.float32)
        .at[slot_ids]
        .set(intersection * widths[:, None])
    )
    packed_at = (
        jnp.zeros((devices * capacity, 2), jnp.float32)
        .at[slot_ids]
        .set(anchors.astype(jnp.float32))
    )
    got_vals, got_at = (
        lax.all_to_all(
            packed.reshape(devices, capacity, 16),
            ("gx", "gy"),
            split_axis=0,
            concat_axis=0,
            tiled=True,
        ),
        lax.all_to_all(
            packed_at.reshape(devices, capacity, 2),
            ("gx", "gy"),
            split_axis=0,
            concat_axis=0,
            tiled=True,
        ),
    )
    local_vals = got_vals.reshape(devices * capacity, 16)
    local_at = got_at.reshape(devices * capacity, 2).astype(jnp.int32)
    cells_x = local_at[:, 0:1] + (offsets // 4)[None, :]
    cells_y = local_at[:, 1:2] + (offsets % 4)[None, :]
    filling = jnp.zeros((TILE, TILE), jnp.float32).at[cells_x, cells_y].add(local_vals)
    z_index = jnp.arange(fields.shape[3], dtype=jnp.int32)
    layers = ((z_index >= ZM - ZP) & (z_index < ZM)).astype(jnp.float32)
    permittivity = eps_background + DELTA_EPS * filling[:, :, None] * layers[None, None, :]
    inv_eps = 1.0 / permittivity
    blank = jnp.zeros_like(eps_background)
    fields_now = tuple((fields[component] for component in range(6)))
    mon_re = jnp.zeros((2, TILE, TILE), jnp.float32)
    mon_im = jnp.zeros((2, TILE, TILE), jnp.float32)
    changes = []
    for moment in range(1, NT + 1):
        before = fields_now[:3]
        fields_now = leap_step(fields_now, inv_eps, (blank, blank, blank))
        monitor = jnp.stack([fields_now[0][:, :, ZM], fields_now[1][:, :, ZM]])
        mon_re = mon_re + math.cos(ANGULAR_STEP * moment) * monitor
        mon_im = mon_im - math.sin(ANGULAR_STEP * moment) * monitor
        changes.append(
            tuple(
                (
                    (fields_now[component] - before[component])[:, :, ZM - ZP : ZM]
                    for component in range(3)
                )
            )
        )
    norm_scale = (TILE * span_x * TILE * span_y) ** (-0.5)
    table_x = kernel_table(U, TILE * span_x, place_x * TILE, TILE)
    table_y = kernel_table(V, TILE * span_y, place_y * TILE, TILE)
    row_count = U // devices
    row_start = linear * row_count
    partial_far = project_forward(mon_re, mon_im, table_x, table_y, norm_scale)
    far_field = lax.psum(partial_far, ("gx", "gy"))
    mine_rows = lax.dynamic_slice_in_dim(far_field, row_start, row_count, 2)
    focal_power = jnp.sum(mine_rows * mine_rows, axis=(0, 1))
    weighted = jnp.stack([target * far_field[0], -(target * far_field[1])])
    back_re, back_im = project_back(weighted, table_x, table_y, norm_scale)
    adjoint = tuple((blank for component in range(6)))
    inv_layer = inv_eps[:, :, ZM - ZP : ZM]
    grad_eps = jnp.zeros((TILE, TILE, ZP), jnp.float32)
    for moment in range(1, NT + 1):
        source_step = NT + 1 - moment
        adj_drive = (
            math.cos(ANGULAR_STEP * source_step) * back_re
            + math.sin(ANGULAR_STEP * source_step) * back_im
        )
        source_x = blank.at[:, :, ZM].set(adj_drive[0])
        source_y = blank.at[:, :, ZM].set(adj_drive[1])
        adjoint = leap_step(adjoint, inv_eps, (source_x, source_y, blank))
        change = changes[source_step - 1]
        product = (
            adjoint[0][:, :, ZM - ZP : ZM] * change[0]
            + adjoint[1][:, :, ZM - ZP : ZM] * change[1]
            + adjoint[2][:, :, ZM - ZP : ZM] * change[2]
        )
        grad_eps = grad_eps - product * inv_layer
    column_grad = jnp.sum(grad_eps, axis=2)
    picked = column_grad[cells_x, cells_y]
    returned = lax.all_to_all(
        picked.reshape(devices, capacity, 16), ("gx", "gy"), split_axis=0, concat_axis=0, tiled=True
    )
    own_vals = returned.reshape(devices * capacity, 16)[slot_ids]
    grad_widths = DELTA_EPS * jnp.sum(intersection * own_vals, axis=1)
    return (jnp.stack(fields_now), focal_power, grad_widths)


def solution(mesh):
    placed = (
        P(None, "gx", "gy", None),
        P("gx", "gy", None),
        P(),
        P(("gx", "gy")),
        P(("gx", "gy"), None),
        P(("gx", "gy"), None),
        P(("gx", "gy"), None),
    )
    return jax.shard_map(
        shards,
        mesh=mesh,
        in_specs=placed,
        out_specs=(P(None, "gx", "gy", None), P(("gx", "gy"), None), P(("gx", "gy"))),
        check_vma=False,
    )
```

profile of v0, /device:TPU:0, one launch (start us, length us, event | category | flops | bytes accessed | tf_op | source)
XLA Modules:
  0.0 417.5 jit_solution(3999675313294106621)
XLA Ops:
  15.7 10.3 %all-to-all-start = ((f32[32,8,2]{1,2,0:T(2,128)}), f32[32,8,2]{1,2,0:T(2,128)S(1)}, u32[]{:S(2)}, u32[]{:S(2)}) async-start(f32[32,8,2]{1,2,0:T(2,128)} %copy.4958), calls=%async_computation | async-start | bytes 65536 | tf_op jit(solution)/shard_map/all_to_all | solution.py:129
  36.0 8.0 %all-to-all-start.1 = ((f32[32,1,128]{2,1,0:T(1,128)}), f32[32,1,128]{2,1,0:T(1,128)S(1)}, u32[]{:S(2)}, u32[]{:S(2)}) async-start(f32[32,1,128]{2,1,0:T(1,128)} %reshape.526), calls=%async_computation.1 | async-start | bytes 32768 | tf_op jit(solution)/shard_map/all_to_all | solution.py:122
  45.6 5.5 %all-to-all-done.1 = f32[32,1,128]{2,1,0:T(1,128)S(1)} async-done(((f32[32,1,128]{2,1,0:T(1,128)}), f32[32,1,128]{2,1,0:T(1,128)S(1)}, u32[]{:S(2)}, u32[]{:S(2)}) %all-to-all-start.1) | async-done | bytes 16416 | tf_op jit(solution)/shard_map/all_to_all | solution.py:122
  52.6 28.8 %scatter_custom_fusion.2 = f32[1024]{0:T(1024)S(1)} fusion(s32[4096]{0:T(1024)S(1)} %reshape.500, f32[4096]{0:T(1024)S(1)} %reshape.502, f32[]{:T(128)} %constant.250.clone.1), kind=kCustom, calls=%fused_computation.635 | custom fusion | flops 4096 | bytes 4100
  89.3 2.8 collective-permute-start.3
  101.3 4.6 %collective-permute-done.4 = f32[2,1,32,128]{3,2,1,0:T(8,128)S(1)} collective-permute-done((f32[2,1,32,128]{3,2,1,0:T(8,128)S(1)}, f32[2,1,32,128]{3,2,1,0:T(8,128)S(1)}, u32[]{:S(2)}, u32[]{:S(2)}) %collective-permute-start.4) | collective-permute-done | bytes 32800 | tf_op jit(solution)/shard_map/ppermute | solution.py:25
  115.6 3.2 collective-permute-done.9
  120.8 3.2 collective-permute-start.11
  124.0 3.0 collective-permute-start.10
  132.1 3.7 collective-permute-done.13
  137.1 5.3 %collective-permute-start.14 = (f32[2,32,1,128]{3,1,2,0:T(8,128)S(1)}, f32[2,32,1,128]{3,1,2,0:T(8,128)S(1)}, u32[]{:S(2)}, u32[]{:S(2)}) collective-permute-start(f32[2,32,1,128]{3,1,2,0:T(8,128)S(1)} %pad_maximum_fusion.71), channel_id=1, source_target_pairs={{0,1},{1,2},{2,3},{3,4},{4,5},{5,6},{6,7},{8,9},{9,10},{10,11},{11... | collective-permute-start | bytes 98312 | tf_op jit(solution)/shard_map/ppermute | solution.py:25
  153.4 3.1 bitcast_dynamic-update-slice_fusion.3
  158.1 128.9 %all-reduce.45.cloned.1.call-done = f32[2,2,256,256]{3,2,1,0:T(8,128)} async-done(((f32[2,2,256,256]{3,2,1,0:T(8,128)}), f32[2,2,256,256]{3,2,1,0:T(8,128)}) %all-reduce.45.cloned.1.call-update) | async-done | bytes 1048592 | tf_op jit(solution)/shard_map/psum | solution.py:171
  298.3 3.0 fusion.94
  312.6 4.0 fusion.98
  316.7 4.5 %collective-permute-start.23 = (f32[2,1,32,128]{3,2,1,0:T(8,128)S(1)}, f32[2,1,32,128]{3,2,1,0:T(8,128)S(1)}, u32[]{:S(2)}, u32[]{:S(2)}) collective-permute-start(f32[2,1,32,128]{3,2,1,0:T(8,128)S(1)} %pad_maximum_fusion.82), channel_id=1, source_target_pairs={{0,8},{8,16},{16,24},{1,9},{9,17},{17,25},{2,10},{10,18},{18,26},{... | collective-permute-start | bytes 98312 | tf_op jit(solution)/shard_map/ppermute | solution.py:25
  333.5 3.3 collective-permute-start.27
  336.9 2.9 collective-permute-start.26
  344.1 3.9 collective-permute-done.29
  352.5 5.0 %collective-permute-start.30 = (f32[2,32,1,128]{3,1,2,0:T(8,128)S(1)}, f32[2,32,1,128]{3,1,2,0:T(8,128)S(1)}, u32[]{:S(2)}, u32[]{:S(2)}) collective-permute-start(f32[2,32,1,128]{3,1,2,0:T(8,128)S(1)} %pad_maximum_fusion.89), channel_id=1, source_target_pairs={{0,1},{1,2},{2,3},{3,4},{4,5},{5,6},{6,7},{8,9},{9,10},{10,11},{11... | collective-permute-start | bytes 98312 | tf_op jit(solution)/shard_map/ppermute | solution.py:25
  358.4 5.4 %fusion.147 = f32[32,32]{1,0:T(8,128)S(1)} fusion(f32[32,32,128]{2,1,0:T(8,128)S(1)} %copy-done.26, f32[32,32,128]{2,1,0:T(8,128)S(1)} %get-tuple-element.164, f32[1,32,128]{2,1,0:T(8,128)S(1)} %get-tuple-element.191, f32[32,32,128]{2,1,0:T(8,128)S(1)} %get-tuple-element.163, f32[32,1,128]{2,1,0:T(1,128)S(1)} %bitcast.474, ...), kind=kLoop, calls=%fused_computation.197 | loop fusion | flops 265216 | bytes 18419712 | tf_op jit(solution)/shard_map/reduce_sum | solution.py:195
  363.9 27.6 %gather_fusion = f32[4096]{0:T(1024)S(1)} fusion(f32[32,32]{0,1:T(8,128)S(1)} %copy.5037, s32[4096]{0:T(1024)S(1)} %reshape.470), kind=kCustom, calls=%fused_computation | custom fusion | bytes 65536 | tf_op jit(solution)/shard_map/gather | solution.py:196
  392.3 9.2 %all-to-all-start.2 = ((f32[32,1,128]{2,1,0:T(1,128)}), f32[32,1,128]{2,1,0:T(1,128)S(1)}, u32[]{:S(2)}, u32[]{:S(2)}) async-start(f32[32,1,128]{2,1,0:T(1,128)} %reshape.528), calls=%async_computation.2 | async-start | bytes 32768 | tf_op jit(solution)/shard_map/all_to_all | solution.py:197
  403.7 4.9 %all-to-all-done.2 = f32[32,1,128]{2,1,0:T(1,128)S(1)} async-done(((f32[32,1,128]{2,1,0:T(1,128)}), f32[32,1,128]{2,1,0:T(1,128)S(1)}, u32[]{:S(2)}, u32[]{:S(2)}) %all-to-all-start.2) | async-done | bytes 16416 | tf_op jit(solution)/shard_map/all_to_all | solution.py:197
  (395 shorter events, 117.2 us)
Async XLA Ops:
  7.2 74.3 %collective-permute-start.16 = (f32[2,1,32,128]{3,2,1,0:T(8,128)S(1)}, f32[2,1,32,128]{3,2,1,0:T(8,128)}, u32[]{:S(2)}, u32[]{:S(2)}) collective-permute-start(f32[2,1,32,128]{3,2,1,0:T(8,128)S(1)} %stack.374), channel_id=1, source_target_pairs={{8,0},{16,8},{24,16},{9,1},{17,9},{25,17},{10,2},{18,10},{26,18},{... | collective-permute-start | bytes 98312 | tf_op jit(solution)/shard_map/ppermute | solution.py:25
  9.4 73.0 %collective-permute-start.17 = (f32[2,32,1,128]{3,1,2,0:T(8,128)}, f32[2,32,1,128]{3,1,2,0:T(8,128)}, u32[]{:S(2)}, u32[]{:S(2)}) collective-permute-start(f32[2,32,1,128]{3,1,2,0:T(8,128)} %stack.375), channel_id=1, source_target_pairs={{1,0},{2,1},{3,2},{4,3},{5,4},{6,5},{7,6},{9,8},{10,9},{11,10},{12... | collective-permute-start | bytes 98312 | tf_op jit(solution)/shard_map/ppermute | solution.py:25
  15.7 20.4 %all-to-all-start = ((f32[32,8,2]{1,2,0:T(2,128)}), f32[32,8,2]{1,2,0:T(2,128)S(1)}, u32[]{:S(2)}, u32[]{:S(2)}) async-start(f32[32,8,2]{1,2,0:T(2,128)} %copy.4958), calls=%async_computation | async-start | bytes 65536 | tf_op jit(solution)/shard_map/all_to_all | solution.py:129
  29.9 58.0 %collective-permute-start.1 = (f32[2,32,1,128]{3,1,2,0:T(8,128)}, f32[2,32,1,128]{3,1,2,0:T(8,128)}, u32[]{:S(2)}, u32[]{:S(2)}) collective-permute-start(f32[2,32,1,128]{3,1,2,0:T(8,128)} %pad_maximum_fusion.58), channel_id=1, source_target_pairs={{1,0},{2,1},{3,2},{4,3},{5,4},{6,5},{7,6},{9,8},{10,9},{11,10},{12... | collective-permute-start | bytes 98312 | tf_op jit(solution)/shard_map/ppermute | solution.py:25
  31.8 56.8 %collective-permute-start = (f32[2,1,32,128]{3,2,1,0:T(8,128)}, f32[2,1,32,128]{3,2,1,0:T(8,128)S(1)}, u32[]{:S(2)}, u32[]{:S(2)}) collective-permute-start(f32[2,1,32,128]{3,2,1,0:T(8,128)} %stack.314), channel_id=1, source_target_pairs={{8,0},{16,8},{24,16},{9,1},{17,9},{25,17},{10,2},{18,10},{26,18},{... | collective-permute-start | bytes 98312 | tf_op jit(solution)/shard_map/ppermute | solution.py:25
  36.0 15.1 %all-to-all-start.1 = ((f32[32,1,128]{2,1,0:T(1,128)}), f32[32,1,128]{2,1,0:T(1,128)S(1)}, u32[]{:S(2)}, u32[]{:S(2)}) async-start(f32[32,1,128]{2,1,0:T(1,128)} %reshape.526), calls=%async_computation.1 | async-start | bytes 32768 | tf_op jit(solution)/shard_map/all_to_all | solution.py:122
  44.0 243.0 %all-reduce.45.cloned.1.call-start = ((), (), s32[]{:S(2)}) async-start(), calls=%async_computation.3 | async-start | bytes 2097152 | tf_op jit(solution)/shard_map/psum | solution.py:171
  83.7 10.7 %collective-permute-start.18 = (f32[2,32,1,128]{3,1,2,0:T(8,128)S(1)}, f32[2,32,1,128]{3,1,2,0:T(8,128)S(1)}, u32[]{:S(2)}, u32[]{:S(2)}) collective-permute-start(f32[2,32,1,128]{3,1,2,0:T(8,128)S(1)} %pad_maximum_fusion.77), channel_id=1, source_target_pairs={{0,1},{1,2},{2,3},{3,4},{4,5},{5,6},{6,7},{8,9},{9,10},{10,11},{11... | collective-permute-start | bytes 98312 | tf_op jit(solution)/shard_map/ppermute | solution.py:25
  85.7 9.4 %collective-permute-start.19 = (f32[2,1,32,128]{3,2,1,0:T(8,128)S(1)}, f32[2,1,32,128]{3,2,1,0:T(8,128)S(1)}, u32[]{:S(2)}, u32[]{:S(2)}) collective-permute-start(f32[2,1,32,128]{3,2,1,0:T(8,128)S(1)} %pad_maximum_fusion.78), channel_id=1, source_target_pairs={{0,8},{8,16},{16,24},{1,9},{9,17},{17,25},{2,10},{10,18},{18,26},{... | collective-permute-start | bytes 98312 | tf_op jit(solution)/shard_map/ppermute | solution.py:25
  89.3 6.6 %collective-permute-start.3 = (f32[2,1,32,128]{3,2,1,0:T(8,128)S(1)}, f32[2,1,32,128]{3,2,1,0:T(8,128)S(1)}, u32[]{:S(2)}, u32[]{:S(2)}) collective-permute-start(f32[2,1,32,128]{3,2,1,0:T(8,128)S(1)} %pad_maximum_fusion.60), channel_id=1, source_target_pairs={{0,8},{8,16},{16,24},{1,9},{9,17},{17,25},{2,10},{10,18},{18,26},{... | collective-permute-start | bytes 98312 | tf_op jit(solution)/shard_map/ppermute | solution.py:25
  100.0 5.9 %collective-permute-start.4 = (f32[2,1,32,128]{3,2,1,0:T(8,128)S(1)}, f32[2,1,32,128]{3,2,1,0:T(8,128)S(1)}, u32[]{:S(2)}, u32[]{:S(2)}) collective-permute-start(f32[2,1,32,128]{3,2,1,0:T(8,128)S(1)} %pad_maximum_fusion.61), channel_id=1, source_target_pairs={{8,0},{16,8},{24,16},{9,1},{17,9},{25,17},{10,2},{18,10},{26,18},{... | collective-permute-start | bytes 98312 | tf_op jit(solution)/shard_map/ppermute | solution.py:25
  114.3 5.8 %collective-permute-start.8 = (f32[2,1,32,128]{3,2,1,0:T(8,128)S(1)}, f32[2,1,32,128]{3,2,1,0:T(8,128)S(1)}, u32[]{:S(2)}, u32[]{:S(2)}) collective-permute-start(f32[2,1,32,128]{3,2,1,0:T(8,128)S(1)} %pad_maximum_fusion.65), channel_id=1, source_target_pairs={{8,0},{16,8},{24,16},{9,1},{17,9},{25,17},{10,2},{18,10},{26,18},{... | collective-permute-start | bytes 98312 | tf_op jit(solution)/shard_map/ppermute | solution.py:25
  120.8 6.2 %collective-permute-start.11 = (f32[2,1,32,128]{3,2,1,0:T(8,128)S(1)}, f32[2,1,32,128]{3,2,1,0:T(8,128)S(1)}, u32[]{:S(2)}, u32[]{:S(2)}) collective-permute-start(f32[2,1,32,128]{3,2,1,0:T(8,128)S(1)} %pad_maximum_fusion.68), channel_id=1, source_target_pairs={{0,8},{8,16},{16,24},{1,9},{9,17},{17,25},{2,10},{10,18},{18,26},{... | collective-permute-start | bytes 98312 | tf_op jit(solution)/shard_map/ppermute | solution.py:25
  129.3 6.5 %collective-permute-start.13 = (f32[2,32,1,128]{3,1,2,0:T(8,128)S(1)}, f32[2,32,1,128]{3,1,2,0:T(8,128)S(1)}, u32[]{:S(2)}, u32[]{:S(2)}) collective-permute-start(f32[2,32,1,128]{3,1,2,0:T(8,128)S(1)} %pad_maximum_fusion.70), channel_id=1, source_target_pairs={{1,0},{2,1},{3,2},{4,3},{5,4},{6,5},{7,6},{9,8},{10,9},{11,10},{12... | collective-permute-start | bytes 98312 | tf_op jit(solution)/shard_map/ppermute | solution.py:25
  130.6 5.8 %collective-permute-start.12 = (f32[2,1,32,128]{3,2,1,0:T(8,128)S(1)}, f32[2,1,32,128]{3,2,1,0:T(8,128)S(1)}, u32[]{:S(2)}, u32[]{:S(2)}) collective-permute-start(f32[2,1,32,128]{3,2,1,0:T(8,128)S(1)} %pad_maximum_fusion.69), channel_id=1, source_target_pairs={{8,0},{16,8},{24,16},{9,1},{17,9},{25,17},{10,2},{18,10},{26,18},{... | collective-permute-start | bytes 98312 | tf_op jit(solution)/shard_map/ppermute | solution.py:25
  137.1 7.3 %collective-permute-start.14 = (f32[2,32,1,128]{3,1,2,0:T(8,128)S(1)}, f32[2,32,1,128]{3,1,2,0:T(8,128)S(1)}, u32[]{:S(2)}, u32[]{:S(2)}) collective-permute-start(f32[2,32,1,128]{3,1,2,0:T(8,128)S(1)} %pad_maximum_fusion.71), channel_id=1, source_target_pairs={{0,1},{1,2},{2,3},{3,4},{4,5},{5,6},{6,7},{8,9},{9,10},{10,11},{11... | collective-permute-start | bytes 98312 | tf_op jit(solution)/shard_map/ppermute | solution.py:25
  301.3 11.2 %collective-permute-start.21 = (f32[2,32,1,128]{3,1,2,0:T(8,128)S(1)}, f32[2,32,1,128]{3,1,2,0:T(8,128)S(1)}, u32[]{:S(2)}, u32[]{:S(2)}) collective-permute-start(f32[2,32,1,128]{3,1,2,0:T(8,128)S(1)} %pad_maximum_fusion.80), channel_id=1, source_target_pairs={{1,0},{2,1},{3,2},{4,3},{5,4},{6,5},{7,6},{9,8},{10,9},{11,10},{12... | collective-permute-start | bytes 98312 | tf_op jit(solution)/shard_map/ppermute | solution.py:25
  303.3 9.2 %collective-permute-start.20 = (f32[2,1,32,128]{3,2,1,0:T(8,128)}, f32[2,1,32,128]{3,2,1,0:T(8,128)S(1)}, u32[]{:S(2)}, u32[]{:S(2)}) collective-permute-start(f32[2,1,32,128]{3,2,1,0:T(8,128)} %pad_maximum_fusion.79), channel_id=1, source_target_pairs={{8,0},{16,8},{24,16},{9,1},{17,9},{25,17},{10,2},{18,10},{26,18},{... | collective-permute-start | bytes 98312 | tf_op jit(solution)/shard_map/ppermute | solution.py:25
  316.7 7.1 %collective-permute-start.23 = (f32[2,1,32,128]{3,2,1,0:T(8,128)S(1)}, f32[2,1,32,128]{3,2,1,0:T(8,128)S(1)}, u32[]{:S(2)}, u32[]{:S(2)}) collective-permute-start(f32[2,1,32,128]{3,2,1,0:T(8,128)S(1)} %pad_maximum_fusion.82), channel_id=1, source_target_pairs={{0,8},{8,16},{16,24},{1,9},{9,17},{17,25},{2,10},{10,18},{18,26},{... | collective-permute-start | bytes 98312 | tf_op jit(solution)/shard_map/ppermute | solution.py:25
  333.5 6.3 %collective-permute-start.27 = (f32[2,1,32,128]{3,2,1,0:T(8,128)S(1)}, f32[2,1,32,128]{3,2,1,0:T(8,128)S(1)}, u32[]{:S(2)}, u32[]{:S(2)}) collective-permute-start(f32[2,1,32,128]{3,2,1,0:T(8,128)S(1)} %pad_maximum_fusion.86), channel_id=1, source_target_pairs={{0,8},{8,16},{16,24},{1,9},{9,17},{17,25},{2,10},{10,18},{18,26},{... | collective-permute-start | bytes 98312 | tf_op jit(solution)/shard_map/ppermute | solution.py:25
  341.5 6.5 %collective-permute-start.29 = (f32[2,32,1,128]{3,1,2,0:T(8,128)S(1)}, f32[2,32,1,128]{3,1,2,0:T(8,128)S(1)}, u32[]{:S(2)}, u32[]{:S(2)}) collective-permute-start(f32[2,32,1,128]{3,1,2,0:T(8,128)S(1)} %pad_maximum_fusion.88), channel_id=1, source_target_pairs={{1,0},{2,1},{3,2},{4,3},{5,4},{6,5},{7,6},{9,8},{10,9},{11,10},{12... | collective-permute-start | bytes 98312 | tf_op jit(solution)/shard_map/ppermute | solution.py:25
  349.9 7.6 %collective-permute-start.31 = (f32[2,1,32,128]{3,2,1,0:T(8,128)S(1)}, f32[2,1,32,128]{3,2,1,0:T(8,128)S(1)}, u32[]{:S(2)}, u32[]{:S(2)}) collective-permute-start(f32[2,1,32,128]{3,2,1,0:T(8,128)S(1)} %pad_maximum_fusion.90), channel_id=1, source_target_pairs={{0,8},{8,16},{16,24},{1,9},{9,17},{17,25},{2,10},{10,18},{18,26},{... | collective-permute-start | bytes 98312 | tf_op jit(solution)/shard_map/ppermute | solution.py:25
  352.5 5.9 %collective-permute-start.30 = (f32[2,32,1,128]{3,1,2,0:T(8,128)S(1)}, f32[2,32,1,128]{3,1,2,0:T(8,128)S(1)}, u32[]{:S(2)}, u32[]{:S(2)}) collective-permute-start(f32[2,32,1,128]{3,1,2,0:T(8,128)S(1)} %pad_maximum_fusion.89), channel_id=1, source_target_pairs={{0,1},{1,2},{2,3},{3,4},{4,5},{5,6},{6,7},{8,9},{9,10},{10,11},{11... | collective-permute-start | bytes 98312 | tf_op jit(solution)/shard_map/ppermute | solution.py:25
  392.3 16.3 %all-to-all-start.2 = ((f32[32,1,128]{2,1,0:T(1,128)}), f32[32,1,128]{2,1,0:T(1,128)S(1)}, u32[]{:S(2)}, u32[]{:S(2)}) async-start(f32[32,1,128]{2,1,0:T(1,128)} %reshape.528), calls=%async_computation.2 | async-start | bytes 32768 | tf_op jit(solution)/shard_map/all_to_all | solution.py:197
  (68 other events, 784.5 us)
Sparse Core Ops, SparseCore 0:
  153.5 133.4 all-reduce.44
where the time goes:
time: 419 us; the launch traced here: 418 us
  waiting for transfers between devices  167 us (40%)
  starting transfers between devices  96.4 us (23%)
  other arithmetic  63.2 us (15%)
  local copies, waits for them, and re-layouts  62 us (15%)
  between operations  16.3 us (4%)
  matrix products  13.1 us (3%)
    psum x1, waiting for transfers between devices, shards(): far_field = lax.psum(partial_far, ('gx', 'gy'))  129 us
    ppermute x32, starting transfers between devices, passed_along(): return lax.ppermute(shard, axis, pairs)  69 us
    unnamed x7, other arithmetic  32.6 us
    gather x1, local copies, waits for them, and re-layouts, shards(): picked = column_grad[cells_x, cells_y]  27.6 us
    ppermute x32, waiting for transfers between devices, passed_along(): return lax.ppermute(shard, axis, pairs)  27.2 us
    dot_general x16, matrix products, contract(): jnp.einsum(pattern, first_op, second_op, precision=lax.Precision.HIGHEST)  13.1 us
    all_to_all x1, starting transfers between devices, shards(): lax.all_to_all(packed_at.reshape(devices, capacity, 2), ('gx', 'gy'), spl...  10.3 us
    another operation x12, local copies, waits for them, and re-layouts  10.2 us
  transfers between devices with their start and end apart: 36, of which 18 were waited for; matrix products, arithmetic and copies ran while one was open for 16% of the time, Pallas kernels for 0%

commit v1 on v0

v1 whole, which is shorter than its diff:
```python
import math

import jax
import jax.numpy as jnp
import numpy as np
from jax import lax
from jax.experimental import pallas as pl
from jax.experimental.pallas import tpu as pltpu
from jax.sharding import PartitionSpec as P

TILE = 32
P_DEV = 128
NT = 4
ZP = 4
U = 256
V = 256
ZM = 64

COURANT = 0.5
ANGULAR_STEP = 0.9
DELTA_EPS = 4.0

HALO = 4
EXT = TILE + 2 * HALO
BAND = 16
BAND_START = ZM - BAND // 2
GROUPS = 128 // BAND
RUN = EXT // GROUPS
LANES = RUN * 128
FEATURES = 24
RIM_ROWS = 4 * TILE
ARRAYS = 7
AHEAD = 8
REACH = 48
YPAD = 64
BF16 = jnp.bfloat16
F32 = jnp.float32


def split_table(table):
    table = np.asarray(table, np.float32)
    high = table.astype(jnp.bfloat16)
    low = (table - high.astype(np.float32)).astype(jnp.bfloat16)
    return np.stack([high, low])


def phase_table(count_out, count_in):
    focal_pos = (np.arange(count_out) + 0.5) / count_out - 0.5
    cell_pos = (np.arange(count_in) + 0.5) / count_in - 0.5
    squared = ((focal_pos[:, None] - cell_pos[None, :]) ** 2).astype(np.float32)
    phase = (np.float32(math.pi * count_out) * squared).astype(np.float64)
    return np.cos(phase), np.sin(phase)


def round_cells(place, count):
    cells = np.arange(EXT)
    cells = np.where(cells < TILE + HALO, cells, cells - EXT) + place * TILE
    return cells, (cells >= 0) & (cells < count * TILE)


def packed_lane(cell, layer):
    return (cell % RUN) * 128 + (cell // RUN) * BAND + layer - BAND_START


def tables(span_x, span_y):
    count_x, count_y = span_x * TILE, span_y * TILE
    norm = (count_x * count_y) ** -0.5
    x_re, x_im = phase_table(U, count_x)
    y_re, y_im = phase_table(V, count_y)
    xr = x_re.reshape(U, span_x, 1, TILE)
    xi = x_im.reshape(U, span_x, 1, TILE)
    first = np.concatenate(
        [
            np.concatenate([xr, -xi], axis=2).reshape(U, -1),
            np.concatenate([xi, xr], axis=2).reshape(U, -1),
        ]
    )
    second = norm * np.block([[y_re.T, y_im.T], [-y_im.T, y_re.T]])
    back_y = np.zeros((span_y, 2 * YPAD, 2 * V))
    for place in range(span_y):
        cells, inside = round_cells(place, span_y)
        for row in range(EXT):
            if inside[row]:
                re, im = y_re[:, cells[row]], y_im[:, cells[row]]
                back_y[place, row] = np.concatenate([re, -im])
                back_y[place, YPAD + row] = np.concatenate([im, re])
    back_x = np.zeros((span_x, U, 2 * YPAD))
    for place in range(span_x):
        cells, inside = round_cells(place, span_x)
        for row in range(EXT):
            if inside[row]:
                back_x[place, :, row] = 2.0 * norm * x_re[:, cells[row]]
                back_x[place, :, YPAD + row] = 2.0 * norm * x_im[:, cells[row]]
    return (
        split_table(first),
        split_table(second),
        np.moveaxis(split_table(back_y), 0, 1),
        np.moveaxis(split_table(back_x), 0, 1),
    )


def choosers():
    fill = np.zeros((4, REACH, LANES), np.float32)
    for step in range(4):
        for row in range(REACH):
            cell = row - AHEAD + step
            if -HALO <= cell < TILE + HALO:
                for layer in range(ZM - ZP, ZM):
                    fill[step, row, packed_lane(cell % EXT, layer)] = DELTA_EPS
    monitor = np.zeros((LANES, 128), np.float32)
    column = np.zeros((LANES, 128), np.float32)
    for cell in range(TILE):
        monitor[packed_lane(cell, ZM), cell] = 1.0
        for layer in range(ZM - ZP, ZM):
            column[packed_lane(cell, layer), cell] = 1.0
    source = np.zeros((128, LANES), np.float32)
    for cell in range(EXT):
        source[cell, packed_lane(cell, ZM)] = 1.0
    return [table.astype(jnp.bfloat16) for table in (fill, monitor, column, source)]


def halves(value):
    high = value.astype(BF16)
    return high, (value - high.astype(F32)).astype(BF16)


def dot(first_op, second_op):
    return jnp.dot(first_op, second_op, preferred_element_type=F32)


def dot_rows(first_op, second_op):
    return lax.dot_general(first_op, second_op, (((1,), (1,)), ((), ())), preferred_element_type=F32)


def lanes_of(shape):
    return lax.broadcasted_iota(jnp.int32, shape, 1)


def rows_of(shape):
    return lax.broadcasted_iota(jnp.int32, shape, 0)


def pack_kernel(fields, eps, features, packed, pay_east, pay_west):
    group = lanes_of((TILE, 128)) // BAND
    for array in range(ARRAYS):
        layer = (lambda x: eps[x]) if array == 6 else (lambda x: fields[array, x])
        kept = [jnp.zeros((TILE, 128), F32) for _ in range(RUN)]
        for x in range(TILE):
            at = x // RUN
            moved = pltpu.roll(layer(x), (BAND * at - BAND_START) % 128, 1)
            kept[x % RUN] = jnp.where(group == at, moved, kept[x % RUN])
        for run in range(RUN):
            packed[array, run] = kept[run]
    for pay, start in ((pay_west, 0), (pay_east, TILE - HALO)):
        for block in range(4):
            built = jnp.zeros((TILE, 128), F32)
            for at in range(8):
                array, x = 2 * block + at // 4, start + at % 4
                if array < ARRAYS:
                    source = eps[x] if array == 6 else fields[array, x]
                    moved = pltpu.roll(source, (BAND * at - BAND_START) % 128, 1)
                    built = jnp.where(group == at, moved, built)
            pay[block * TILE : (block + 1) * TILE] = built
        pay[RIM_ROWS : RIM_ROWS + FEATURES] = features[...]


def widen_kernel(span_x, place, packed, features, from_west, from_east, *rest):
    others, (wide, pay_north, pay_south, row_features) = rest[:-4], rest[-4:]
    group = lanes_of((TILE, 128)) // BAND
    has_west = place[0] > 0
    has_east = place[0] < span_x - 1
    for array in range(ARRAYS):
        kept = [packed[array, run] for run in range(RUN)]
        rows = slice((array // 2) * TILE, (array // 2 + 1) * TILE)
        east = jnp.where(has_east, from_east[rows], 0.0)
        west = jnp.where(has_west, from_west[rows], 0.0)
        for step in range(HALO):
            at = (array % 2) * 4 + step
            for block, x in ((east, TILE + step), (west, TILE + HALO + step)):
                to = x // RUN
                moved = pltpu.roll(block, (BAND * (to - at)) % 128, 1)
                kept[x % RUN] = jnp.where(group == to, moved, kept[x % RUN])
        for run in range(RUN):
            wide[array, run] = kept[run]
    low = rows_of((8, 128)) < 4
    for block in range(4):
        for run in range(RUN):
            even, odd = 2 * block, min(2 * block + 1, ARRAYS - 1)
            rows = slice((block * RUN + run) * 8, (block * RUN + run + 1) * 8)
            pay_south[rows] = jnp.where(low, wide[even, run, 0:8], pltpu.roll(wide[odd, run, 0:8], 4, 0))
            pay_north[rows] = jnp.where(
                low, pltpu.roll(wide[even, run, TILE - 8 : TILE], 4, 0), wide[odd, run, TILE - 8 : TILE]
            )
    every = [features[...], from_west[RIM_ROWS:], from_east[RIM_ROWS:]] + [other[...] for other in others]
    for at, part in enumerate(every):
        rows = slice(at * FEATURES, (at + 1) * FEATURES)
        row_features[rows] = part
        for pay in (pay_north, pay_south):
            pay[4 * RUN * 8 + at * FEATURES : 4 * RUN * 8 + (at + 1) * FEATURES] = part


def packed_ahead_x(ref, component, run):
    if run < RUN - 1:
        return ref[component, run + 1]
    return pltpu.roll(ref[component, 0], 128 - BAND, 1)


def packed_behind_x(ref, component, run):
    if run > 0:
        return ref[component, run - 1]
    return pltpu.roll(ref[component, RUN - 1], BAND, 1)


def ahead_y(value):
    return pltpu.roll(value, EXT - 1, 0)


def behind_y(value):
    return pltpu.roll(value, 1, 0)


def ahead_z(value):
    return pltpu.roll(value, 127, 1)


def behind_z(value):
    return pltpu.roll(value, 1, 1)


def packed_magnetic(elec, magn, half_magn):
    for run in range(RUN):
        ex, ey, ez = elec[0, run], elec[1, run], elec[2, run]
        ey_next, ez_next = packed_ahead_x(elec, 1, run), packed_ahead_x(elec, 2, run)
        rate = half_magn[run]
        magn[0, run] = magn[0, run] - rate * ((ahead_y(ez) - ez) - (ahead_z(ey) - ey))
        magn[1, run] = magn[1, run] - rate * ((ahead_z(ex) - ex) - (ez_next - ez))
        magn[2, run] = magn[2, run] - rate * ((ey_next - ey) - (ahead_y(ex) - ex))


def packed_curl(magn, run):
    hx, hy, hz = magn[0, run], magn[1, run], magn[2, run]
    hy_last, hz_last = packed_behind_x(magn, 1, run), packed_behind_x(magn, 2, run)
    return (
        (hz - behind_y(hz)) - (hy - behind_z(hy)),
        (hx - behind_z(hx)) - (hz - hz_last),
        (hy - hy_last) - (hx - behind_y(hx)),
    )


def packed_inside(place, span_x, span_y, run):
    shape = (EXT, 128)
    cell_x = (lanes_of(shape) // BAND) * RUN + run
    cell_y = rows_of(shape)

    def side(cell, at, span):
        last = jnp.where(at < span - 1, TILE + HALO, TILE)
        first = jnp.where(at > 0, TILE + HALO, EXT)
        return (cell < last) | (cell >= first)

    return side(cell_x, place[0], span_x) & side(cell_y, place[1], span_y)


def forward_kernel(span_x, span_y, place, wide, row_features, from_south, from_north, *rest):
    others = rest[: span_y - 3]
    fill_table, monitor_table = rest[span_y - 3 : span_y - 1]
    monitor, changes, inverse, half_magn, elec, magn, ends, starts, mons = rest[span_y - 1 :]
    rim_rows = 4 * RUN * 8
    corner_x = (place[0] * TILE).astype(F32)
    corner_y = (place[1] * TILE).astype(F32)
    row = rows_of((EXT, 128))
    cell_y = jnp.where(row < TILE + HALO, row, row - EXT).astype(F32) + corner_y
    cell_x = (rows_of((REACH, 128)) - AHEAD).astype(F32) + corner_x
    sources = [(row_features, 0), (from_south, rim_rows), (from_north, rim_rows)] + [(other, 0) for other in others]
    chunk = 0
    for ref, offset in sources:
        for at in range(span_x):
            base = offset + at * FEATURES
            lanes = slice(chunk * 128, (chunk + 1) * 128)
            chunk += 1
            ends[:, lanes] = (cell_x == ref[base + 16 : base + 17]).astype(F32).astype(BF16)
            ahead = cell_y - ref[base + 17 : base + 18]
            hits = [ahead == float(step) for step in range(4)]
            for step_x in range(4):
                value = jnp.zeros((EXT, 128), F32)
                for step_y in range(4):
                    k = base + 4 * step_x + step_y
                    value = jnp.where(hits[step_y], ref[k : k + 1], value)
                high, low = halves(value)
                starts[step_x * EXT : (step_x + 1) * EXT, lanes] = high
                starts[(4 + step_x) * EXT : (5 + step_x) * EXT, lanes] = low
    counted = dot_rows(starts[...], ends[...])
    counted = counted[: 4 * EXT] + counted[4 * EXT :]
    filled = jnp.zeros((EXT, LANES), F32)
    for step_x in range(4):
        high, low = halves(counted[step_x * EXT : (step_x + 1) * EXT])
        filled = filled + dot(high, fill_table[step_x]) + dot(low, fill_table[step_x])
    has_south = place[1] > 0
    has_north = place[1] < span_y - 1
    low_rows = rows_of((8, 128)) < 4
    for array in range(ARRAYS):
        for run in range(RUN):
            at = ((array // 2) * RUN + run) * 8
            north = jnp.where(has_north, from_north[at : at + 8], 0.0)
            south = jnp.where(has_south, from_south[at : at + 8], 0.0)
            if array % 2 == 0:
                rim = jnp.where(low_rows, north, pltpu.roll(south, 4, 0))
            else:
                rim = jnp.where(low_rows, pltpu.roll(north, 4, 0), south)
            if array < 3:
                elec[array, run, :TILE] = wide[array, run]
                elec[array, run, TILE:] = rim
            elif array < 6:
                magn[array - 3, run, :TILE] = wide[array, run]
                magn[array - 3, run, TILE:] = rim
            else:
                inside = packed_inside(place, span_x, span_y, run)
                eps = jnp.concatenate([wide[array, run], rim], axis=0)
                eps = eps + filled[:, run * 128 : (run + 1) * 128]
                inverse[run] = jnp.where(inside, 1.0 / jnp.where(inside, eps, 1.0), 0.0)
                half_magn[run] = jnp.where(inside, COURANT, 0.0)
    for moment in range(1, NT + 1):
        packed_magnetic(elec, magn, half_magn)
        cos, sin = math.cos(ANGULAR_STEP * moment), math.sin(ANGULAR_STEP * moment)
        for run in range(RUN):
            rate = COURANT * inverse[run]
            for component, curl in enumerate(packed_curl(magn, run)):
                change = curl * rate
                now = elec[component, run] + change
                elec[component, run] = now
                changes[moment - 1, component, run] = change[:TILE]
                if component < 2:
                    own = now[:TILE]
                    if moment == 1:
                        mons[2 * component, run] = cos * own
                        mons[2 * component + 1, run] = -sin * own
                    else:
                        mons[2 * component, run] += cos * own
                        mons[2 * component + 1, run] += -sin * own
    built = jnp.zeros((4 * TILE, 128), F32)
    for run in range(RUN):
        high, low = halves(mons[:, run].reshape(4 * TILE, 128))
        table = monitor_table[run * 128 : (run + 1) * 128]
        built = built + dot(high, table) + dot(low, table)
    payload = built[:TILE]
    for part in range(1, 4):
        payload = payload + pltpu.roll(built[part * TILE : (part + 1) * TILE], part * TILE, 1)
    monitor[...] = payload


def focal_kernel(span_x, span_y, place, *rest):
    gathered = rest[:span_y]
    first, second, back_y, back_x, column_table, source_table, target, changes, inverse = rest[span_y : span_y + 9]
    power, column, sorted_mon, sums, elec, magn, half_magn, drive, grads = rest[span_y + 9 :]
    count_y = span_y * TILE
    for step_y, ref in enumerate(gathered):
        at_y = lax.rem(place[1] - step_y + span_y, span_y)
        for step_x in range(span_x):
            at_x = lax.rem(place[0] - step_x + span_x, span_x)
            sorted_mon[at_x, pl.ds(pl.multiple_of(at_y * TILE, TILE), TILE)] = ref[step_x * TILE : (step_x + 1) * TILE]
    left = lanes_of((count_y, 128)) < 64
    total = jnp.zeros((U, V), F32)
    half_parts = []
    for component in range(2):
        pieces = []
        for pair in range(span_x // 2):
            even, odd = sorted_mon[2 * pair], sorted_mon[2 * pair + 1]
            if component == 0:
                pieces.append(jnp.where(left, even, pltpu.roll(odd, 64, 1)))
            else:
                pieces.append(jnp.where(left, pltpu.roll(even, 64, 1), odd))
        high, low = halves(jnp.concatenate(pieces, axis=1))
        part = dot_rows(first[0], high) + dot_rows(first[0], low) + dot_rows(first[1], high)
        high, low = halves(part)
        far = jnp.zeros((U, 2 * V), F32)
        for at, rows in ((0, slice(0, U)), (1, slice(U, 2 * U))):
            span = slice(at * count_y, (at + 1) * count_y)
            far = far + dot(high[rows], second[0, span]) + dot(low[rows], second[0, span])
            far = far + dot(high[rows], second[1, span])
        far_re, far_im = far[:, :V], far[:, V:]
        total = total + far_re * far_re + far_im * far_im
        weighted = jnp.concatenate([target[...] * far_re, -(target[...] * far_im)], axis=1)
        high, low = halves(weighted)
        half_parts.append(dot_rows(back_y[0], high) + dot_rows(back_y[0], low) + dot_rows(back_y[1], high))
    sums[...] = total
    devices = span_x * span_y
    rows = U // devices
    start = (place[0] * span_y + place[1]) * rows
    if rows % 8 == 0:
        power[...] = sums[pl.ds(pl.multiple_of(start, 8), rows)]
    else:
        near = sums[pl.ds(pl.multiple_of((start // 8) * 8, 8), 8)]
        spot = rows_of((8, V))
        for at in range(rows):
            mine = jnp.where(spot == start % 8 + at, near, 0.0)
            power[at : at + 1] = jnp.sum(mine, axis=0, keepdims=True)
    high, low = halves(jnp.concatenate(half_parts, axis=0))
    back = dot(high, back_x[0]) + dot(low, back_x[0]) + dot(high, back_x[1])
    turned = pltpu.roll(back, YPAD, 1)
    lanes_ok = lanes_of((YPAD, 128)) < EXT
    for component in range(2):
        re = slice(2 * component * YPAD, (2 * component + 1) * YPAD)
        im = slice((2 * component + 1) * YPAD, (2 * component + 2) * YPAD)
        for at, value in ((0, back[re] - turned[im]), (1, back[im] + turned[re])):
            high, low = halves(jnp.where(lanes_ok, value, 0.0))
            placed = dot(high, source_table[...]) + dot(low, source_table[...])
            for run in range(RUN):
                drive[2 * component + at, run] = placed[:EXT, run * 128 : (run + 1) * 128]
    for run in range(RUN):
        inside = packed_inside(place, span_x, span_y, run)
        half_magn[run] = jnp.where(inside, COURANT, 0.0)
        grads[run] = jnp.zeros((TILE, 128), F32)
        for component in range(3):
            elec[component, run] = jnp.zeros((EXT, 128), F32)
            magn[component, run] = jnp.zeros((EXT, 128), F32)
    for moment in range(1, NT + 1):
        step = NT + 1 - moment
        cos, sin = math.cos(ANGULAR_STEP * step), math.sin(ANGULAR_STEP * step)
        if moment > 1:
            packed_magnetic(elec, magn, half_magn)
        for run in range(RUN):
            rate = COURANT * inverse[run]
            for component, curl in enumerate(packed_curl(magn, run)):
                if component < 2:
                    curl = curl - (cos * drive[2 * component, run] + sin * drive[2 * component + 1, run])
                now = elec[component, run] + curl * rate
                elec[component, run] = now
                grads[run] += now[:TILE] * changes[step - 1, component, run]
    built = jnp.zeros((TILE, 128), F32)
    for run in range(RUN):
        high, low = halves(-grads[run] * inverse[run, :TILE])
        table = column_table[run * 128 : (run + 1) * 128]
        built = built + dot(high, table) + dot(low, table)
    payload = built[:8]
    for part in range(1, TILE // 8):
        payload = payload + pltpu.roll(built[8 * part : 8 * part + 8], part * TILE, 1)
    for at in range(devices):
        column[at] = payload


def widths_kernel(received, intersection, tile, anchors, grad):
    high, low = halves(received[...])
    rows = received.shape[0]
    spot = lanes_of((P_DEV, rows))
    lane = lanes_of((P_DEV, 128))
    anchor_x, anchor_y = anchors[:, 0:1], anchors[:, 1:2]
    total = jnp.zeros((P_DEV, 128), F32)
    for step_y in range(4):
        cell_y = anchor_y + step_y
        chosen = (spot == tile[...] * 8 + (cell_y & 7)).astype(F32).astype(BF16)
        values = dot(chosen, high) + dot(chosen, low)
        ahead = lane - ((cell_y >> 3) * TILE + anchor_x)
        for step_x in range(4):
            k = 4 * step_x + step_y
            total = total + jnp.where(ahead == step_x, values * intersection[:, k : k + 1], 0.0)
    summed = jnp.sum(total, axis=1, keepdims=True)
    turned = jnp.where(rows_of((P_DEV, P_DEV)) == lanes_of((P_DEV, P_DEV)), summed, 0.0)
    grad[...] = DELTA_EPS * jnp.sum(turned, axis=0, keepdims=True)


def full_kernel(fields, eps, inverse, from_east, from_west, from_north, from_south, out, elec, magn, rate_elec, rate_magn):
    rim = slice(TILE, TILE + HALO)
    end = slice(TILE + HALO, EXT)
    shape = (EXT, 128)
    lane = lanes_of(shape)
    in_layers = (lane >= ZM - ZP) & (lane < ZM)
    inside_one = lane < 127
    inside_zero = lane > 0

    def fill(x, _):
        for array in range(6):
            ref, at = (elec, array) if array < 3 else (magn, array - 3)
            ref[at, x, :TILE] = fields[array, x]
            ref[at, x, rim] = from_north[array, x]
            ref[at, x, end] = from_south[array, x]
        rate_elec[x, :TILE] = eps[x]
        rate_elec[x, rim] = from_north[6, x]
        rate_elec[x, end] = from_south[6, x]
        return 0

    lax.fori_loop(0, TILE, fill, 0)
    for step in range(2 * HALO):
        x = TILE + step
        block, at_x = (from_east, step) if step < HALO else (from_west, step - HALO)
        for array in range(7):
            ref, at = (elec, array) if array < 3 else ((magn, array - 3) if array < 6 else (None, 0))
            view = rate_elec.at[x] if ref is None else ref.at[at, x]
            view[:TILE] = block[array, at_x]
            view[rim] = from_north[array, x]
            view[end] = from_south[array, x]
    for x in range(EXT):
        at = x // RUN
        spread = pltpu.roll(inverse[x % RUN], (BAND_START - BAND * at) % 128, 1)
        value = rate_elec[x]
        inside = value > 0.0
        plain = jnp.where(inside, 1.0 / jnp.where(inside, value, 1.0), 0.0)
        rate_elec[x] = COURANT * jnp.where(in_layers, spread, plain)
        rate_magn[x] = jnp.where(inside, COURANT, 0.0)

    def magnetic(x, _):
        x_next = jnp.where(x == EXT - 1, 0, x + 1)
        ex, ey, ez = elec[0, x], elec[1, x], elec[2, x]
        rate = rate_magn[x]
        dz_ey = jnp.where(inside_one, ahead_z(ey), 0.0) - ey
        dz_ex = jnp.where(inside_one, ahead_z(ex), 0.0) - ex
        magn[0, x] = magn[0, x] - rate * ((ahead_y(ez) - ez) - dz_ey)
        magn[1, x] = magn[1, x] - rate * (dz_ex - (elec[2, x_next] - ez))
        magn[2, x] = magn[2, x] - rate * ((elec[1, x_next] - ey) - (ahead_y(ex) - ex))
        return 0

    def electric(x, _):
        x_last = jnp.where(x == 0, EXT - 1, x - 1)
        hx, hy, hz = magn[0, x], magn[1, x], magn[2, x]
        rate = rate_elec[x]
        dz_hy = hy - jnp.where(inside_zero, behind_z(hy), 0.0)
        dz_hx = hx - jnp.where(inside_zero, behind_z(hx), 0.0)
        elec[0, x] = elec[0, x] + rate * ((hz - behind_y(hz)) - dz_hy)
        elec[1, x] = elec[1, x] + rate * (dz_hx - (hz - magn[2, x_last]))
        elec[2, x] = elec[2, x] + rate * ((hy - magn[1, x_last]) - (hx - behind_y(hx)))
        return 0

    for moment in range(NT):
        lax.fori_loop(0, EXT, magnetic, 0)
        lax.fori_loop(0, EXT, electric, 0)

    def store(x, _):
        for array in range(3):
            out[array, x] = elec[array, x, :TILE]
            out[3 + array, x] = magn[array, x, :TILE]
        return 0

    lax.fori_loop(0, TILE, store, 0)


def call(kernel, out_shape, scalars, operands, scratch=(), flops=1_000_000, limit=48):
    smem = pl.BlockSpec(memory_space=pltpu.SMEM)
    vmem = pl.BlockSpec(memory_space=pltpu.VMEM)
    many = isinstance(out_shape, (tuple, list))
    return pl.pallas_call(
        kernel,
        out_shape=out_shape,
        in_specs=[smem] * len(scalars) + [vmem] * len(operands),
        out_specs=[vmem] * len(out_shape) if many else vmem,
        scratch_shapes=list(scratch),
        compiler_params=pltpu.CompilerParams(vmem_limit_bytes=limit * 1024 * 1024),
        cost_estimate=pl.CostEstimate(flops=flops, bytes_accessed=4_000_000, transcendentals=0),
    )(*scalars, *operands)


def shape_of(*dims, dtype=F32):
    return jax.ShapeDtypeStruct(dims, dtype)


def turned(value, axis, by):
    count = lax.axis_size(axis)
    return lax.ppermute(value, axis, [(i, (i + by) % count) for i in range(count)])


def passed_along(shard, axis, by):
    count = lax.axis_size(axis)
    pairs = [(i, i + by) for i in range(count) if 0 <= i + by < count]
    return lax.ppermute(shard, axis, pairs)


def shards(fields, eps_background, target, widths, intersection, pillar_tile, anchors):
    span_x = lax.axis_size("gx")
    span_y = lax.axis_size("gy")
    devices = span_x * span_y
    place_x = lax.axis_index("gx")
    place_y = lax.axis_index("gy")
    place = jnp.stack([place_x, place_y]).astype(jnp.int32)
    first, second, back_y, back_x = tables(span_x, span_y)
    fill_table, monitor_table, column_table, source_table = choosers()
    back_y = lax.dynamic_index_in_dim(jnp.asarray(back_y), place_y, 0, keepdims=False)
    back_x = lax.dynamic_index_in_dim(jnp.asarray(back_x), place_x, 0, keepdims=False)

    tile = pillar_tile[:, 0]
    start_x = (tile // span_y) * TILE + anchors[:, 0]
    start_y = (tile % span_y) * TILE + anchors[:, 1]
    features = jnp.concatenate(
        [
            (intersection * widths[:, None]).T,
            start_x[None].astype(F32),
            start_y[None].astype(F32),
            jnp.zeros((FEATURES - 18, P_DEV), F32),
        ]
    )
    pay_rows = RIM_ROWS + FEATURES
    packed, pay_east, pay_west = call(
        pack_kernel,
        (shape_of(ARRAYS, RUN, TILE, 128), shape_of(pay_rows, 128), shape_of(pay_rows, 128)),
        (),
        (fields, eps_background, features),
    )
    from_west = turned(pay_east, "gx", 1)
    from_east = turned(pay_west, "gx", -1)
    others = [turned(features, "gx", by) for by in range(2, span_x - 1)]
    row_rows = span_x * FEATURES
    pay_rows = 4 * RUN * 8 + row_rows
    wide, pay_north, pay_south, row_features = call(
        lambda *refs: widen_kernel(span_x, *refs),
        (
            shape_of(ARRAYS, RUN, TILE, 128),
            shape_of(pay_rows, 128),
            shape_of(pay_rows, 128),
            shape_of(row_rows, 128),
        ),
        (place,),
        (packed, features, from_west, from_east, *others),
    )
    from_south = turned(pay_north, "gy", 1)
    from_north = turned(pay_south, "gy", -1)
    others = [turned(row_features, "gy", by) for by in range(2, span_y - 1)]
    ext = (RUN, EXT, 128)
    monitor, changes, inverse = call(
        lambda *refs: forward_kernel(span_x, span_y, *refs),
        (shape_of(TILE, 128), shape_of(NT, 3, RUN, TILE, 128), shape_of(*ext)),
        (place,),
        (wide, row_features, from_south, from_north, *others, jnp.asarray(fill_table), jnp.asarray(monitor_table)),
        scratch=(
            pltpu.VMEM(ext, F32),
            pltpu.VMEM((3, *ext), F32),
            pltpu.VMEM((3, *ext), F32),
            pltpu.VMEM((REACH, devices * P_DEV), BF16),
            pltpu.VMEM((8 * EXT, devices * P_DEV), BF16),
            pltpu.VMEM((4, RUN, TILE, 128), F32),
        ),
    )
    row_mon = jnp.concatenate([monitor] + [turned(monitor, "gx", by) for by in range(1, span_x)])
    gathered = [row_mon] + [turned(row_mon, "gy", by) for by in range(1, span_y)]

    strip_west = jnp.concatenate([fields[:, :HALO], eps_background[None, :HALO]])
    strip_east = jnp.concatenate([fields[:, -HALO:], eps_background[None, -HALO:]])
    rim_east = passed_along(strip_west, "gx", -1)
    rim_west = passed_along(strip_east, "gx", 1)

    def y_strip(rows):
        own = jnp.concatenate([fields[:, :, rows], eps_background[None, :, rows]])
        return jnp.concatenate([own, rim_east[:, :, rows], rim_west[:, :, rows]], axis=1)

    rim_north = passed_along(y_strip(slice(0, HALO)), "gy", -1)
    rim_south = passed_along(y_strip(slice(TILE - HALO, TILE)), "gy", 1)
    final_fields = call(
        full_kernel,
        shape_of(6, TILE, TILE, 128),
        (),
        (fields, eps_background, inverse, rim_east, rim_west, rim_north, rim_south),
        scratch=(
            pltpu.VMEM((3, EXT, EXT, 128), F32),
            pltpu.VMEM((3, EXT, EXT, 128), F32),
            pltpu.VMEM((EXT, EXT, 128), F32),
            pltpu.VMEM((EXT, EXT, 128), F32),
        ),
        flops=50_000_000,
    )

    count_y = span_y * TILE
    focal_power, column = call(
        lambda *refs: focal_kernel(span_x, span_y, *refs),
        (shape_of(U // devices, V), shape_of(devices, 8, 128)),
        (place,),
        (
            *gathered,
            jnp.asarray(first),
            jnp.asarray(second),
            back_y,
            back_x,
            jnp.asarray(column_table),
            jnp.asarray(source_table),
            target,
            changes,
            inverse,
        ),
        scratch=(
            pltpu.VMEM((span_x, count_y, 128), F32),
            pltpu.VMEM((U, V), F32),
            pltpu.VMEM((3, *ext), F32),
            pltpu.VMEM((3, *ext), F32),
            pltpu.VMEM(ext, F32),
            pltpu.VMEM((4, *ext), F32),
            pltpu.VMEM((RUN, TILE, 128), F32),
        ),
    )
    received = lax.all_to_all(column, ("gx", "gy"), split_axis=0, concat_axis=0, tiled=True)
    grad_widths = call(
        widths_kernel,
        shape_of(1, P_DEV),
        (),
        (received.reshape(devices * 8, 128), intersection, pillar_tile, anchors),
    )
    return (final_fields, focal_power, grad_widths.reshape(P_DEV))


def solution(mesh):
    placed = (
        P(None, "gx", "gy", None),
        P("gx", "gy", None),
        P(),
        P(("gx", "gy")),
        P(("gx", "gy"), None),
        P(("gx", "gy"), None),
        P(("gx", "gy"), None),
    )
    return jax.shard_map(
        shards,
        mesh=mesh,
        in_specs=placed,
        out_specs=(P(None, "gx", "gy", None), P(("gx", "gy"), None), P(("gx", "gy"))),
        check_vma=False,
    )
```

time: 419 us -> 134 us (0.32)
  waiting for transfers between devices: 167 us -> 20.2 us
  other arithmetic: 63.2 us -> 5.39 us
  starting transfers between devices: 96.4 us -> 44.8 us
  local copies, waits for them, and re-layouts: 62 us -> 17.4 us
  Pallas kernels: 0 us -> 44 us
  between operations: 16.3 us -> 0.92 us
  matrix products: 13.1 us -> 0 us
    psum x1 -> x0, waiting for transfers between devices: 129 us -> none  [shards(): far_field = lax.psum(partial_far, ('gx', 'gy'))]
    ppermute x32 -> x4, starting transfers between devices: 69 us -> 11.4 us  [passed_along(): return lax.ppermute(shard, axis, pairs)]
    pallas_call x0 -> x6, Pallas kernels: none -> 44 us  [call(): pl.pallas_call(kernel, out_shape=out_shape, in_specs=[smem] * len(scalars...]
    unnamed x7 -> x0, other arithmetic: 32.6 us -> none
    ppermute x0 -> x20, starting transfers between devices: none -> 29.8 us  [turned(): lax.ppermute(value, axis, [(i, (i + by) % count) for i in range(count)])]
    gather x2 -> x0, local copies, waits for them, and re-layouts: 28.2 us -> none  [the longest x1 27.6 us: shards(): picked = column_grad[cells_x, cells_y]]
    ppermute x32 -> x4, waiting for transfers between devices: 27.2 us -> 0.01 us  [passed_along(): return lax.ppermute(shard, axis, pairs)]
    all_to_all x3 -> x1, starting transfers between devices: 27.4 us -> 3.6 us  [shards(): lax.all_to_all(column, ('gx', 'gy'), split_axis=0, concat_axis=0, tiled=T...]
  transfers between devices with their start and end apart: 36 -> 25, of which waited for: 18 -> 10; matrix products, arithmetic and copies ran while one was open for 16% -> 7% of each run, Pallas kernels for 0% -> 9%
where the time goes in v1:
time: 134 us; the launch traced here: 133 us
  starting transfers between devices  44.8 us (33%)
  Pallas kernels  44 us (33%)
  waiting for transfers between devices  20.2 us (15%)
  local copies, waits for them, and re-layouts  17.4 us (13%)
  other arithmetic  5.39 us (4%)
    pallas_call x6, Pallas kernels, call(): pl.pallas_call(kernel, out_shape=out_shape, in_specs=[smem] * len(scalars...  44 us
    ppermute x20, starting transfers between devices, turned(): lax.ppermute(value, axis, [(i, (i + by) % count) for i in range(count)])  29.8 us
    unnamed x44, local copies, waits for them, and re-layouts  14.5 us
    ppermute x20, waiting for transfers between devices, turned(): lax.ppermute(value, axis, [(i, (i + by) % count) for i in range(count)])  14.2 us
    ppermute x4, starting transfers between devices, passed_along(): return lax.ppermute(shard, axis, pairs)  11.4 us
    all_to_all x1, waiting for transfers between devices, shards(): lax.all_to_all(column, ('gx', 'gy'), split_axis=0, concat_axis=0, tiled=T...  5.95 us
    concatenate x2, other arithmetic, y_strip(): jnp.concatenate([own, rim_east[:, :, rows], rim_west[:, :, rows]], axis=1)  3.7 us
    all_to_all x1, starting transfers between devices, shards(): lax.all_to_all(column, ('gx', 'gy'), split_axis=0, concat_axis=0, tiled=T...  3.6 us
  transfers between devices with their start and end apart: 25, of which 10 were waited for; matrix products, arithmetic and copies ran while one was open for 7% of the time, Pallas kernels for 9%

profile of v1, /device:TPU:0, one launch (start us, length us, event | category | flops | bytes accessed | tf_op | source)
XLA Modules:
  0.0 132.6 jit_solution(9498185514769581475)
XLA Ops:
  2.3 4.0 %collective-permute-start.2 = (f32[24,128]{1,0:T(8,128)S(1)}, f32[24,128]{1,0:T(8,128)S(1)}, u32[]{:S(2)}, u32[]{:S(2)}) collective-permute-start(f32[24,128]{1,0:T(8,128)S(1)} %maximum_maximum_fusion.features.refs_2_), channel_id=1, source_target_pairs={{0,16},{8,24},{16,0},{24,8},{1,17},{9,25},{17,1},{25,9},{2,18},{10... | collective-permute-start | bytes 36872 | tf_op jit(solution)/shard_map/ppermute | solution.py:555
  6.3 1.9 %copy-done = f32[6,32,32,128]{3,2,1,0:T(8,128)S(1)} copy-done((f32[6,32,32,128]{3,2,1,0:T(8,128)S(1)}, f32[6,32,32,128]{3,2,1,0:T(8,128)}, u32[]{:S(2)}) %copy-start) | copy-done | bytes 3145752
  10.5 1.6 %collective-permute-start = (f32[152,128]{1,0:T(8,128)S(1)}, f32[152,128]{1,0:T(8,128)S(1)}, u32[]{:S(2)}, u32[]{:S(2)}) collective-permute-start(f32[152,128]{1,0:T(8,128)S(1)} %get-tuple-element.16), channel_id=1, source_target_pairs={{0,8},{8,16},{16,24},{24,0},{1,9},{9,17},{17,25},{25,1},{2,10},{10... | collective-permute-start | bytes 233480 | tf_op jit(solution)/shard_map/ppermute | solution.py:555
  12.1 2.2 %collective-permute-start.1 = (f32[152,128]{1,0:T(8,128)S(1)}, f32[152,128]{1,0:T(8,128)S(1)}, u32[]{:S(2)}, u32[]{:S(2)}) collective-permute-start(f32[152,128]{1,0:T(8,128)S(1)} %get-tuple-element.17), channel_id=1, source_target_pairs={{0,24},{8,0},{16,8},{24,16},{1,25},{9,1},{17,9},{25,17},{2,26},{10... | collective-permute-start | bytes 233480 | tf_op jit(solution)/shard_map/ppermute | solution.py:555
  15.3 1.8 %collective-permute-done.refs_3_ = f32[152,128]{1,0:T(8,128)S(1)} collective-permute-done((f32[152,128]{1,0:T(8,128)S(1)}, f32[152,128]{1,0:T(8,128)S(1)}, u32[]{:S(2)}, u32[]{:S(2)}) %collective-permute-start) | collective-permute-done | bytes 77856 | tf_op jit(solution)/shard_map/ppermute | solution.py:555
  18.1 2.5 %collective-permute-start.9 = (f32[96,128]{1,0:T(8,128)S(1)}, f32[96,128]{1,0:T(8,128)S(1)}, u32[]{:S(2)}, u32[]{:S(2)}) collective-permute-start(f32[96,128]{1,0:T(8,128)S(1)} %get-tuple-element.19.refs_2_), channel_id=1, source_target_pairs={{0,6},{1,7},{2,0},{3,1},{4,2},{5,3},{6,4},{7,5},{8,14},{9,15},{10,... | collective-permute-start | bytes 147464 | tf_op jit(solution)/shard_map/ppermute | solution.py:555
  21.5 2.3 %collective-permute-start.4 = (f32[256,128]{1,0:T(8,128)S(1)}, f32[256,128]{1,0:T(8,128)S(1)}, u32[]{:S(2)}, u32[]{:S(2)}) collective-permute-start(f32[256,128]{1,0:T(8,128)S(1)} %get-tuple-element.21), channel_id=1, source_target_pairs={{0,7},{1,0},{2,1},{3,2},{4,3},{5,4},{6,5},{7,6},{8,15},{9,8},{10,9... | collective-permute-start | bytes 393224 | tf_op jit(solution)/shard_map/ppermute | solution.py:555
  26.7 2.1 %collective-permute-done.6.refs_6_ = f32[96,128]{1,0:T(8,128)S(1)} collective-permute-done((f32[96,128]{1,0:T(8,128)S(1)}, f32[96,128]{1,0:T(8,128)S(1)}, u32[]{:S(2)}, u32[]{:S(2)}) %collective-permute-start.6) | collective-permute-done | bytes 49184 | tf_op jit(solution)/shard_map/ppermute | solution.py:555
  28.9 4.6 %collective-permute-start.11 = (f32[7,4,32,128]{3,2,1,0:T(8,128)S(1)}, f32[7,4,32,128]{3,2,1,0:T(8,128)S(1)}, u32[]{:S(2)}, u32[]{:S(2)}) collective-permute-start(f32[7,4,32,128]{3,2,1,0:T(8,128)S(1)} %pad_maximum_fusion.3), channel_id=1, source_target_pairs={{0,8},{8,16},{16,24},{1,9},{9,17},{17,25},{2,10},{10,18},{18,26},{... | collective-permute-start | bytes 1376264 | tf_op jit(solution)/shard_map/ppermute | solution.py:561
  33.5 3.5 %shard_map.168 = (f32[32,128]{1,0:T(8,128)S(1)}, f32[4,3,5,32,128]{4,3,2,1,0:T(8,128)S(1)}, f32[5,40,128]{2,1,0:T(8,128)S(1)}) custom-call(s32[2]{0:T(128)S(1)} %pad_add_fusion.refs_0_, f32[7,5,32,128]{3,2,1,0:T(8,128)S(1)} %get-tuple-element.18.refs_1_, f32[96,128]{1,0:T(8,128)S(1)} %get-tuple-element.19.refs_2_, ...), custom_call_target="tpu_custom_call" | custom-call | flops 1000000 | bytes 4000000 | tf_op jit(solution)/shard_map/pallas_call | solution.py:538
  37.3 1.6 %collective-permute-start.15 = (f32[32,128]{1,0:T(8,128)S(1)}, f32[32,128]{1,0:T(8,128)S(1)}, u32[]{:S(2)}, u32[]{:S(2)}) collective-permute-start(f32[32,128]{1,0:T(8,128)S(1)} %get-tuple-element.23), channel_id=1, source_target_pairs={{0,16},{8,24},{16,0},{24,8},{1,17},{9,25},{17,1},{25,9},{2,18},{10... | collective-permute-start | bytes 49160 | tf_op jit(solution)/shard_map/ppermute | solution.py:555
  40.3 4.7 %collective-permute-done.14 = f32[32,128]{1,0:T(8,128)S(1)} collective-permute-done((f32[32,128]{1,0:T(8,128)S(1)}, f32[32,128]{1,0:T(8,128)S(1)}, u32[]{:S(2)}, u32[]{:S(2)}) %collective-permute-start.14) | collective-permute-done | bytes 16416 | tf_op jit(solution)/shard_map/ppermute | solution.py:555
  45.1 1.9 %pad_maximum_fusion = f32[7,40,4,128]{3,2,1,0:T(4,128)} fusion(f32[7,4,4,128]{3,2,1,0:T(4,128)S(1)} %get-tuple-element.38, f32[7,4,4,128]{3,2,1,0:T(4,128)S(1)} %get-tuple-element.36, f32[1,32,4,128]{3,2,1,0:T(4,128)} %get-tuple-element.32, f32[6,32,4,128]{3,2,1,0:T(4,128)S(1)} %get-tuple-element.28), kind=kLoop, calls=%fused_computation | loop fusion | flops 430080 | bytes 1146880 | tf_op jit(solution)/shard_map/concatenate | solution.py:638
  48.3 1.8 %pad_maximum_fusion.1 = f32[7,40,4,128]{3,2,1,0:T(4,128)} fusion(f32[7,4,4,128]{3,2,1,0:T(4,128)S(1)} %get-tuple-element.37, f32[7,4,4,128]{3,2,1,0:T(4,128)S(1)} %get-tuple-element.35, f32[1,32,4,128]{3,2,1,0:T(4,128)} %get-tuple-element.31, f32[6,32,4,128]{3,2,1,0:T(4,128)S(1)} %get-tuple-element.27), kind=kLoop, calls=%fused_computation.1 | loop fusion | flops 430080 | bytes 1146880 | tf_op jit(solution)/shard_map/concatenate | solution.py:638
  50.1 4.1 %collective-permute-start.13 = (f32[7,40,4,128]{3,2,1,0:T(4,128)}, f32[7,40,4,128]{3,2,1,0:T(4,128)}, u32[]{:S(2)}, u32[]{:S(2)}) collective-permute-start(f32[7,40,4,128]{3,2,1,0:T(4,128)} %pad_maximum_fusion.1), channel_id=1, source_target_pairs={{0,1},{1,2},{2,3},{3,4},{4,5},{5,6},{6,7},{8,9},{9,10},{10,11},{11... | collective-permute-start | bytes 1720328 | tf_op jit(solution)/shard_map/ppermute | solution.py:561
  54.9 1.5 %collective-permute-start.22 = (f32[128,128]{1,0:T(8,128)S(1)}, f32[128,128]{1,0:T(8,128)S(1)}, u32[]{:S(2)}, u32[]{:S(2)}) collective-permute-start(f32[128,128]{1,0:T(8,128)S(1)} %constant_dynamic-update-slice_fusion.refs_1_), channel_id=1, source_target_pairs={{0,6},{1,7},{2,0},{3,1},{4,2},{5,3},{6,4},{7,5},{8,14},{9,15},{10,... | collective-permute-start | bytes 196616 | tf_op jit(solution)/shard_map/ppermute | solution.py:555
  57.4 3.2 %collective-permute-start.20 = (f32[128,128]{1,0:T(8,128)S(1)}, f32[128,128]{1,0:T(8,128)S(1)}, u32[]{:S(2)}, u32[]{:S(2)}) collective-permute-start(f32[128,128]{1,0:T(8,128)S(1)} %constant_dynamic-update-slice_fusion.refs_1_), channel_id=1, source_target_pairs={{0,4},{1,5},{2,6},{3,7},{4,0},{5,1},{6,2},{7,3},{8,12},{9,13},{10,... | collective-permute-start | bytes 196616 | tf_op jit(solution)/shard_map/ppermute | solution.py:555
  62.4 4.7 %collective-permute-start.19 = (f32[128,128]{1,0:T(8,128)S(1)}, f32[128,128]{1,0:T(8,128)S(1)}, u32[]{:S(2)}, u32[]{:S(2)}) collective-permute-start(f32[128,128]{1,0:T(8,128)S(1)} %constant_dynamic-update-slice_fusion.refs_1_), channel_id=1, source_target_pairs={{0,3},{1,4},{2,5},{3,6},{4,7},{5,0},{6,1},{7,2},{8,11},{9,12},{10,... | collective-permute-start | bytes 196616 | tf_op jit(solution)/shard_map/ppermute | solution.py:555
  69.4 3.0 %collective-permute-done.18.refs_3_ = f32[128,128]{1,0:T(8,128)S(1)} collective-permute-done((f32[128,128]{1,0:T(8,128)S(1)}, f32[128,128]{1,0:T(8,128)S(1)}, u32[]{:S(2)}, u32[]{:S(2)}) %collective-permute-start.18) | collective-permute-done | bytes 65568 | tf_op jit(solution)/shard_map/ppermute | solution.py:555
  78.4 6.0 %shard_map.170 = (f32[8,256]{1,0:T(8,128)}, f32[32,8,128]{2,1,0:T(8,128)}) custom-call(s32[2]{0:T(128)S(1)} %pad_add_fusion.refs_0_, f32[128,128]{1,0:T(8,128)S(1)} %constant_dynamic-update-slice_fusion.refs_1_, f32[128,128]{1,0:T(8,128)S(1)} %collective-permute-done.17.refs_2_, f32[128,128]{1,0:T(8,128)S(1)} %collective-permute-done.18.refs_3_, ...), custom_call_target="tpu_custom_call" | custom-call | flops 1000000 | bytes 4000000 | tf_op jit(solution)/shard_map/pallas_call | solution.py:538
  84.4 3.6 %all-to-all-start = ((f32[32,8,128]{2,1,0:T(8,128)}), f32[32,8,128]{2,1,0:T(8,128)S(1)}, u32[]{:S(2)}, u32[]{:S(2)}) async-start(f32[32,8,128]{2,1,0:T(8,128)} %get-tuple-element.26), calls=%async_computation | async-start | bytes 262144 | tf_op jit(solution)/shard_map/all_to_all | solution.py:683
  90.3 6.0 %all-to-all-done = f32[32,8,128]{2,1,0:T(8,128)S(1)} async-done(((f32[32,8,128]{2,1,0:T(8,128)}), f32[32,8,128]{2,1,0:T(8,128)S(1)}, u32[]{:S(2)}, u32[]{:S(2)}) %all-to-all-start) | async-done | bytes 131104 | tf_op jit(solution)/shard_map/all_to_all | solution.py:683
  97.1 1.6 %shard_map.171 = f32[1,128]{1,0:T(1,128)} custom-call(f32[256,128]{1,0:T(8,128)S(1)} %bitcast.43, f32[128,16]{1,0:T(8,128)S(1)} %copy.18.intersection, s32[128,1]{1,0:T(8,128)S(1)} %copy.19.tile, s32[128,2]{1,0:T(8,128)S(1)} %copy-done.13), custom_call_target="tpu_custom_call" | custom-call | flops 1000000 | bytes 4000000 | tf_op jit(solution)/shard_map/pallas_call | solution.py:538
  101.7 30.9 %shard_map.169 = f32[6,32,32,128]{3,2,1,0:T(8,128)} custom-call(f32[6,32,32,128]{3,2,1,0:T(8,128)S(1)} %copy-done.1, f32[32,32,128]{2,1,0:T(8,128)S(1)} %copy-done.3, f32[5,40,128]{2,1,0:T(8,128)S(1)} %get-tuple-element.22.inverse.refs_17_, f32[7,4,32,128]{3,2,1,0:T(8,128)S(1)} %copy-done.8, f32[7,4,32,128]{3,2,1,0:T(8,128)S(1)} %copy-done.10, ...), custom_call_target="tpu_custom_call" | custom-call | flops 50000000 | bytes 4000000 | tf_op jit(solution)/shard_map/pallas_call | solution.py:538
  (95 shorter events, 30.6 us)
Async XLA Ops:
  2.3 13.1 %collective-permute-start.2 = (f32[24,128]{1,0:T(8,128)S(1)}, f32[24,128]{1,0:T(8,128)S(1)}, u32[]{:S(2)}, u32[]{:S(2)}) collective-permute-start(f32[24,128]{1,0:T(8,128)S(1)} %maximum_maximum_fusion.features.refs_2_), channel_id=1, source_target_pairs={{0,16},{8,24},{16,0},{24,8},{1,17},{9,25},{17,1},{25,9},{2,18},{10... | collective-permute-start | bytes 36872 | tf_op jit(solution)/shard_map/ppermute | solution.py:555
  10.5 6.7 %collective-permute-start = (f32[152,128]{1,0:T(8,128)S(1)}, f32[152,128]{1,0:T(8,128)S(1)}, u32[]{:S(2)}, u32[]{:S(2)}) collective-permute-start(f32[152,128]{1,0:T(8,128)S(1)} %get-tuple-element.16), channel_id=1, source_target_pairs={{0,8},{8,16},{16,24},{24,0},{1,9},{9,17},{17,25},{25,1},{2,10},{10... | collective-permute-start | bytes 233480 | tf_op jit(solution)/shard_map/ppermute | solution.py:555
  12.1 5.2 %collective-permute-start.1 = (f32[152,128]{1,0:T(8,128)S(1)}, f32[152,128]{1,0:T(8,128)S(1)}, u32[]{:S(2)}, u32[]{:S(2)}) collective-permute-start(f32[152,128]{1,0:T(8,128)S(1)} %get-tuple-element.17), channel_id=1, source_target_pairs={{0,24},{8,0},{16,8},{24,16},{1,25},{9,1},{17,9},{25,17},{2,26},{10... | collective-permute-start | bytes 233480 | tf_op jit(solution)/shard_map/ppermute | solution.py:555
  18.1 5.7 %collective-permute-start.9 = (f32[96,128]{1,0:T(8,128)S(1)}, f32[96,128]{1,0:T(8,128)S(1)}, u32[]{:S(2)}, u32[]{:S(2)}) collective-permute-start(f32[96,128]{1,0:T(8,128)S(1)} %get-tuple-element.19.refs_2_), channel_id=1, source_target_pairs={{0,6},{1,7},{2,0},{3,1},{4,2},{5,3},{6,4},{7,5},{8,14},{9,15},{10,... | collective-permute-start | bytes 147464 | tf_op jit(solution)/shard_map/ppermute | solution.py:555
  20.6 4.7 %collective-permute-start.8 = (f32[96,128]{1,0:T(8,128)S(1)}, f32[96,128]{1,0:T(8,128)S(1)}, u32[]{:S(2)}, u32[]{:S(2)}) collective-permute-start(f32[96,128]{1,0:T(8,128)S(1)} %get-tuple-element.19.refs_2_), channel_id=1, source_target_pairs={{0,5},{1,6},{2,7},{3,0},{4,1},{5,2},{6,3},{7,4},{8,13},{9,14},{10,... | collective-permute-start | bytes 147464 | tf_op jit(solution)/shard_map/ppermute | solution.py:555
  20.6 4.8 %collective-permute-start.7 = (f32[96,128]{1,0:T(8,128)S(1)}, f32[96,128]{1,0:T(8,128)S(1)}, u32[]{:S(2)}, u32[]{:S(2)}) collective-permute-start(f32[96,128]{1,0:T(8,128)S(1)} %get-tuple-element.19.refs_2_), channel_id=1, source_target_pairs={{0,4},{1,5},{2,6},{3,7},{4,0},{5,1},{6,2},{7,3},{8,12},{9,13},{10,... | collective-permute-start | bytes 147464 | tf_op jit(solution)/shard_map/ppermute | solution.py:555
  21.1 12.3 %collective-permute-start.3 = (f32[256,128]{1,0:T(8,128)S(1)}, f32[256,128]{1,0:T(8,128)S(1)}, u32[]{:S(2)}, u32[]{:S(2)}) collective-permute-start(f32[256,128]{1,0:T(8,128)S(1)} %get-tuple-element.20), channel_id=1, source_target_pairs={{0,1},{1,2},{2,3},{3,4},{4,5},{5,6},{6,7},{7,0},{8,9},{9,10},{10,1... | collective-permute-start | bytes 393224 | tf_op jit(solution)/shard_map/ppermute | solution.py:555
  21.5 11.9 %collective-permute-start.4 = (f32[256,128]{1,0:T(8,128)S(1)}, f32[256,128]{1,0:T(8,128)S(1)}, u32[]{:S(2)}, u32[]{:S(2)}) collective-permute-start(f32[256,128]{1,0:T(8,128)S(1)} %get-tuple-element.21), channel_id=1, source_target_pairs={{0,7},{1,0},{2,1},{3,2},{4,3},{5,4},{6,5},{7,6},{8,15},{9,8},{10,9... | collective-permute-start | bytes 393224 | tf_op jit(solution)/shard_map/ppermute | solution.py:555
  23.8 21.1 %collective-permute-start.10 = (f32[7,4,32,128]{3,2,1,0:T(8,128)S(1)}, f32[7,4,32,128]{3,2,1,0:T(8,128)S(1)}, u32[]{:S(2)}, u32[]{:S(2)}) collective-permute-start(f32[7,4,32,128]{3,2,1,0:T(8,128)S(1)} %pad_maximum_fusion.2), channel_id=1, source_target_pairs={{8,0},{16,8},{24,16},{9,1},{17,9},{25,17},{10,2},{18,10},{26,18},{... | collective-permute-start | bytes 1376264 | tf_op jit(solution)/shard_map/ppermute | solution.py:561
  25.3 3.6 %collective-permute-start.6 = (f32[96,128]{1,0:T(8,128)S(1)}, f32[96,128]{1,0:T(8,128)S(1)}, u32[]{:S(2)}, u32[]{:S(2)}) collective-permute-start(f32[96,128]{1,0:T(8,128)S(1)} %get-tuple-element.19.refs_2_), channel_id=1, source_target_pairs={{0,3},{1,4},{2,5},{3,6},{4,7},{5,0},{6,1},{7,2},{8,11},{9,12},{10,... | collective-permute-start | bytes 147464 | tf_op jit(solution)/shard_map/ppermute | solution.py:555
  25.4 8.0 %collective-permute-start.5 = (f32[96,128]{1,0:T(8,128)S(1)}, f32[96,128]{1,0:T(8,128)S(1)}, u32[]{:S(2)}, u32[]{:S(2)}) collective-permute-start(f32[96,128]{1,0:T(8,128)S(1)} %get-tuple-element.19.refs_2_), channel_id=1, source_target_pairs={{0,2},{1,3},{2,4},{3,5},{4,6},{5,7},{6,0},{7,1},{8,10},{9,11},{10,... | collective-permute-start | bytes 147464 | tf_op jit(solution)/shard_map/ppermute | solution.py:555
  28.9 16.2 %collective-permute-start.11 = (f32[7,4,32,128]{3,2,1,0:T(8,128)S(1)}, f32[7,4,32,128]{3,2,1,0:T(8,128)S(1)}, u32[]{:S(2)}, u32[]{:S(2)}) collective-permute-start(f32[7,4,32,128]{3,2,1,0:T(8,128)S(1)} %pad_maximum_fusion.3), channel_id=1, source_target_pairs={{0,8},{8,16},{16,24},{1,9},{9,17},{17,25},{2,10},{10,18},{18,26},{... | collective-permute-start | bytes 1376264 | tf_op jit(solution)/shard_map/ppermute | solution.py:561
  37.0 17.2 %collective-permute-start.16 = (f32[32,128]{1,0:T(8,128)S(1)}, f32[32,128]{1,0:T(8,128)S(1)}, u32[]{:S(2)}, u32[]{:S(2)}) collective-permute-start(f32[32,128]{1,0:T(8,128)S(1)} %get-tuple-element.23), channel_id=1, source_target_pairs={{0,24},{8,0},{16,8},{24,16},{1,25},{9,1},{17,9},{25,17},{2,26},{10... | collective-permute-start | bytes 49160 | tf_op jit(solution)/shard_map/ppermute | solution.py:555
  37.3 7.7 %collective-permute-start.15 = (f32[32,128]{1,0:T(8,128)S(1)}, f32[32,128]{1,0:T(8,128)S(1)}, u32[]{:S(2)}, u32[]{:S(2)}) collective-permute-start(f32[32,128]{1,0:T(8,128)S(1)} %get-tuple-element.23), channel_id=1, source_target_pairs={{0,16},{8,24},{16,0},{24,8},{1,17},{9,25},{17,1},{25,9},{2,18},{10... | collective-permute-start | bytes 49160 | tf_op jit(solution)/shard_map/ppermute | solution.py:555
  38.9 6.1 %collective-permute-start.14 = (f32[32,128]{1,0:T(8,128)S(1)}, f32[32,128]{1,0:T(8,128)S(1)}, u32[]{:S(2)}, u32[]{:S(2)}) collective-permute-start(f32[32,128]{1,0:T(8,128)S(1)} %get-tuple-element.23), channel_id=1, source_target_pairs={{0,8},{8,16},{16,24},{24,0},{1,9},{9,17},{17,25},{25,1},{2,10},{10... | collective-permute-start | bytes 49160 | tf_op jit(solution)/shard_map/ppermute | solution.py:555
  47.0 51.7 %collective-permute-start.12 = (f32[7,40,4,128]{3,2,1,0:T(4,128)}, f32[7,40,4,128]{3,2,1,0:T(4,128)}, u32[]{:S(2)}, u32[]{:S(2)}) collective-permute-start(f32[7,40,4,128]{3,2,1,0:T(4,128)} %pad_maximum_fusion), channel_id=1, source_target_pairs={{1,0},{2,1},{3,2},{4,3},{5,4},{6,5},{7,6},{9,8},{10,9},{11,10},{12... | collective-permute-start | bytes 1720328 | tf_op jit(solution)/shard_map/ppermute | solution.py:561
  50.1 48.6 %collective-permute-start.13 = (f32[7,40,4,128]{3,2,1,0:T(4,128)}, f32[7,40,4,128]{3,2,1,0:T(4,128)}, u32[]{:S(2)}, u32[]{:S(2)}) collective-permute-start(f32[7,40,4,128]{3,2,1,0:T(4,128)} %pad_maximum_fusion.1), channel_id=1, source_target_pairs={{0,1},{1,2},{2,3},{3,4},{4,5},{5,6},{6,7},{8,9},{9,10},{10,11},{11... | collective-permute-start | bytes 1720328 | tf_op jit(solution)/shard_map/ppermute | solution.py:561
  54.9 7.5 %collective-permute-start.22 = (f32[128,128]{1,0:T(8,128)S(1)}, f32[128,128]{1,0:T(8,128)S(1)}, u32[]{:S(2)}, u32[]{:S(2)}) collective-permute-start(f32[128,128]{1,0:T(8,128)S(1)} %constant_dynamic-update-slice_fusion.refs_1_), channel_id=1, source_target_pairs={{0,6},{1,7},{2,0},{3,1},{4,2},{5,3},{6,4},{7,5},{8,14},{9,15},{10,... | collective-permute-start | bytes 196616 | tf_op jit(solution)/shard_map/ppermute | solution.py:555
  56.4 10.8 %collective-permute-start.21 = (f32[128,128]{1,0:T(8,128)S(1)}, f32[128,128]{1,0:T(8,128)S(1)}, u32[]{:S(2)}, u32[]{:S(2)}) collective-permute-start(f32[128,128]{1,0:T(8,128)S(1)} %constant_dynamic-update-slice_fusion.refs_1_), channel_id=1, source_target_pairs={{0,5},{1,6},{2,7},{3,0},{4,1},{5,2},{6,3},{7,4},{8,13},{9,14},{10,... | collective-permute-start | bytes 196616 | tf_op jit(solution)/shard_map/ppermute | solution.py:555
  57.4 11.1 %collective-permute-start.20 = (f32[128,128]{1,0:T(8,128)S(1)}, f32[128,128]{1,0:T(8,128)S(1)}, u32[]{:S(2)}, u32[]{:S(2)}) collective-permute-start(f32[128,128]{1,0:T(8,128)S(1)} %constant_dynamic-update-slice_fusion.refs_1_), channel_id=1, source_target_pairs={{0,4},{1,5},{2,6},{3,7},{4,0},{5,1},{6,2},{7,3},{8,12},{9,13},{10,... | collective-permute-start | bytes 196616 | tf_op jit(solution)/shard_map/ppermute | solution.py:555
  62.4 7.0 %collective-permute-start.19 = (f32[128,128]{1,0:T(8,128)S(1)}, f32[128,128]{1,0:T(8,128)S(1)}, u32[]{:S(2)}, u32[]{:S(2)}) collective-permute-start(f32[128,128]{1,0:T(8,128)S(1)} %constant_dynamic-update-slice_fusion.refs_1_), channel_id=1, source_target_pairs={{0,3},{1,4},{2,5},{3,6},{4,7},{5,0},{6,1},{7,2},{8,11},{9,12},{10,... | collective-permute-start | bytes 196616 | tf_op jit(solution)/shard_map/ppermute | solution.py:555
  67.2 5.2 %collective-permute-start.18 = (f32[128,128]{1,0:T(8,128)S(1)}, f32[128,128]{1,0:T(8,128)S(1)}, u32[]{:S(2)}, u32[]{:S(2)}) collective-permute-start(f32[128,128]{1,0:T(8,128)S(1)} %constant_dynamic-update-slice_fusion.refs_1_), channel_id=1, source_target_pairs={{0,2},{1,3},{2,4},{3,5},{4,6},{5,7},{6,0},{7,1},{8,10},{9,11},{10,... | collective-permute-start | bytes 196616 | tf_op jit(solution)/shard_map/ppermute | solution.py:555
  68.5 4.6 %collective-permute-start.17 = (f32[128,128]{1,0:T(8,128)S(1)}, f32[128,128]{1,0:T(8,128)S(1)}, u32[]{:S(2)}, u32[]{:S(2)}) collective-permute-start(f32[128,128]{1,0:T(8,128)S(1)} %constant_dynamic-update-slice_fusion.refs_1_), channel_id=1, source_target_pairs={{0,1},{1,2},{2,3},{3,4},{4,5},{5,6},{6,7},{7,0},{8,9},{9,10},{10,1... | collective-permute-start | bytes 196616 | tf_op jit(solution)/shard_map/ppermute | solution.py:555
  84.4 11.8 %all-to-all-start = ((f32[32,8,128]{2,1,0:T(8,128)}), f32[32,8,128]{2,1,0:T(8,128)S(1)}, u32[]{:S(2)}, u32[]{:S(2)}) async-start(f32[32,8,128]{2,1,0:T(8,128)} %get-tuple-element.26), calls=%async_computation | async-start | bytes 262144 | tf_op jit(solution)/shard_map/all_to_all | solution.py:683
  (20 other events, 216.7 us)

commit v2 on v1

v2 whole, which is shorter than its diff:
```python
import math

import jax
import jax.numpy as jnp
import numpy as np
from jax import lax
from jax.experimental import pallas as pl
from jax.experimental.pallas import tpu as pltpu
from jax.sharding import PartitionSpec as P

TILE = 32
P_DEV = 128
NT = 4
ZP = 4
U = 256
V = 256
ZM = 64

COURANT = 0.5
ANGULAR_STEP = 0.9
DELTA_EPS = 4.0

HALO = 4
EXT = TILE + 2 * HALO
BAND = 16
BAND_START = ZM - BAND // 2
GROUPS = 128 // BAND
RUN = EXT // GROUPS
LANES = RUN * 128
FEATURES = 24
RIM_ROWS = 4 * TILE
SIDE_ROWS = 4 * RUN * 8
FOLD = 24
ARRAYS = 7
AHEAD = 8
REACH = 48
YPAD = 64
UNROLL = 8
BF16 = jnp.bfloat16
F32 = jnp.float32


def split_table(table):
    table = np.asarray(table, np.float32)
    high = table.astype(jnp.bfloat16)
    low = (table - high.astype(np.float32)).astype(jnp.bfloat16)
    return np.stack([high, low])


def phase_table(count_out, count_in):
    focal_pos = (np.arange(count_out) + 0.5) / count_out - 0.5
    cell_pos = (np.arange(count_in) + 0.5) / count_in - 0.5
    squared = ((focal_pos[:, None] - cell_pos[None, :]) ** 2).astype(np.float32)
    phase = (np.float32(math.pi * count_out) * squared).astype(np.float64)
    return np.cos(phase), np.sin(phase)


def round_cells(place, count):
    cells = np.arange(EXT)
    cells = np.where(cells < TILE + HALO, cells, cells - EXT) + place * TILE
    return cells, (cells >= 0) & (cells < count * TILE)


def packed_lane(cell, layer):
    return (cell % RUN) * 128 + (cell // RUN) * BAND + layer - BAND_START


def tables(span_x, span_y):
    count_x, count_y = span_x * TILE, span_y * TILE
    norm = (count_x * count_y) ** -0.5
    x_re, x_im = phase_table(U, count_x)
    y_re, y_im = phase_table(V, count_y)
    xr = x_re.reshape(U, span_x, 1, TILE)
    xi = x_im.reshape(U, span_x, 1, TILE)
    first = np.concatenate(
        [
            np.concatenate([xr, -xi], axis=2).reshape(U, -1),
            np.concatenate([xi, xr], axis=2).reshape(U, -1),
        ]
    )
    second = norm * np.block([[y_re.T, y_im.T], [-y_im.T, y_re.T]])
    back_y = np.zeros((span_y, 2 * YPAD, 2 * V))
    for place in range(span_y):
        cells, inside = round_cells(place, span_y)
        for row in range(EXT):
            if inside[row]:
                re, im = y_re[:, cells[row]], y_im[:, cells[row]]
                back_y[place, row] = np.concatenate([re, -im])
                back_y[place, YPAD + row] = np.concatenate([im, re])
    back_x = np.zeros((span_x, U, 2 * YPAD))
    for place in range(span_x):
        cells, inside = round_cells(place, span_x)
        for row in range(EXT):
            if inside[row]:
                back_x[place, :, row] = 2.0 * norm * x_re[:, cells[row]]
                back_x[place, :, YPAD + row] = 2.0 * norm * x_im[:, cells[row]]
    return (
        split_table(first),
        split_table(second),
        np.moveaxis(split_table(back_y), 0, 1),
        np.moveaxis(split_table(back_x), 0, 1),
    )


def choosers():
    window = np.zeros((4, REACH, 128), np.float32)
    for step in range(4):
        for row in range(REACH):
            cell = row - AHEAD + step
            if -HALO <= cell < TILE + HALO:
                window[step, row, cell % EXT] = 1.0
    fill = np.zeros((128, LANES), np.float32)
    for cell in range(EXT):
        for layer in range(ZM - ZP, ZM):
            fill[cell, packed_lane(cell, layer)] = DELTA_EPS
    monitor = np.zeros((LANES, 128), np.float32)
    column = np.zeros((LANES, 128), np.float32)
    for cell in range(TILE):
        monitor[packed_lane(cell, ZM), cell] = 1.0
        for layer in range(ZM - ZP, ZM):
            column[packed_lane(cell, layer), cell] = 1.0
    source = np.zeros((128, LANES), np.float32)
    for cell in range(EXT):
        source[cell, packed_lane(cell, ZM)] = 1.0
    return [table.astype(jnp.bfloat16) for table in (window, fill, monitor, column, source)]


def halves(value):
    high = value.astype(BF16)
    return high, (value - high.astype(F32)).astype(BF16)


def dot(first_op, second_op):
    return jnp.dot(first_op, second_op, preferred_element_type=F32)


def dot_rows(first_op, second_op):
    return lax.dot_general(first_op, second_op, (((1,), (1,)), ((), ())), preferred_element_type=F32)


def lanes_of(shape):
    return lax.broadcasted_iota(jnp.int32, shape, 1)


def rows_of(shape):
    return lax.broadcasted_iota(jnp.int32, shape, 0)


def my_place():
    return lax.axis_index("gx"), lax.axis_index("gy")


def start_copies(pairs, semaphores):
    copies = [pltpu.make_async_copy(source, dest, semaphores.at[at]) for at, (source, dest) in enumerate(pairs)]
    for copy in copies:
        copy.start()
    return copies


def pack_kernel(
    span_y, fields, eps, intersection, widths, tile, anchors,
    packed, pay_a, pay_b, features, strip_a, strip_b,
    held, held_intersection, held_widths, held_tile, held_anchors, arriving, leaving,
):
    pairs = [(eps if at == 6 else fields.at[at], held.at[at]) for at in range(ARRAYS)]
    small = ((intersection, held_intersection), (widths, held_widths), (tile, held_tile), (anchors, held_anchors))
    arrivals = start_copies(list(small) + pairs, arriving)
    for arrival in arrivals[:4]:
        arrival.wait()
    arrivals = arrivals[4:]
    intersection, widths, tile, anchors = held_intersection, held_widths, held_tile, held_anchors
    values = intersection[...] * widths[...]
    place = tile[...]
    start_x = (lax.div(place, span_y) * TILE + anchors[0:1]).astype(F32)
    start_y = (lax.rem(place, span_y) * TILE + anchors[1:2]).astype(F32)
    row = rows_of((8, P_DEV))
    corner = jnp.where(row == 0, start_x, jnp.where(row == 1, start_y, 0.0))
    for ref, offset in ((features, 0), (pay_a, RIM_ROWS), (pay_b, RIM_ROWS)):
        ref[offset : offset + 16] = values
        ref[offset + 16 : offset + FEATURES] = corner
    group = lanes_of((TILE, 128)) // BAND
    even = my_place()[0] % 2 == 0
    edge_a = jnp.where(even, TILE - HALO, 0)
    edge_b = jnp.where(even, 0, TILE - HALO)
    departures = []
    built = {}
    for array in range(ARRAYS):
        arrivals[array].wait()
        for at, (strip, start) in enumerate(((strip_a, edge_a), (strip_b, edge_b))):
            copy = pltpu.make_async_copy(
                held.at[array, pl.ds(start, HALO)], strip.at[array], leaving.at[2 * array + at]
            )
            copy.start()
            departures.append(copy)
        kept = [jnp.zeros((TILE, 128), F32) for _ in range(RUN)]
        for x in range(TILE):
            at = x // RUN
            moved = pltpu.roll(held[array, x], (BAND * at - BAND_START) % 128, 1)
            kept[x % RUN] = jnp.where(group == at, moved, kept[x % RUN])
        for run in range(RUN):
            packed[array, run] = kept[run]
        for name, pay, start in (("a", pay_a, edge_a), ("b", pay_b, edge_b)):
            block = built.get(name, jnp.zeros((TILE, 128), F32))
            for step in range(HALO):
                at = (array % 2) * 4 + step
                moved = pltpu.roll(held[array, start + step], (BAND * at - BAND_START) % 128, 1)
                block = jnp.where(group == at, moved, block)
            if array % 2 == 1 or array == ARRAYS - 1:
                pay[array // 2 * TILE : (array // 2 + 1) * TILE] = block
                built.pop(name, None)
            else:
                built[name] = block
    for copy in departures:
        copy.wait()


def paired_low(even, odd):
    return jnp.where(rows_of((8, 128)) < 4, even, pltpu.roll(odd, 4, 0))


def paired_high(even, odd):
    return jnp.where(rows_of((8, 128)) < 4, pltpu.roll(even, 4, 0), odd)


def rim_of(north, south, at):
    return paired_low(north, south) if at % 2 == 0 else paired_high(north, south)


def widen_kernel(span_x, packed, from_a, from_b, wide, pay_a, pay_b):
    place = my_place()
    even_x, even_y = place[0] % 2 == 0, place[1] % 2 == 0
    group = lanes_of((TILE, 128)) // BAND
    has_west = place[0] > 0
    has_east = place[0] < span_x - 1
    for array in range(ARRAYS):
        kept = [packed[array, run] for run in range(RUN)]
        rows = slice((array // 2) * TILE, (array // 2 + 1) * TILE)
        first, second = from_a[rows], from_b[rows]
        east = jnp.where(has_east, jnp.where(even_x, first, second), 0.0)
        west = jnp.where(has_west, jnp.where(even_x, second, first), 0.0)
        for step in range(HALO):
            at = (array % 2) * 4 + step
            for block, x in ((east, TILE + step), (west, TILE + HALO + step)):
                to = x // RUN
                moved = pltpu.roll(block, (BAND * (to - at)) % 128, 1)
                kept[x % RUN] = jnp.where(group == to, moved, kept[x % RUN])
        for run in range(RUN):
            wide[array, run] = kept[run]
    for block in range(4):
        for run in range(RUN):
            even, odd = 2 * block, min(2 * block + 1, ARRAYS - 1)
            rows = slice((block * RUN + run) * 8, (block * RUN + run + 1) * 8)
            south = paired_low(wide[even, run, 0:8], wide[odd, run, 0:8])
            north = paired_high(wide[even, run, TILE - 8 :], wide[odd, run, TILE - 8 :])
            pay_a[rows] = jnp.where(even_y, north, south)
            pay_b[rows] = jnp.where(even_y, south, north)

def windows_kernel(span_x, span_y, features, from_a, from_b, *rest):
    others, window_table, (windows, ends, starts) = rest[: span_x - 3], rest[span_x - 3], rest[span_x - 2 :]
    place = my_place()
    every = [(features, 0), (from_a, RIM_ROWS), (from_b, RIM_ROWS)] + [(other, 0) for other in others]
    cell_x = (rows_of((REACH, 128)) - AHEAD + place[0] * TILE).astype(F32)
    row = rows_of((EXT, 128))
    cell_y = jnp.where(row < TILE + HALO, row, row - EXT)
    high_rows, low_rows = 4 * EXT * span_y, 8 * EXT * span_y
    for chunk, (ref, base) in enumerate(every):
        lanes = slice(chunk * 128, (chunk + 1) * 128)
        ends[:, lanes] = (cell_x == ref[base + 16 : base + 17]).astype(F32).astype(BF16)
        start_y = ref[base + 17 : base + 18]
        for by in range(span_y):
            ahead = (cell_y + by * TILE).astype(F32) - start_y
            hits = [ahead == float(step) for step in range(4)]
            for step_x in range(4):
                value = jnp.zeros((EXT, 128), F32)
                for step_y in range(4):
                    k = base + 4 * step_x + step_y
                    value = jnp.where(hits[step_y], ref[k : k + 1], value)
                high, low = halves(value)
                at = (4 * by + step_x) * EXT
                starts[at : at + EXT, lanes] = high
                starts[high_rows + at : high_rows + at + EXT, lanes] = low
    counted = dot_rows(starts[...], ends[...])
    counted = counted[:high_rows] + counted[high_rows:low_rows]
    for by in range(span_y):
        window = jnp.zeros((EXT, 128), F32)
        for step_x in range(4):
            at = (4 * by + step_x) * EXT
            high, low = halves(counted[at : at + EXT])
            window = window + dot(high, window_table[step_x]) + dot(low, window_table[step_x])
        windows[by, :16] = window[:16] + pltpu.roll(window[FOLD:], 64, 1)
        windows[by, 16:] = window[16:FOLD]


def strips_kernel(span_x, fields, eps, rim_a, rim_b, pay_a, pay_b, first, last, arriving):
    place = my_place()
    even_x, even_y = place[0] % 2 == 0, place[1] % 2 == 0
    pairs = []
    for array in range(ARRAYS):
        own = eps if array == 6 else fields.at[array]
        pairs += [(own.at[:, 0:8], first.at[array]), (own.at[:, TILE - 8 : TILE], last.at[array])]
    arrivals = start_copies(pairs, arriving)

    def pair(array, at, even, odd):
        south = paired_low(even[0:8], odd[0:8])
        north = paired_high(even[-8:], odd[-8:])
        pay_a[array, at] = jnp.where(even_y, north, south)
        pay_b[array, at] = jnp.where(even_y, south, north)

    for before, offset, present in (
        (even_x, (HALO + TILE) // 2, place[0] < span_x - 1),
        (jnp.logical_not(even_x), 0, place[0] > 0),
    ):
        for array in range(ARRAYS):
            for at in range(HALO // 2):
                blocks = (jnp.where(before, rim_a[array, 2 * at + side], rim_b[array, 2 * at + side]) for side in range(2))
                pair(array, offset + at, *(jnp.where(present, block, 0.0) for block in blocks))
    for array in range(ARRAYS):
        arrivals[2 * array].wait()
        arrivals[2 * array + 1].wait()
        for at in range(TILE // 2):
            blocks = (
                jnp.concatenate([first[array, 2 * at + side], last[array, 2 * at + side]], axis=0) for side in range(2)
            )
            pair(array, HALO // 2 + at, *blocks)


def packed_ahead_x(ref, component, run):
    if run < RUN - 1:
        return ref[component, run + 1]
    return pltpu.roll(ref[component, 0], 128 - BAND, 1)


def packed_behind_x(ref, component, run):
    if run > 0:
        return ref[component, run - 1]
    return pltpu.roll(ref[component, RUN - 1], BAND, 1)


def ahead_y(value):
    return pltpu.roll(value, EXT - 1, 0)


def behind_y(value):
    return pltpu.roll(value, 1, 0)


def ahead_z(value):
    return pltpu.roll(value, 127, 1)


def behind_z(value):
    return pltpu.roll(value, 1, 1)


def packed_magnetic(elec, magn, half_magn):
    for run in range(RUN):
        ex, ey, ez = elec[0, run], elec[1, run], elec[2, run]
        ey_next, ez_next = packed_ahead_x(elec, 1, run), packed_ahead_x(elec, 2, run)
        rate = half_magn[run]
        magn[0, run] = magn[0, run] - rate * ((ahead_y(ez) - ez) - (ahead_z(ey) - ey))
        magn[1, run] = magn[1, run] - rate * ((ahead_z(ex) - ex) - (ez_next - ez))
        magn[2, run] = magn[2, run] - rate * ((ey_next - ey) - (ahead_y(ex) - ex))


def packed_curl(magn, run):
    hx, hy, hz = magn[0, run], magn[1, run], magn[2, run]
    hy_last, hz_last = packed_behind_x(magn, 1, run), packed_behind_x(magn, 2, run)
    return (
        (hz - behind_y(hz)) - (hy - behind_z(hy)),
        (hx - behind_z(hx)) - (hz - hz_last),
        (hy - hy_last) - (hx - behind_y(hx)),
    )


def packed_inside(place, span_x, span_y, run):
    shape = (EXT, 128)
    cell_x = (lanes_of(shape) // BAND) * RUN + run
    cell_y = rows_of(shape)

    def side(cell, at, span):
        last = jnp.where(at < span - 1, TILE + HALO, TILE)
        first = jnp.where(at > 0, TILE + HALO, EXT)
        return (cell < last) | (cell >= first)

    return side(cell_x, place[0], span_x) & side(cell_y, place[1], span_y)


def forward_kernel(
    span_x, span_y, wide, windows, from_a, from_b, fill_table, monitor_table,
    monitor, changes, inverse, half_magn, elec, magn, mons,
):
    place = my_place()
    folded = windows[0]
    for by in range(1, span_y):
        folded = folded + windows[by]
    filling = jnp.concatenate([folded, pltpu.roll(folded[:16], 64, 1)], axis=0)
    high, low = halves(jnp.where(lanes_of((EXT, 128)) < EXT, filling, 0.0))
    filled = dot(high, fill_table[...]) + dot(low, fill_table[...])
    even_y = place[1] % 2 == 0
    has_south = place[1] > 0
    has_north = place[1] < span_y - 1
    for array in range(ARRAYS):
        for run in range(RUN):
            at = ((array // 2) * RUN + run) * 8
            first, second = from_a[at : at + 8], from_b[at : at + 8]
            north = jnp.where(has_north, jnp.where(even_y, first, second), 0.0)
            south = jnp.where(has_south, jnp.where(even_y, second, first), 0.0)
            rim = rim_of(north, south, array)
            if array < 3:
                elec[array, run, :TILE] = wide[array, run]
                elec[array, run, TILE:] = rim
            elif array < 6:
                magn[array - 3, run, :TILE] = wide[array, run]
                magn[array - 3, run, TILE:] = rim
            else:
                inside = packed_inside(place, span_x, span_y, run)
                eps = jnp.concatenate([wide[array, run], rim], axis=0)
                eps = eps + filled[:, run * 128 : (run + 1) * 128]
                inverse[run] = jnp.where(inside, 1.0 / jnp.where(inside, eps, 1.0), 0.0)
                half_magn[run] = jnp.where(inside, COURANT, 0.0)
    for moment in range(1, NT + 1):
        packed_magnetic(elec, magn, half_magn)
        cos, sin = math.cos(ANGULAR_STEP * moment), math.sin(ANGULAR_STEP * moment)
        for run in range(RUN):
            rate = COURANT * inverse[run]
            for component, curl in enumerate(packed_curl(magn, run)):
                change = curl * rate
                now = elec[component, run] + change
                elec[component, run] = now
                changes[moment - 1, component, run] = change[:TILE]
                if component < 2:
                    own = now[:TILE]
                    if moment == 1:
                        mons[2 * component, run] = cos * own
                        mons[2 * component + 1, run] = -sin * own
                    else:
                        mons[2 * component, run] += cos * own
                        mons[2 * component + 1, run] += -sin * own
    built = jnp.zeros((4 * TILE, 128), F32)
    for run in range(RUN):
        high, low = halves(mons[:, run].reshape(4 * TILE, 128))
        table = monitor_table[run * 128 : (run + 1) * 128]
        built = built + dot(high, table) + dot(low, table)
    payload = built[:TILE]
    for part in range(1, 4):
        payload = payload + pltpu.roll(built[part * TILE : (part + 1) * TILE], part * TILE, 1)
    for at in range(span_x * span_y):
        monitor[at] = payload


def focal_kernel(
    span_x, span_y, gathered, first, second, back_y, back_x, column_table, source_table, target, changes, inverse,
    power, column, *rest,
):
    place = my_place()
    held = rest[:10]
    sums, elec, magn, half_magn, drive, grads, arriving = rest[10:]
    sources = (
        gathered, first, second, target, back_y.at[place[1]], back_x.at[place[0]], source_table, inverse, changes,
        column_table,
    )
    arrivals = start_copies(list(zip(sources, held, strict=True)), arriving)
    gathered, first, second, target, back_y, back_x, source_table, inverse, changes, column_table = held
    count_y = span_y * TILE
    arrivals[0].wait()
    arrivals[1].wait()
    left = lanes_of((count_y, 128)) < 64
    total = jnp.zeros((U, V), F32)
    half_parts = []
    for component in range(2):
        pieces = []
        for pair in range(span_x // 2):
            even, odd = (
                gathered[(2 * pair + at) * span_y : (2 * pair + at + 1) * span_y].reshape(count_y, 128) for at in range(2)
            )
            if component == 0:
                pieces.append(jnp.where(left, even, pltpu.roll(odd, 64, 1)))
            else:
                pieces.append(jnp.where(left, pltpu.roll(even, 64, 1), odd))
        high, low = halves(jnp.concatenate(pieces, axis=1))
        part = dot_rows(first[0], high) + dot_rows(first[0], low) + dot_rows(first[1], high)
        high, low = halves(part)
        if component == 0:
            arrivals[2].wait()
            arrivals[3].wait()
            arrivals[4].wait()
        far = jnp.zeros((U, 2 * V), F32)
        for at, rows in ((0, slice(0, U)), (1, slice(U, 2 * U))):
            span = slice(at * count_y, (at + 1) * count_y)
            far = far + dot(high[rows], second[0, span]) + dot(low[rows], second[0, span])
            far = far + dot(high[rows], second[1, span])
        far_re, far_im = far[:, :V], far[:, V:]
        total = total + far_re * far_re + far_im * far_im
        weighted = jnp.concatenate([target[...] * far_re, -(target[...] * far_im)], axis=1)
        high, low = halves(weighted)
        half_parts.append(dot_rows(back_y[0], high) + dot_rows(back_y[0], low) + dot_rows(back_y[1], high))
    sums[...] = total
    devices = span_x * span_y
    rows = U // devices
    start = (place[0] * span_y + place[1]) * rows
    if rows % 8 == 0:
        power[...] = sums[pl.ds(pl.multiple_of(start, 8), rows)]
    else:
        near = sums[pl.ds(pl.multiple_of((start // 8) * 8, 8), 8)]
        spot = rows_of((8, V))
        for at in range(rows):
            mine = jnp.where(spot == start % 8 + at, near, 0.0)
            power[at : at + 1] = jnp.sum(mine, axis=0, keepdims=True)
    for arrival in arrivals[5:]:
        arrival.wait()
    high, low = halves(jnp.concatenate(half_parts, axis=0))
    back = dot(high, back_x[0]) + dot(low, back_x[0]) + dot(high, back_x[1])
    turned = pltpu.roll(back, YPAD, 1)
    lanes_ok = lanes_of((YPAD, 128)) < EXT
    for component in range(2):
        re = slice(2 * component * YPAD, (2 * component + 1) * YPAD)
        im = slice((2 * component + 1) * YPAD, (2 * component + 2) * YPAD)
        for at, value in ((0, back[re] - turned[im]), (1, back[im] + turned[re])):
            high, low = halves(jnp.where(lanes_ok, value, 0.0))
            placed = dot(high, source_table[...]) + dot(low, source_table[...])
            for run in range(RUN):
                drive[2 * component + at, run] = placed[:EXT, run * 128 : (run + 1) * 128]
    for run in range(RUN):
        inside = packed_inside(place, span_x, span_y, run)
        half_magn[run] = jnp.where(inside, COURANT, 0.0)
        grads[run] = jnp.zeros((TILE, 128), F32)
        for component in range(3):
            elec[component, run] = jnp.zeros((EXT, 128), F32)
            magn[component, run] = jnp.zeros((EXT, 128), F32)
    for moment in range(1, NT + 1):
        step = NT + 1 - moment
        cos, sin = math.cos(ANGULAR_STEP * step), math.sin(ANGULAR_STEP * step)
        if moment > 1:
            packed_magnetic(elec, magn, half_magn)
        for run in range(RUN):
            rate = COURANT * inverse[run]
            for component, curl in enumerate(packed_curl(magn, run)):
                if component < 2:
                    curl = curl - (cos * drive[2 * component, run] + sin * drive[2 * component + 1, run])
                now = elec[component, run] + curl * rate
                elec[component, run] = now
                grads[run] += now[:TILE] * changes[step - 1, component, run]
    built = jnp.zeros((TILE, 128), F32)
    for run in range(RUN):
        high, low = halves(-grads[run] * inverse[run, :TILE])
        table = column_table[run * 128 : (run + 1) * 128]
        built = built + dot(high, table) + dot(low, table)
    payload = built[:8]
    for part in range(1, TILE // 8):
        payload = payload + pltpu.roll(built[8 * part : 8 * part + 8], part * TILE, 1)
    for at in range(devices):
        column[at] = payload


def widths_kernel(received, intersection, tile, anchors, grad):
    high, low = halves(received[...])
    rows = received.shape[0]
    spot = rows_of((rows, P_DEV))
    lane = rows_of((128, P_DEV))
    anchor_x, anchor_y = anchors[0:1], anchors[1:2]
    contracted = (((0,), (0,)), ((), ()))
    total = jnp.zeros((128, P_DEV), F32)
    for step_y in range(4):
        cell_y = anchor_y + step_y
        chosen = (spot == tile[...] * 8 + (cell_y & 7)).astype(F32).astype(BF16)
        values = lax.dot_general(high, chosen, contracted, preferred_element_type=F32)
        values = values + lax.dot_general(low, chosen, contracted, preferred_element_type=F32)
        ahead = lane - ((cell_y >> 3) * TILE + anchor_x)
        for step_x in range(4):
            k = 4 * step_x + step_y
            total = total + jnp.where(ahead == step_x, values * intersection[k : k + 1], 0.0)
    grad[...] = DELTA_EPS * jnp.sum(total, axis=0, keepdims=True)


def full_kernel(
    span_x, span_y, fields, eps, rim_a, rim_b, inverse, from_a, from_b,
    out, one, two, rate_elec, rate_magn, held, arriving, leaving,
):
    place = my_place()
    even_x, even_y = place[0] % 2 == 0, place[1] % 2 == 0
    side_a = jnp.where(even_x, HALO + TILE, 0)
    side_b = jnp.where(even_x, 0, HALO + TILE)
    pairs = []
    for array in range(ARRAYS):
        dest = rate_elec if array == 6 else one.at[array]
        own = eps if array == 6 else fields.at[array]
        pairs.append((rim_a.at[array], dest.at[pl.ds(side_a, HALO), :TILE]))
        pairs.append((own, dest.at[HALO : HALO + TILE, :TILE]))
        pairs.append((rim_b.at[array], dest.at[pl.ds(side_b, HALO), :TILE]))
    arrivals = start_copies(pairs, arriving)
    lane = lanes_of((EXT, 128))
    in_layers = (lane >= ZM - ZP) & (lane < ZM)
    below_top = lane < 127
    above_bottom = lane > 0
    has_south = place[1] > 0
    has_north = place[1] < span_y - 1
    for array in range(ARRAYS):
        dest = rate_elec if array == 6 else one.at[array]
        for at in range(EXT // 2):
            first, second = from_a[array, at], from_b[array, at]
            north = jnp.where(has_north, jnp.where(even_y, first, second), 0.0)
            south = jnp.where(has_south, jnp.where(even_y, second, first), 0.0)
            for odd in range(2):
                dest[2 * at + odd, TILE:] = rim_of(north, south, odd)
    for arrival in arrivals:
        arrival.wait()
    for present, offset in ((place[0] > 0, 0), (place[0] < span_x - 1, HALO + TILE)):

        @pl.when(jnp.logical_not(present))
        def _():
            blank = jnp.zeros((EXT, 128), F32)
            for step in range(HALO):
                rate_elec[offset + step] = blank
                for array in range(6):
                    one[array, offset + step] = blank

    for x in range(EXT):
        cell = (x - HALO) % EXT
        spread = pltpu.roll(inverse[cell % RUN], (BAND_START - BAND * (cell // RUN)) % 128, 1)
        value = rate_elec[x]
        inside = value > 0.0
        plain = jnp.where(inside, 1.0 / jnp.where(inside, value, 1.0), 0.0)
        rate_elec[x] = COURANT * jnp.where(in_layers, spread, plain)
        rate_magn[x] = jnp.where(inside, COURANT, 0.0)

    def magnetic(rate, magn, ex, ey, ez, ey_next, ez_next):
        hx, hy, hz = magn
        dz_ey = jnp.where(below_top, ahead_z(ey), 0.0) - ey
        dz_ex = jnp.where(below_top, ahead_z(ex), 0.0) - ex
        return (
            hx - rate * ((ahead_y(ez) - ez) - dz_ey),
            hy - rate * (dz_ex - (ez_next - ez)),
            hz - rate * ((ey_next - ey) - (ahead_y(ex) - ex)),
        )

    def electric(rate, elec, hx, hy, hz, hy_last, hz_last):
        ex, ey, ez = elec
        dz_hy = hy - jnp.where(above_bottom, behind_z(hy), 0.0)
        dz_hx = hx - jnp.where(above_bottom, behind_z(hx), 0.0)
        return (
            ex + rate * ((hz - behind_y(hz)) - dz_hy),
            ey + rate * (dz_hx - (hz - hz_last)),
            ez + rate * ((hy - hy_last) - (hx - behind_y(hx))),
        )

    def sweep(source, dest, start, stop, shift, state):
        def read(first, x):
            return tuple(source[first + component, x] for component in range(3))

        def advance(x, state):
            elec, hy_last, hz_last = state
            after = read(0, x + 1)
            magn = magnetic(rate_magn[x], read(3, x), *elec, after[1], after[2])
            new = electric(rate_elec[x], elec, *magn, hy_last, hz_last) + magn
            for array in range(6):
                dest[array, x - shift] = new[array][:TILE] if shift else new[array]
            return after, magn[1], magn[2]

        if state is None:
            before, elec = read(0, start - 1), read(0, start)
            magn = magnetic(rate_magn[start - 1], read(3, start - 1), *before, elec[1], elec[2])
            state = elec, magn[1], magn[2]

        def cells(at, state):
            for step in range(UNROLL):
                state = advance(start + UNROLL * at + step, state)
            return state

        whole = (stop - start) // UNROLL
        state = lax.fori_loop(0, whole, cells, state)
        for x in range(start + UNROLL * whole, stop):
            state = advance(x, state)
        return state

    for moment in range(1, NT):
        source, dest = (one, two) if moment % 2 == 1 else (two, one)
        sweep(source, dest, moment, EXT - moment, 0, None)
    state = None
    departures = []
    source = one if NT % 2 == 1 else two
    for part in range(2):
        begin, end = part * TILE // 2, (part + 1) * TILE // 2
        state = sweep(source, held, HALO + begin, HALO + end, HALO, state)
        for array in range(6):
            copy = pltpu.make_async_copy(
                held.at[array, begin:end], out.at[array, begin:end], leaving.at[6 * part + array]
            )
            copy.start()
            departures.append(copy)
    for copy in departures:
        copy.wait()


def call(kernel, out_shape, operands, scratch=(), micros=1.0, room=52, anywhere=(), out_anywhere=()):
    vmem = pl.BlockSpec(memory_space=pltpu.VMEM)
    hbm = pl.BlockSpec(memory_space=pl.ANY)
    many = isinstance(out_shape, (tuple, list))
    out_specs = [hbm if at in out_anywhere else vmem for at in range(len(out_shape) if many else 1)]
    return pl.pallas_call(
        kernel,
        out_shape=out_shape,
        in_specs=[hbm if at in anywhere else vmem for at in range(len(operands))],
        out_specs=out_specs if many else out_specs[0],
        scratch_shapes=list(scratch),
        compiler_params=pltpu.CompilerParams(vmem_limit_bytes=room * 1024 * 1024),
        cost_estimate=pl.CostEstimate(flops=1_000_000, bytes_accessed=int(3e6 * micros), transcendentals=0),
    )(*operands)


def shape_of(*dims, dtype=F32):
    return jax.ShapeDtypeStruct(dims, dtype)


def matchings(count):
    circle = count - 1
    pairings = []
    for turn in range(circle):
        partner = {turn: circle, circle: turn}
        for step in range(1, count // 2):
            one, other = (turn + step) % circle, (turn - step) % circle
            partner[one], partner[other] = other, one
        pairings.append(partner)
    ring = [0]
    while len(ring) < count:
        ring.append(pairings[(len(ring) + 1) % 2][ring[-1]])
    assert sorted(ring) == list(range(count))
    name = {node: at for at, node in enumerate(ring)}
    return [[(name[one], name[other]) for one, other in sorted(partner.items())] for partner in pairings]


def paired(value, axis, second, wrapped=True):
    count = lax.axis_size(axis)
    if not second:
        return lax.ppermute(value, axis, [(i, i ^ 1) for i in range(count)])
    pairs = [(i, (i + (1 if i % 2 else -1)) % count) for i in range(count)]
    if not wrapped:
        pairs = [(i, j) if abs(i - j) == 1 else (i, i) for i, j in pairs]
    return lax.ppermute(value, axis, pairs)


def to_all(value):
    return lax.all_to_all(value, ("gx", "gy"), split_axis=0, concat_axis=0, tiled=True)


def shards(fields, eps_background, target, widths, intersection, pillar_tile, anchors):
    span_x = lax.axis_size("gx")
    span_y = lax.axis_size("gy")
    devices = span_x * span_y
    first, second, back_y, back_x = tables(span_x, span_y)
    window_table, fill_table, monitor_table, column_table, source_table = choosers()
    intersection, tile, anchors = intersection.T, pillar_tile.T, anchors.T

    strip = shape_of(ARRAYS, HALO, TILE, 128)
    dma = pltpu.SemaphoreType.DMA
    rim_rows = RIM_ROWS + FEATURES
    packed, pay_a, pay_b, features, strip_a, strip_b = call(
        lambda *refs: pack_kernel(span_y, *refs),
        (
            shape_of(ARRAYS, RUN, TILE, 128),
            shape_of(rim_rows, 128),
            shape_of(rim_rows, 128),
            shape_of(FEATURES, P_DEV),
            strip,
            strip,
        ),
        (fields, eps_background, intersection, widths[None], tile, anchors),
        scratch=(
            pltpu.VMEM((ARRAYS, TILE, TILE, 128), F32),
            pltpu.VMEM((16, P_DEV), F32),
            pltpu.VMEM((1, P_DEV), F32),
            pltpu.VMEM((1, P_DEV), jnp.int32),
            pltpu.VMEM((2, P_DEV), jnp.int32),
            dma((ARRAYS + 4,)),
            dma((2 * ARRAYS,)),
        ),
        micros=3.0,
        room=60,
        anywhere=tuple(range(6)),
        out_anywhere=(4, 5),
    )
    pairings = matchings(span_x)
    from_a = lax.ppermute(pay_a, "gx", pairings[0])
    from_b = lax.ppermute(pay_b, "gx", pairings[1])
    others = [lax.ppermute(features, "gx", pairs) for pairs in pairings[2:]]
    known = span_x * P_DEV
    sides = shape_of(SIDE_ROWS, 128)
    wide, pay_a, pay_b = call(
        lambda *refs: widen_kernel(span_x, *refs),
        (shape_of(ARRAYS, RUN, TILE, 128), sides, sides),
        (packed, from_a, from_b),
    )
    from_a, pay_a = lax.optimization_barrier((from_a, pay_a))
    windows = call(
        lambda *refs: windows_kernel(span_x, span_y, *refs),
        shape_of(span_y, FOLD, 128),
        (features, from_a, from_b, *others, jnp.asarray(window_table)),
        scratch=(pltpu.VMEM((REACH, known), BF16), pltpu.VMEM((8 * EXT * span_y, known), BF16)),
        micros=3.0,
    )
    strip_a, strip_b, windows = lax.optimization_barrier((strip_a, strip_b, windows))
    windows = lax.all_to_all(windows, "gy", split_axis=0, concat_axis=0, tiled=True)
    from_a = paired(pay_a, "gy", False)
    from_b = paired(pay_b, "gy", True)
    ext = (RUN, EXT, 128)
    monitor, changes, inverse = call(
        lambda *refs: forward_kernel(span_x, span_y, *refs),
        (shape_of(devices, TILE, 128), shape_of(NT, 3, RUN, TILE, 128), shape_of(*ext)),
        (wide, windows, from_a, from_b, jnp.asarray(fill_table), jnp.asarray(monitor_table)),
        scratch=(
            pltpu.VMEM(ext, F32),
            pltpu.VMEM((3, *ext), F32),
            pltpu.VMEM((3, *ext), F32),
            pltpu.VMEM((4, RUN, TILE, 128), F32),
        ),
        micros=5.0,
    )

    rim_a = paired(strip_a, "gx", False)
    rim_b = paired(strip_b, "gx", True, wrapped=False)
    monitor, rim_a, rim_b = lax.optimization_barrier((monitor, rim_a, rim_b))
    gathered = to_all(monitor)
    pairs = shape_of(ARRAYS, EXT // 2, 8, 128)
    edge = pltpu.VMEM((ARRAYS, TILE, 8, 128), F32)
    pay_a, pay_b = call(
        lambda *refs: strips_kernel(span_x, *refs),
        (pairs, pairs),
        (fields, eps_background, rim_a, rim_b),
        scratch=(edge, edge, dma((2 * ARRAYS,))),
        micros=2.0,
        anywhere=(0, 1),
    )
    side_a = paired(pay_a, "gy", False)
    side_b = paired(pay_b, "gy", True, wrapped=False)
    final_fields = call(
        lambda *refs: full_kernel(span_x, span_y, *refs),
        shape_of(6, TILE, TILE, 128),
        (fields, eps_background, rim_a, rim_b, inverse, side_a, side_b),
        scratch=(
            pltpu.VMEM((6, EXT, EXT, 128), F32),
            pltpu.VMEM((6, EXT, EXT, 128), F32),
            pltpu.VMEM((EXT, EXT, 128), F32),
            pltpu.VMEM((EXT, EXT, 128), F32),
            pltpu.VMEM((6, TILE, TILE, 128), F32),
            dma((3 * ARRAYS,)),
            dma((12,)),
        ),
        micros=10.0,
        anywhere=(0, 1, 2, 3),
        out_anywhere=(0,),
    )

    focal_power, column = call(
        lambda *refs: focal_kernel(span_x, span_y, *refs),
        (shape_of(U // devices, V), shape_of(devices, 8, 128)),
        (
            gathered,
            jnp.asarray(first),
            jnp.asarray(second),
            jnp.asarray(back_y),
            jnp.asarray(back_x),
            jnp.asarray(column_table),
            jnp.asarray(source_table),
            target,
            changes,
            inverse,
        ),
        scratch=(
            pltpu.VMEM((devices, TILE, 128), F32),
            pltpu.VMEM(first.shape, BF16),
            pltpu.VMEM(second.shape, BF16),
            pltpu.VMEM((U, V), F32),
            pltpu.VMEM(back_y.shape[1:], BF16),
            pltpu.VMEM(back_x.shape[1:], BF16),
            pltpu.VMEM(source_table.shape, BF16),
            pltpu.VMEM(ext, F32),
            pltpu.VMEM((NT, 3, RUN, TILE, 128), F32),
            pltpu.VMEM(column_table.shape, BF16),
            pltpu.VMEM((U, V), F32),
            pltpu.VMEM((3, *ext), F32),
            pltpu.VMEM((3, *ext), F32),
            pltpu.VMEM(ext, F32),
            pltpu.VMEM((4, *ext), F32),
            pltpu.VMEM((RUN, TILE, 128), F32),
            dma((10,)),
        ),
        micros=6.0,
        anywhere=tuple(range(10)),
    )
    received = to_all(column)
    grad_widths = call(
        widths_kernel,
        shape_of(1, P_DEV),
        (received.reshape(devices * 8, 128), intersection, tile, anchors),
    )
    return (final_fields, focal_power, grad_widths.reshape(P_DEV))


def solution(mesh):
    placed = (
        P(None, "gx", "gy", None),
        P("gx", "gy", None),
        P(),
        P(("gx", "gy")),
        P(("gx", "gy"), None),
        P(("gx", "gy"), None),
        P(("gx", "gy"), None),
    )
    return jax.shard_map(
        shards,
        mesh=mesh,
        in_specs=placed,
        out_specs=(P(None, "gx", "gy", None), P(("gx", "gy"), None), P(("gx", "gy"))),
        check_vma=False,
    )
```

time: 134 us -> 76.7 us (0.57)
  starting transfers between devices: 44.8 us -> 28.3 us
  local copies, waits for them, and re-layouts: 17.4 us -> 1.82 us
  Pallas kernels: 44 us -> 30.4 us
  waiting for transfers between devices: 20.2 us -> 14.4 us
  other arithmetic: 5.39 us -> 0 us
    ppermute x24 -> x9, starting transfers between devices: 41.2 us -> 17.3 us  [the longest x3 10.1 us: paired(): return lax.ppermute(value, axis, pairs)]
    pallas_call x6 -> x8, Pallas kernels: 44 us -> 30.4 us  [call(): pl.pallas_call(kernel, out_shape=out_shape, in_specs=[hbm if at in anywhe...]
    unnamed x44 -> x26, local copies, waits for them, and re-layouts: 14.5 us -> 1.82 us
    all_to_all x1 -> x3, starting transfers between devices: 3.6 us -> 11 us  [the longest x2 7.3 us: to_all(): lax.all_to_all(value, ('gx', 'gy'), split_axis=0, concat_axis=0, tiled=True)]
    ppermute x24 -> x9, waiting for transfers between devices: 14.2 us -> 7.73 us  [the longest x1 4.3 us: shards(): from_b = lax.ppermute(pay_b, 'gx', pairings[1])]
    concatenate x5 -> x0, other arithmetic: 3.84 us -> none  [the longest x2 3.7 us: y_strip(): jnp.concatenate([own, rim_east[:, :, rows], rim_west[:, :, rows]], axis=1)]
    squeeze x2 -> x0, local copies, waits for them, and re-layouts: 1.88 us -> none  [the longest x1 0.97 us: shards(): lax.dynamic_index_in_dim(jnp.asarray(back_y), place_y, 0, keepdims=False)]
    all_to_all x1 -> x3, waiting for transfers between devices: 5.95 us -> 6.7 us  [the longest x2 6.7 us: to_all(): lax.all_to_all(value, ('gx', 'gy'), split_axis=0, concat_axis=0, tiled=True)]
  transfers between devices with their start and end apart: 25 -> 12, of which waited for: 10 -> 3; matrix products, arithmetic and copies ran while one was open for 7% -> 0% of each run, Pallas kernels for 9% -> 29%
where the time goes in v2:
time: 76.7 us; the launch traced here: 75.8 us
  Pallas kernels  30.4 us (40%)
  starting transfers between devices  28.3 us (37%)
  waiting for transfers between devices  14.4 us (19%)
  local copies, waits for them, and re-layouts  1.82 us (2%)
  between operations  0.88 us (1%)
    pallas_call x8, Pallas kernels, call(): pl.pallas_call(kernel, out_shape=out_shape, in_specs=[hbm if at in anywhe...  30.4 us
    ppermute x3, starting transfers between devices, paired(): return lax.ppermute(value, axis, pairs)  10.1 us
    all_to_all x2, starting transfers between devices, to_all(): lax.all_to_all(value, ('gx', 'gy'), split_axis=0, concat_axis=0, tiled=True)  7.3 us
    all_to_all x2, waiting for transfers between devices, to_all(): lax.all_to_all(value, ('gx', 'gy'), split_axis=0, concat_axis=0, tiled=True)  6.7 us
    ppermute x1, waiting for transfers between devices, shards(): from_b = lax.ppermute(pay_b, 'gx', pairings[1])  4.3 us
    all_to_all x1, starting transfers between devices, shards(): lax.all_to_all(windows, 'gy', split_axis=0, concat_axis=0, tiled=True)  3.72 us
    ppermute x3, waiting for transfers between devices, paired(): return lax.ppermute(value, axis, pairs)  3.42 us
    ppermute x1, starting transfers between devices, shards(): from_a = lax.ppermute(pay_a, 'gx', pairings[0])  3.09 us
  transfers between devices with their start and end apart: 12, of which 3 were waited for; matrix products, arithmetic and copies ran while one was open for 0% of the time, Pallas kernels for 29%

profile of v2, /device:TPU:0, one launch (start us, length us, event | category | flops | bytes accessed | tf_op | source)
XLA Modules:
  0.0 75.8 jit_solution(1206680813687717235)
XLA Ops:
  0.7 4.5 %shard_map.175 = (f32[7,5,32,128]{3,2,1,0:T(8,128)}, f32[152,128]{1,0:T(8,128)}, f32[152,128]{1,0:T(8,128)}, f32[24,128]{1,0:T(8,128)}, f32[7,4,32,128]{3,2,1,0:T(8,128)}, /*index=5*/f32[7,4,32,128]{3,2,1,0:T(8,128)}) custom-call(f32[6,32,32,128]{3,2,1,0:T(8,128)} %refs_0_.5, f32[32,32,128]{2,1,0:T(8,128)} %refs_1_.6, f32[16,128]{1,0:T(8,128)} %bitcast.7, ...), custom_call_target="tpu_custom_call" | custom-call | flops 1000000 | bytes 9000000 | tf_op jit(solution)/shard_map/pallas_call | solution.py:699
  5.2 3.1 %collective-permute-start = (f32[152,128]{1,0:T(8,128)}, f32[152,128]{1,0:T(8,128)S(1)}, u32[]{:S(2)}, u32[]{:S(2)}) collective-permute-start(f32[152,128]{1,0:T(8,128)} %get-tuple-element.28), channel_id=1, source_target_pairs={{0,8},{16,24},{24,16},{8,0},{1,9},{17,25},{25,17},{9,1},{2,10},{18... | collective-permute-start | bytes 233480 | tf_op jit(solution)/shard_map/ppermute | solution.py:782
  8.3 2.5 %collective-permute-start.1 = (f32[152,128]{1,0:T(8,128)}, f32[152,128]{1,0:T(8,128)S(1)}, u32[]{:S(2)}, u32[]{:S(2)}) collective-permute-start(f32[152,128]{1,0:T(8,128)} %get-tuple-element.29), channel_id=1, source_target_pairs={{0,24},{16,8},{24,0},{8,16},{1,25},{17,9},{25,1},{9,17},{2,26},{18... | collective-permute-start | bytes 233480 | tf_op jit(solution)/shard_map/ppermute | solution.py:783
  10.8 4.3 %collective-permute-done.1.refs_2_ = f32[152,128]{1,0:T(8,128)S(1)} collective-permute-done((f32[152,128]{1,0:T(8,128)}, f32[152,128]{1,0:T(8,128)S(1)}, u32[]{:S(2)}, u32[]{:S(2)}) %collective-permute-start.1) | collective-permute-done | bytes 77856 | tf_op jit(solution)/shard_map/ppermute | solution.py:783
  15.2 1.1 %copy-done.1 = f32[7,5,32,128]{3,2,1,0:T(8,128)S(1)} copy-done((f32[7,5,32,128]{3,2,1,0:T(8,128)S(1)}, f32[7,5,32,128]{3,2,1,0:T(8,128)}, u32[]{:S(2)}) %copy-start.1) | copy-done | bytes 573464
  16.2 0.3 shard_map.176
  16.5 0.7 copy-done.10
  17.2 2.9 %shard_map.177 = f32[8,24,128]{2,1,0:T(8,128)} custom-call(f32[24,128]{1,0:T(8,128)S(1)} %copy-done.10, f32[152,128]{1,0:T(8,128)S(1)} %collective-permute-done.refs_1_, f32[152,128]{1,0:T(8,128)S(1)} %collective-permute-done.1.refs_2_, f32[24,128]{1,0:T(8,128)S(1)} %collective-permute-done.2.refs_3_, bf16[4,48,128]{2,1,0:T(8,128)(2,1)S(1)} %copy-done.8), custom_call_target="tpu_custom_call" | custom-call | flops 1000000 | bytes 9000000 | tf_op jit(solution)/shard_map/pallas_call | solution.py:699
  20.1 0.7 collective-permute-start.5
  20.7 1.7 %collective-permute-start.6 = (f32[7,4,32,128]{3,2,1,0:T(8,128)}, f32[7,4,32,128]{3,2,1,0:T(8,128)S(1)}, u32[]{:S(2)}, u32[]{:S(2)}) collective-permute-start(f32[7,4,32,128]{3,2,1,0:T(8,128)} %get-tuple-element.41), channel_id=1, source_target_pairs={{0,0},{8,16},{16,8},{24,24},{1,1},{9,17},{17,9},{25,25},{2,2},{10,... | collective-permute-start | bytes 1376264 | tf_op jit(solution)/shard_map/ppermute | solution.py:738
  22.4 3.7 %all-to-all-start = ((f32[8,24,128]{2,1,0:T(8,128)}), f32[8,24,128]{2,1,0:T(8,128)S(1)}, u32[]{:S(2)}, u32[]{:S(2)}) async-start(f32[8,24,128]{2,1,0:T(8,128)} %shard_map.177), calls=%async_computation | async-start | bytes 196608 | tf_op jit(solution)/shard_map/all_to_all | solution.py:801
  26.1 0.5 collective-permute-start.3
  26.6 2.5 %collective-permute-start.4 = (f32[160,128]{1,0:T(8,128)S(1)}, f32[160,128]{1,0:T(8,128)S(1)}, u32[]{:S(2)}, u32[]{:S(2)}) collective-permute-start(f32[160,128]{1,0:T(8,128)S(1)} %get-tuple-element.38), channel_id=1, source_target_pairs={{0,7},{1,2},{2,1},{3,4},{4,3},{5,6},{6,5},{7,0},{8,15},{9,10},{10,... | collective-permute-start | bytes 245768 | tf_op jit(solution)/shard_map/ppermute | solution.py:738
  29.1 3.4 %collective-permute-done.4.refs_3_ = f32[160,128]{1,0:T(8,128)S(1)} collective-permute-done((f32[160,128]{1,0:T(8,128)S(1)}, f32[160,128]{1,0:T(8,128)S(1)}, u32[]{:S(2)}, u32[]{:S(2)}) %collective-permute-start.4) | collective-permute-done | bytes 81952 | tf_op jit(solution)/shard_map/ppermute | solution.py:738
  32.6 2.1 %shard_map.178 = (f32[32,32,128]{2,1,0:T(8,128)}, f32[4,3,5,32,128]{4,3,2,1,0:T(8,128)}, f32[5,40,128]{2,1,0:T(8,128)S(1)}) custom-call(f32[7,5,32,128]{3,2,1,0:T(8,128)S(1)} %get-tuple-element.30.refs_0_, f32[8,24,128]{2,1,0:T(8,128)S(1)} %all-to-all-done.refs_1_, f32[160,128]{1,0:T(8,128)S(1)} %collective-permute-done.3.refs_2_, ...), custom_call_target="tpu_custom_call" | custom-call | flops 1000000 | bytes 15000000 | tf_op jit(solution)/shard_map/pallas_call | solution.py:699
  34.7 4.2 %all-to-all-start.1 = ((f32[32,32,128]{2,1,0:T(8,128)}), f32[32,32,128]{2,1,0:T(8,128)S(1)}, u32[]{:S(2)}, u32[]{:S(2)}) async-start(f32[32,32,128]{2,1,0:T(8,128)} %get-tuple-element.47), calls=%async_computation.1 | async-start | bytes 1048576 | tf_op jit(solution)/shard_map/all_to_all | solution.py:742
  39.0 2.6 %shard_map.179 = (f32[7,20,8,128]{3,2,1,0:T(8,128)}, f32[7,20,8,128]{3,2,1,0:T(8,128)}) custom-call(f32[6,32,32,128]{3,2,1,0:T(8,128)} %refs_0_.5, f32[32,32,128]{2,1,0:T(8,128)S(1)} %copy-done, f32[7,4,32,128]{3,2,1,0:T(8,128)S(1)} %collective-permute-done.5.refs_2_, f32[7,4,32,128]{3,2,1,0:T(8,128)S(1)} %collective-permute-done.6.refs_3_), custom_call_target="tpu_custom_call" | custom-call | flops 1000000 | bytes 6000000 | tf_op jit(solution)/shard_map/pallas_call | solution.py:699
  41.6 0.3 collective-permute-start.7
  41.9 5.9 %collective-permute-start.8 = (f32[7,20,8,128]{3,2,1,0:T(8,128)}, f32[7,20,8,128]{3,2,1,0:T(8,128)}, u32[]{:S(2)}, u32[]{:S(2)}) collective-permute-start(f32[7,20,8,128]{3,2,1,0:T(8,128)} %get-tuple-element.46), channel_id=1, source_target_pairs={{0,0},{1,2},{2,1},{3,4},{4,3},{5,6},{6,5},{7,7},{8,8},{9,10},{10,9... | collective-permute-start | bytes 1720328 | tf_op jit(solution)/shard_map/ppermute | solution.py:738
  47.8 6.7 %all-to-all-done.1.refs_0_ = f32[32,32,128]{2,1,0:T(8,128)S(1)} async-done(((f32[32,32,128]{2,1,0:T(8,128)}), f32[32,32,128]{2,1,0:T(8,128)S(1)}, u32[]{:S(2)}, u32[]{:S(2)}) %all-to-all-start.1) | async-done | bytes 524320 | tf_op jit(solution)/shard_map/all_to_all | solution.py:742
  54.6 6.4 %shard_map.181 = (f32[8,256]{1,0:T(8,128)}, f32[32,8,128]{2,1,0:T(8,128)}) custom-call(f32[32,32,128]{2,1,0:T(8,128)S(1)} %all-to-all-done.1.refs_0_, bf16[2,512,256]{2,1,0:T(8,128)(2,1)S(1)} %copy-done.2, bf16[2,512,512]{2,1,0:T(8,128)(2,1)} %constant.22.clone.refs_2_, bf16[8,2,128,512]{3,2,1,0:T(8,128)(2,1)} %constant.23.clone.refs_3_, ...), custom_call_target="tpu_custom_call" | custom-call | flops 1000000 | bytes 18000000 | tf_op jit(solution)/shard_map/pallas_call | solution.py:699
  61.0 3.1 %all-to-all-start.2 = ((f32[32,8,128]{2,1,0:T(8,128)}), f32[32,8,128]{2,1,0:T(8,128)S(1)}, u32[]{:S(2)}, u32[]{:S(2)}) async-start(f32[32,8,128]{2,1,0:T(8,128)} %get-tuple-element.50), calls=%async_computation.2 | async-start | bytes 262144 | tf_op jit(solution)/shard_map/all_to_all | solution.py:742
  64.1 10.8 %shard_map.180 = f32[6,32,32,128]{3,2,1,0:T(8,128)} custom-call(f32[6,32,32,128]{3,2,1,0:T(8,128)} %refs_0_.5, f32[32,32,128]{2,1,0:T(8,128)S(1)} %copy-done, f32[7,4,32,128]{3,2,1,0:T(8,128)S(1)} %collective-permute-done.5.refs_2_, f32[7,4,32,128]{3,2,1,0:T(8,128)S(1)} %collective-permute-done.6.refs_3_, ...), custom_call_target="tpu_custom_call" | custom-call | flops 1000000 | bytes 30000000 | tf_op jit(solution)/shard_map/pallas_call | solution.py:699
  74.9 0.9 %shard_map.182 = f32[1,128]{1,0:T(1,128)} custom-call(f32[256,128]{1,0:T(8,128)S(1)} %bitcast.6, f32[16,128]{1,0:T(8,128)S(1)} %bitcast.8, s32[1,128]{1,0:T(1,128)S(1)} %bitcast.12, s32[2,128]{1,0:T(2,128)S(1)} %bitcast.10), custom_call_target="tpu_custom_call" | custom-call | flops 1000000 | bytes 3000000 | tf_op jit(solution)/shard_map/pallas_call | solution.py:699
  (34 shorter events, 0.2 us)
Async XLA Ops:
  0.6 15.9 %copy-start.8 = (bf16[4,48,128]{2,1,0:T(8,128)(2,1)S(1)}, bf16[4,48,128]{2,1,0:T(8,128)(2,1)}, u32[]{:S(2)}) copy-start(bf16[4,48,128]{2,1,0:T(8,128)(2,1)} %constant.18.clone.refs_4_) | copy-start | bytes 147460
  0.6 31.9 %copy-start.6 = (bf16[640,128]{1,0:T(8,128)(2,1)S(1)}, bf16[640,128]{1,0:T(8,128)(2,1)}, u32[]{:S(2)}) copy-start(bf16[640,128]{1,0:T(8,128)(2,1)} %constant.20.clone.refs_5_) | copy-start | bytes 491524
  0.7 31.9 %copy-start.7 = (bf16[128,640]{1,0:T(8,128)(2,1)S(1)}, bf16[128,640]{1,0:T(8,128)(2,1)}, u32[]{:S(2)}) copy-start(bf16[128,640]{1,0:T(8,128)(2,1)} %constant.19.clone.refs_4_) | copy-start | bytes 491524
  0.7 38.3 %copy-start = (f32[32,32,128]{2,1,0:T(8,128)S(1)}, f32[32,32,128]{2,1,0:T(8,128)}, u32[]{:S(2)}) copy-start(f32[32,32,128]{2,1,0:T(8,128)} %refs_1_.6) | copy-start | bytes 1572868
  5.2 5.7 %collective-permute-start = (f32[152,128]{1,0:T(8,128)}, f32[152,128]{1,0:T(8,128)S(1)}, u32[]{:S(2)}, u32[]{:S(2)}) collective-permute-start(f32[152,128]{1,0:T(8,128)} %get-tuple-element.28), channel_id=1, source_target_pairs={{0,8},{16,24},{24,16},{8,0},{1,9},{17,25},{25,17},{9,1},{2,10},{18... | collective-permute-start | bytes 233480 | tf_op jit(solution)/shard_map/ppermute | solution.py:782
  8.3 6.9 %collective-permute-start.1 = (f32[152,128]{1,0:T(8,128)}, f32[152,128]{1,0:T(8,128)S(1)}, u32[]{:S(2)}, u32[]{:S(2)}) collective-permute-start(f32[152,128]{1,0:T(8,128)} %get-tuple-element.29), channel_id=1, source_target_pairs={{0,24},{16,8},{24,0},{8,16},{1,25},{17,9},{25,1},{9,17},{2,26},{18... | collective-permute-start | bytes 233480 | tf_op jit(solution)/shard_map/ppermute | solution.py:783
  10.7 5.7 %collective-permute-start.2 = (f32[24,128]{1,0:T(8,128)}, f32[24,128]{1,0:T(8,128)S(1)}, u32[]{:S(2)}, u32[]{:S(2)}) collective-permute-start(f32[24,128]{1,0:T(8,128)} %get-tuple-element.33.refs_0_), channel_id=1, source_target_pairs={{0,16},{16,0},{24,8},{8,24},{1,17},{17,1},{25,9},{9,25},{2,18},{18... | collective-permute-start | bytes 36872 | tf_op jit(solution)/shard_map/ppermute | solution.py:784
  15.1 1.1 %copy-start.1 = (f32[7,5,32,128]{3,2,1,0:T(8,128)S(1)}, f32[7,5,32,128]{3,2,1,0:T(8,128)}, u32[]{:S(2)}) copy-start(f32[7,5,32,128]{3,2,1,0:T(8,128)} %get-tuple-element.27.refs_0_) | copy-start | bytes 1720324
  20.1 14.6 %collective-permute-start.5 = (f32[7,4,32,128]{3,2,1,0:T(8,128)}, f32[7,4,32,128]{3,2,1,0:T(8,128)S(1)}, u32[]{:S(2)}, u32[]{:S(2)}) collective-permute-start(f32[7,4,32,128]{3,2,1,0:T(8,128)} %get-tuple-element.40), channel_id=1, source_target_pairs={{0,8},{8,0},{16,24},{24,16},{1,9},{9,1},{17,25},{25,17},{2,10},{10... | collective-permute-start | bytes 1376264 | tf_op jit(solution)/shard_map/ppermute | solution.py:734
  20.7 14.0 %collective-permute-start.6 = (f32[7,4,32,128]{3,2,1,0:T(8,128)}, f32[7,4,32,128]{3,2,1,0:T(8,128)S(1)}, u32[]{:S(2)}, u32[]{:S(2)}) collective-permute-start(f32[7,4,32,128]{3,2,1,0:T(8,128)} %get-tuple-element.41), channel_id=1, source_target_pairs={{0,0},{8,16},{16,8},{24,24},{1,1},{9,17},{17,9},{25,25},{2,2},{10,... | collective-permute-start | bytes 1376264 | tf_op jit(solution)/shard_map/ppermute | solution.py:738
  22.4 10.2 %all-to-all-start = ((f32[8,24,128]{2,1,0:T(8,128)}), f32[8,24,128]{2,1,0:T(8,128)S(1)}, u32[]{:S(2)}, u32[]{:S(2)}) async-start(f32[8,24,128]{2,1,0:T(8,128)} %shard_map.177), calls=%async_computation | async-start | bytes 196608 | tf_op jit(solution)/shard_map/all_to_all | solution.py:801
  26.1 3.0 %collective-permute-start.3 = (f32[160,128]{1,0:T(8,128)S(1)}, f32[160,128]{1,0:T(8,128)S(1)}, u32[]{:S(2)}, u32[]{:S(2)}) collective-permute-start(f32[160,128]{1,0:T(8,128)S(1)} %get-tuple-element.37), channel_id=1, source_target_pairs={{0,1},{1,0},{2,3},{3,2},{4,5},{5,4},{6,7},{7,6},{8,9},{9,8},{10,11... | collective-permute-start | bytes 245768 | tf_op jit(solution)/shard_map/ppermute | solution.py:734
  26.6 6.0 %collective-permute-start.4 = (f32[160,128]{1,0:T(8,128)S(1)}, f32[160,128]{1,0:T(8,128)S(1)}, u32[]{:S(2)}, u32[]{:S(2)}) collective-permute-start(f32[160,128]{1,0:T(8,128)S(1)} %get-tuple-element.38), channel_id=1, source_target_pairs={{0,7},{1,2},{2,1},{3,4},{4,3},{5,6},{6,5},{7,0},{8,15},{9,10},{10,... | collective-permute-start | bytes 245768 | tf_op jit(solution)/shard_map/ppermute | solution.py:738
  32.6 22.0 %copy-start.2 = (bf16[2,512,256]{2,1,0:T(8,128)(2,1)S(1)}, bf16[2,512,256]{2,1,0:T(8,128)(2,1)}, u32[]{:S(2)}) copy-start(bf16[2,512,256]{2,1,0:T(8,128)(2,1)} %constant.21.clone.refs_1_) | copy-start | bytes 1572868
  32.6 22.0 %copy-start.3 = (f32[256,256]{1,0:T(8,128)S(1)}, f32[256,256]{1,0:T(8,128)}, u32[]{:S(2)}) copy-start(f32[256,256]{1,0:T(8,128)} %refs_7_.1) | copy-start | bytes 786436
  34.7 19.8 %copy-start.4 = (bf16[128,640]{1,0:T(8,128)(2,1)S(1)}, bf16[128,640]{1,0:T(8,128)(2,1)}, u32[]{:S(2)}) copy-start(bf16[128,640]{1,0:T(8,128)(2,1)} %constant.26.clone.refs_6_) | copy-start | bytes 491524
  34.7 19.8 %copy-start.5 = (bf16[640,128]{1,0:T(8,128)(2,1)S(1)}, bf16[640,128]{1,0:T(8,128)(2,1)}, u32[]{:S(2)}) copy-start(bf16[640,128]{1,0:T(8,128)(2,1)} %constant.25.clone.refs_5_) | copy-start | bytes 491524
  34.7 19.8 %all-to-all-start.1 = ((f32[32,32,128]{2,1,0:T(8,128)}), f32[32,32,128]{2,1,0:T(8,128)S(1)}, u32[]{:S(2)}, u32[]{:S(2)}) async-start(f32[32,32,128]{2,1,0:T(8,128)} %get-tuple-element.47), calls=%async_computation.1 | async-start | bytes 1048576 | tf_op jit(solution)/shard_map/all_to_all | solution.py:742
  41.6 22.5 %collective-permute-start.7 = (f32[7,20,8,128]{3,2,1,0:T(8,128)}, f32[7,20,8,128]{3,2,1,0:T(8,128)}, u32[]{:S(2)}, u32[]{:S(2)}) collective-permute-start(f32[7,20,8,128]{3,2,1,0:T(8,128)} %get-tuple-element.45), channel_id=1, source_target_pairs={{0,1},{1,0},{2,3},{3,2},{4,5},{5,4},{6,7},{7,6},{8,9},{9,8},{10,11... | collective-permute-start | bytes 1720328 | tf_op jit(solution)/shard_map/ppermute | solution.py:734
  41.9 22.1 %collective-permute-start.8 = (f32[7,20,8,128]{3,2,1,0:T(8,128)}, f32[7,20,8,128]{3,2,1,0:T(8,128)}, u32[]{:S(2)}, u32[]{:S(2)}) collective-permute-start(f32[7,20,8,128]{3,2,1,0:T(8,128)} %get-tuple-element.46), channel_id=1, source_target_pairs={{0,0},{1,2},{2,1},{3,4},{4,3},{5,6},{6,5},{7,7},{8,8},{9,10},{10,9... | collective-permute-start | bytes 1720328 | tf_op jit(solution)/shard_map/ppermute | solution.py:738
  61.0 13.9 %all-to-all-start.2 = ((f32[32,8,128]{2,1,0:T(8,128)}), f32[32,8,128]{2,1,0:T(8,128)S(1)}, u32[]{:S(2)}, u32[]{:S(2)}) async-start(f32[32,8,128]{2,1,0:T(8,128)} %get-tuple-element.50), calls=%async_computation.2 | async-start | bytes 262144 | tf_op jit(solution)/shard_map/all_to_all | solution.py:742
  64.0 10.9 %copy-start.9 = (f32[128,16]{0,1:T(8,128)S(1)}, f32[128,16]{0,1:T(8,128)}, u32[]{:S(2)}) copy-start(f32[128,16]{0,1:T(8,128)} %param.20) | copy-start | bytes 24580
  64.0 10.9 %copy-start.11 = (s32[128,2]{0,1:T(2,128)S(1)}, s32[128,2]{0,1:T(2,128)}, u32[]{:S(2)}) copy-start(s32[128,2]{0,1:T(2,128)} %param.22) | copy-start | bytes 3076
  64.1 10.9 %copy-start.12 = (s32[128,1]{0,1:T(1,128)S(1)}, s32[128,1]{0,1:T(1,128)}, u32[]{:S(2)}) copy-start(s32[128,1]{0,1:T(1,128)} %param.21) | copy-start | bytes 1540
  (1 other events, 0.7 us)

commit v3 on v2

--- a/solution.py
+++ b/solution.py
@@ -157,41 +157,55 @@
     return copies
 
 
-def pack_kernel(
+def edges_kernel(
     span_y, fields, eps, intersection, widths, tile, anchors,
-    packed, pay_a, pay_b, features, strip_a, strip_b,
-    held, held_intersection, held_widths, held_tile, held_anchors, arriving, leaving,
+    pay_a, pay_b, features, strip_a, strip_b,
+    held_a, held_b, held_intersection, held_widths, held_tile, held_anchors, arriving, leaving,
 ):
-    pairs = [(eps if at == 6 else fields.at[at], held.at[at]) for at in range(ARRAYS)]
+    even = my_place()[0] % 2 == 0
+    edge_a = jnp.where(even, TILE - HALO, 0)
+    edge_b = jnp.where(even, 0, TILE - HALO)
     small = ((intersection, held_intersection), (widths, held_widths), (tile, held_tile), (anchors, held_anchors))
+    pairs = []
+    for array in range(ARRAYS):
+        own = eps if array == 6 else fields.at[array]
+        for edge, held in ((edge_a, held_a), (edge_b, held_b)):
+            pairs.append((own.at[pl.ds(edge, HALO)], held.at[array]))
     arrivals = start_copies(list(small) + pairs, arriving)
     for arrival in arrivals[:4]:
         arrival.wait()
-    arrivals = arrivals[4:]
-    intersection, widths, tile, anchors = held_intersection, held_widths, held_tile, held_anchors
-    values = intersection[...] * widths[...]
-    place = tile[...]
-    start_x = (lax.div(place, span_y) * TILE + anchors[0:1]).astype(F32)
-    start_y = (lax.rem(place, span_y) * TILE + anchors[1:2]).astype(F32)
+    values = held_intersection[...] * held_widths[...]
+    place = held_tile[...]
+    start_x = (lax.div(place, span_y) * TILE + held_anchors[0:1]).astype(F32)
+    start_y = (lax.rem(place, span_y) * TILE + held_anchors[1:2]).astype(F32)
     row = rows_of((8, P_DEV))
     corner = jnp.where(row == 0, start_x, jnp.where(row == 1, start_y, 0.0))
     for ref, offset in ((features, 0), (pay_a, RIM_ROWS), (pay_b, RIM_ROWS)):
         ref[offset : offset + 16] = values
         ref[offset + 16 : offset + FEATURES] = corner
+    for arrival in arrivals[4:]:
+        arrival.wait()
+    departures = start_copies([(held_a, strip_a), (held_b, strip_b)], leaving)
     group = lanes_of((TILE, 128)) // BAND
-    even = my_place()[0] % 2 == 0
-    edge_a = jnp.where(even, TILE - HALO, 0)
-    edge_b = jnp.where(even, 0, TILE - HALO)
-    departures = []
-    built = {}
+    for pay, held in ((pay_a, held_a), (pay_b, held_b)):
+        for block in range(4):
+            built = jnp.zeros((TILE, 128), F32)
+            for at in range(8):
+                array = 2 * block + at // 4
+                if array < ARRAYS:
+                    moved = pltpu.roll(held[array, at % 4], (BAND * at - BAND_START) % 128, 1)
+                    built = jnp.where(group == at, moved, built)
+            pay[block * TILE : (block + 1) * TILE] = built
+    for copy in departures:
+        copy.wait()
+
+
+def pack_kernel(fields, eps, packed, held, arriving):
+    pairs = [(eps if at == 6 else fields.at[at], held.at[at]) for at in range(ARRAYS)]
+    arrivals = start_copies(pairs, arriving)
+    group = lanes_of((TILE, 128)) // BAND
     for array in range(ARRAYS):
         arrivals[array].wait()
-        for at, (strip, start) in enumerate(((strip_a, edge_a), (strip_b, edge_b))):
-            copy = pltpu.make_async_copy(
-                held.at[array, pl.ds(start, HALO)], strip.at[array], leaving.at[2 * array + at]
-            )
-            copy.start()
-            departures.append(copy)
         kept = [jnp.zeros((TILE, 128), F32) for _ in range(RUN)]
         for x in range(TILE):
             at = x // RUN
@@ -199,19 +213,6 @@
             kept[x % RUN] = jnp.where(group == at, moved, kept[x % RUN])
         for run in range(RUN):
             packed[array, run] = kept[run]
-        for name, pay, start in (("a", pay_a, edge_a), ("b", pay_b, edge_b)):
-            block = built.get(name, jnp.zeros((TILE, 128), F32))
-            for step in range(HALO):
-                at = (array % 2) * 4 + step
-                moved = pltpu.roll(held[array, start + step], (BAND * at - BAND_START) % 128, 1)
-                block = jnp.where(group == at, moved, block)
-            if array % 2 == 1 or array == ARRAYS - 1:
-                pay[array // 2 * TILE : (array // 2 + 1) * TILE] = block
-                built.pop(name, None)
-            else:
-                built[name] = block
-    for copy in departures:
-        copy.wait()
 
 
 def paired_low(even, odd):
@@ -753,30 +754,34 @@
     strip = shape_of(ARRAYS, HALO, TILE, 128)
     dma = pltpu.SemaphoreType.DMA
     rim_rows = RIM_ROWS + FEATURES
-    packed, pay_a, pay_b, features, strip_a, strip_b = call(
-        lambda *refs: pack_kernel(span_y, *refs),
-        (
-            shape_of(ARRAYS, RUN, TILE, 128),
-            shape_of(rim_rows, 128),
-            shape_of(rim_rows, 128),
-            shape_of(FEATURES, P_DEV),
-            strip,
-            strip,
-        ),
+    edges = pltpu.VMEM((ARRAYS, HALO, TILE, 128), F32)
+    pay_a, pay_b, features, strip_a, strip_b = call(
+        lambda *refs: edges_kernel(span_y, *refs),
+        (shape_of(rim_rows, 128), shape_of(rim_rows, 128), shape_of(FEATURES, P_DEV), strip, strip),
         (fields, eps_background, intersection, widths[None], tile, anchors),
         scratch=(
-            pltpu.VMEM((ARRAYS, TILE, TILE, 128), F32),
+            edges,
+            edges,
             pltpu.VMEM((16, P_DEV), F32),
             pltpu.VMEM((1, P_DEV), F32),
             pltpu.VMEM((1, P_DEV), jnp.int32),
             pltpu.VMEM((2, P_DEV), jnp.int32),
-            dma((ARRAYS + 4,)),
-            dma((2 * ARRAYS,)),
+            dma((2 * ARRAYS + 4,)),
+            dma((2,)),
         ),
-        micros=3.0,
+        micros=2.0,
         room=60,
         anywhere=tuple(range(6)),
-        out_anywhere=(4, 5),
+        out_anywhere=(3, 4),
+    )
+    packed = call(
+        pack_kernel,
+        shape_of(ARRAYS, RUN, TILE, 128),
+        (fields, eps_background),
+        scratch=(pltpu.VMEM((ARRAYS, TILE, TILE, 128), F32), dma((ARRAYS,))),
+        micros=4.0,
+        room=52,
+        anywhere=(0, 1),
     )
     pairings = matchings(span_x)
     from_a = lax.ppermute(pay_a, "gx", pairings[0])

time: 76.7 us -> 73.8 us (0.962)
  waiting for transfers between devices: 14.4 us -> 12.2 us
  local copies, waits for them, and re-layouts: 1.82 us -> 0.07 us
  Pallas kernels: 30.4 us -> 31.6 us
    ppermute x1, waiting for transfers between devices: 4.3 us -> 1.76 us  [shards(): from_b = lax.ppermute(pay_b, 'gx', pairings[1])]
    unnamed x26 -> x24, local copies, waits for them, and re-layouts: 1.82 us -> 0.07 us
    pallas_call x8 -> x9, Pallas kernels: 30.4 us -> 31.6 us  [call(): pl.pallas_call(kernel, out_shape=out_shape, in_specs=[hbm if at in anywhe...]
  transfers between devices with their start and end apart: 12 -> 12, of which waited for: 3 -> 4; matrix products, arithmetic and copies ran while one was open for 0% -> 0% of each run, Pallas kernels for 29% -> 34%
where the time goes in v3:
time: 73.8 us; the launch traced here: 72.9 us
  Pallas kernels  31.6 us (43%)
  starting transfers between devices  28.3 us (38%)
  waiting for transfers between devices  12.2 us (17%)
  between operations  0.87 us (1%)
    pallas_call x9, Pallas kernels, call(): pl.pallas_call(kernel, out_shape=out_shape, in_specs=[hbm if at in anywhe...  31.6 us
    ppermute x3, starting transfers between devices, paired(): return lax.ppermute(value, axis, pairs)  10.1 us
    all_to_all x2, starting transfers between devices, to_all(): lax.all_to_all(value, ('gx', 'gy'), split_axis=0, concat_axis=0, tiled=True)  7.4 us
    all_to_all x2, waiting for transfers between devices, to_all(): lax.all_to_all(value, ('gx', 'gy'), split_axis=0, concat_axis=0, tiled=True)  6.71 us
    all_to_all x1, starting transfers between devices, shards(): lax.all_to_all(windows, 'gy', split_axis=0, concat_axis=0, tiled=True)  3.72 us
    ppermute x3, waiting for transfers between devices, paired(): return lax.ppermute(value, axis, pairs)  3.42 us
    ppermute x1, starting transfers between devices, shards(): from_a = lax.ppermute(pay_a, 'gx', pairings[0])  3.09 us
    ppermute x1, starting transfers between devices, shards(): from_b = lax.ppermute(pay_b, 'gx', pairings[1])  2.47 us
  transfers between devices with their start and end apart: 12, of which 4 were waited for; matrix products, arithmetic and copies ran while one was open for 0% of the time, Pallas kernels for 34%

profile of v3, /device:TPU:0, one launch (start us, length us, event | category | flops | bytes accessed | tf_op | source)
XLA Modules:
  0.0 72.9 jit_solution(7369541071162819715)
XLA Ops:
  0.6 3.1 %shard_map.176 = (f32[152,128]{1,0:T(8,128)}, f32[152,128]{1,0:T(8,128)}, f32[24,128]{1,0:T(8,128)}, f32[7,4,32,128]{3,2,1,0:T(8,128)}, f32[7,4,32,128]{3,2,1,0:T(8,128)}) custom-call(f32[6,32,32,128]{3,2,1,0:T(8,128)} %refs_0_.5, f32[32,32,128]{2,1,0:T(8,128)} %refs_1_.6, f32[16,128]{1,0:T(8,128)} %bitcast.7, f32[1,128]{1,0:T(1,128)} %bitcast.13, ...), custom_call_target="tpu_custom_call" | custom-call | flops 1000000 | bytes 6000000 | tf_op jit(solution)/shard_map/pallas_call | solution.py:700
  3.8 3.1 %collective-permute-start = (f32[152,128]{1,0:T(8,128)}, f32[152,128]{1,0:T(8,128)S(1)}, u32[]{:S(2)}, u32[]{:S(2)}) collective-permute-start(f32[152,128]{1,0:T(8,128)} %get-tuple-element.26), channel_id=1, source_target_pairs={{0,8},{16,24},{24,16},{8,0},{1,9},{17,25},{25,17},{9,1},{2,10},{18... | collective-permute-start | bytes 233480 | tf_op jit(solution)/shard_map/ppermute | solution.py:787
  6.9 2.5 %collective-permute-start.1 = (f32[152,128]{1,0:T(8,128)}, f32[152,128]{1,0:T(8,128)S(1)}, u32[]{:S(2)}, u32[]{:S(2)}) collective-permute-start(f32[152,128]{1,0:T(8,128)} %get-tuple-element.27), channel_id=1, source_target_pairs={{0,24},{16,8},{24,0},{8,16},{1,25},{17,9},{25,1},{9,17},{2,26},{18... | collective-permute-start | bytes 233480 | tf_op jit(solution)/shard_map/ppermute | solution.py:788
  9.5 2.5 %shard_map.175.refs_0_ = f32[7,5,32,128]{3,2,1,0:T(8,128)S(1)} custom-call(f32[6,32,32,128]{3,2,1,0:T(8,128)} %refs_0_.5, f32[32,32,128]{2,1,0:T(8,128)S(1)} %copy-done), custom_call_target="tpu_custom_call" | custom-call | flops 1000000 | bytes 12000000 | tf_op jit(solution)/shard_map/pallas_call | solution.py:700
  12.0 1.8 %collective-permute-done.1.refs_2_ = f32[152,128]{1,0:T(8,128)S(1)} collective-permute-done((f32[152,128]{1,0:T(8,128)}, f32[152,128]{1,0:T(8,128)S(1)}, u32[]{:S(2)}, u32[]{:S(2)}) %collective-permute-start.1) | collective-permute-done | bytes 77856 | tf_op jit(solution)/shard_map/ppermute | solution.py:788
  13.8 0.3 shard_map.177
  14.0 0.3 collective-permute-done.2.refs_3_
  14.3 2.9 %shard_map.178 = f32[8,24,128]{2,1,0:T(8,128)} custom-call(f32[24,128]{1,0:T(8,128)S(1)} %copy-done.9, f32[152,128]{1,0:T(8,128)S(1)} %collective-permute-done.refs_1_, f32[152,128]{1,0:T(8,128)S(1)} %collective-permute-done.1.refs_2_, f32[24,128]{1,0:T(8,128)S(1)} %collective-permute-done.2.refs_3_, bf16[4,48,128]{2,1,0:T(8,128)(2,1)S(1)} %copy-done.7), custom_call_target="tpu_custom_call" | custom-call | flops 1000000 | bytes 9000000 | tf_op jit(solution)/shard_map/pallas_call | solution.py:700
  17.2 0.5 collective-permute-start.5
  17.7 1.7 %collective-permute-start.6 = (f32[7,4,32,128]{3,2,1,0:T(8,128)}, f32[7,4,32,128]{3,2,1,0:T(8,128)S(1)}, u32[]{:S(2)}, u32[]{:S(2)}) collective-permute-start(f32[7,4,32,128]{3,2,1,0:T(8,128)} %get-tuple-element.39), channel_id=1, source_target_pairs={{0,0},{8,16},{16,8},{24,24},{1,1},{9,17},{17,9},{25,25},{2,2},{10,... | collective-permute-start | bytes 1376264 | tf_op jit(solution)/shard_map/ppermute | solution.py:739
  19.4 3.7 %all-to-all-start = ((f32[8,24,128]{2,1,0:T(8,128)}), f32[8,24,128]{2,1,0:T(8,128)S(1)}, u32[]{:S(2)}, u32[]{:S(2)}) async-start(f32[8,24,128]{2,1,0:T(8,128)} %shard_map.178), calls=%async_computation | async-start | bytes 196608 | tf_op jit(solution)/shard_map/all_to_all | solution.py:806
  23.1 0.5 collective-permute-start.3
  23.6 2.5 %collective-permute-start.4 = (f32[160,128]{1,0:T(8,128)S(1)}, f32[160,128]{1,0:T(8,128)S(1)}, u32[]{:S(2)}, u32[]{:S(2)}) collective-permute-start(f32[160,128]{1,0:T(8,128)S(1)} %get-tuple-element.36), channel_id=1, source_target_pairs={{0,7},{1,2},{2,1},{3,4},{4,3},{5,6},{6,5},{7,0},{8,15},{9,10},{10,... | collective-permute-start | bytes 245768 | tf_op jit(solution)/shard_map/ppermute | solution.py:739
  26.1 3.4 %collective-permute-done.4.refs_3_ = f32[160,128]{1,0:T(8,128)S(1)} collective-permute-done((f32[160,128]{1,0:T(8,128)S(1)}, f32[160,128]{1,0:T(8,128)S(1)}, u32[]{:S(2)}, u32[]{:S(2)}) %collective-permute-start.4) | collective-permute-done | bytes 81952 | tf_op jit(solution)/shard_map/ppermute | solution.py:739
  29.6 2.1 %shard_map.179 = (f32[32,32,128]{2,1,0:T(8,128)}, f32[4,3,5,32,128]{4,3,2,1,0:T(8,128)}, f32[5,40,128]{2,1,0:T(8,128)S(1)}) custom-call(f32[7,5,32,128]{3,2,1,0:T(8,128)S(1)} %get-tuple-element.28.refs_0_, f32[8,24,128]{2,1,0:T(8,128)S(1)} %all-to-all-done.refs_1_, f32[160,128]{1,0:T(8,128)S(1)} %collective-permute-done.3.refs_2_, ...), custom_call_target="tpu_custom_call" | custom-call | flops 1000000 | bytes 15000000 | tf_op jit(solution)/shard_map/pallas_call | solution.py:700
  31.7 4.3 %all-to-all-start.1 = ((f32[32,32,128]{2,1,0:T(8,128)}), f32[32,32,128]{2,1,0:T(8,128)S(1)}, u32[]{:S(2)}, u32[]{:S(2)}) async-start(f32[32,32,128]{2,1,0:T(8,128)} %get-tuple-element.45), calls=%async_computation.1 | async-start | bytes 1048576 | tf_op jit(solution)/shard_map/all_to_all | solution.py:743
  36.1 2.6 %shard_map.180 = (f32[7,20,8,128]{3,2,1,0:T(8,128)}, f32[7,20,8,128]{3,2,1,0:T(8,128)}) custom-call(f32[6,32,32,128]{3,2,1,0:T(8,128)} %refs_0_.5, f32[32,32,128]{2,1,0:T(8,128)S(1)} %copy-done, f32[7,4,32,128]{3,2,1,0:T(8,128)S(1)} %collective-permute-done.5.refs_2_, f32[7,4,32,128]{3,2,1,0:T(8,128)S(1)} %collective-permute-done.6.refs_3_), custom_call_target="tpu_custom_call" | custom-call | flops 1000000 | bytes 6000000 | tf_op jit(solution)/shard_map/pallas_call | solution.py:700
  38.7 0.3 collective-permute-start.7
  39.0 5.9 %collective-permute-start.8 = (f32[7,20,8,128]{3,2,1,0:T(8,128)}, f32[7,20,8,128]{3,2,1,0:T(8,128)}, u32[]{:S(2)}, u32[]{:S(2)}) collective-permute-start(f32[7,20,8,128]{3,2,1,0:T(8,128)} %get-tuple-element.44), channel_id=1, source_target_pairs={{0,0},{1,2},{2,1},{3,4},{4,3},{5,6},{6,5},{7,7},{8,8},{9,10},{10,9... | collective-permute-start | bytes 1720328 | tf_op jit(solution)/shard_map/ppermute | solution.py:739
  44.9 6.7 %all-to-all-done.1.refs_0_ = f32[32,32,128]{2,1,0:T(8,128)S(1)} async-done(((f32[32,32,128]{2,1,0:T(8,128)}), f32[32,32,128]{2,1,0:T(8,128)S(1)}, u32[]{:S(2)}, u32[]{:S(2)}) %all-to-all-start.1) | async-done | bytes 524320 | tf_op jit(solution)/shard_map/all_to_all | solution.py:743
  51.6 6.4 %shard_map.182 = (f32[8,256]{1,0:T(8,128)}, f32[32,8,128]{2,1,0:T(8,128)}) custom-call(f32[32,32,128]{2,1,0:T(8,128)S(1)} %all-to-all-done.1.refs_0_, bf16[2,512,256]{2,1,0:T(8,128)(2,1)S(1)} %copy-done.1, bf16[2,512,512]{2,1,0:T(8,128)(2,1)} %constant.22.clone.refs_2_, bf16[8,2,128,512]{3,2,1,0:T(8,128)(2,1)} %constant.23.clone.refs_3_, ...), custom_call_target="tpu_custom_call" | custom-call | flops 1000000 | bytes 18000000 | tf_op jit(solution)/shard_map/pallas_call | solution.py:700
  58.1 3.1 %all-to-all-start.2 = ((f32[32,8,128]{2,1,0:T(8,128)}), f32[32,8,128]{2,1,0:T(8,128)S(1)}, u32[]{:S(2)}, u32[]{:S(2)}) async-start(f32[32,8,128]{2,1,0:T(8,128)} %get-tuple-element.48), calls=%async_computation.2 | async-start | bytes 262144 | tf_op jit(solution)/shard_map/all_to_all | solution.py:743
  61.2 10.8 %shard_map.181 = f32[6,32,32,128]{3,2,1,0:T(8,128)} custom-call(f32[6,32,32,128]{3,2,1,0:T(8,128)} %refs_0_.5, f32[32,32,128]{2,1,0:T(8,128)S(1)} %copy-done, f32[7,4,32,128]{3,2,1,0:T(8,128)S(1)} %collective-permute-done.5.refs_2_, f32[7,4,32,128]{3,2,1,0:T(8,128)S(1)} %collective-permute-done.6.refs_3_, ...), custom_call_target="tpu_custom_call" | custom-call | flops 1000000 | bytes 30000000 | tf_op jit(solution)/shard_map/pallas_call | solution.py:700
  72.0 0.9 %shard_map.183 = f32[1,128]{1,0:T(1,128)} custom-call(f32[256,128]{1,0:T(8,128)S(1)} %bitcast.6, f32[16,128]{1,0:T(8,128)S(1)} %bitcast.8, s32[1,128]{1,0:T(1,128)S(1)} %bitcast.12, s32[2,128]{1,0:T(2,128)S(1)} %bitcast.10), custom_call_target="tpu_custom_call" | custom-call | flops 1000000 | bytes 3000000 | tf_op jit(solution)/shard_map/pallas_call | solution.py:700
  (33 shorter events, 0.2 us)
Async XLA Ops:
  0.6 8.8 %copy-start = (f32[32,32,128]{2,1,0:T(8,128)S(1)}, f32[32,32,128]{2,1,0:T(8,128)}, u32[]{:S(2)}) copy-start(f32[32,32,128]{2,1,0:T(8,128)} %refs_1_.6) | copy-start | bytes 1572868
  3.7 10.6 %copy-start.7 = (bf16[4,48,128]{2,1,0:T(8,128)(2,1)S(1)}, bf16[4,48,128]{2,1,0:T(8,128)(2,1)}, u32[]{:S(2)}) copy-start(bf16[4,48,128]{2,1,0:T(8,128)(2,1)} %constant.18.clone.refs_4_) | copy-start | bytes 147460
  3.7 10.5 %copy-start.9 = (f32[24,128]{1,0:T(8,128)S(1)}, f32[24,128]{1,0:T(8,128)}, u32[]{:S(2)}) copy-start(f32[24,128]{1,0:T(8,128)} %get-tuple-element.31.refs_0_) | copy-start | bytes 36868
  3.8 25.8 %copy-start.5 = (bf16[640,128]{1,0:T(8,128)(2,1)S(1)}, bf16[640,128]{1,0:T(8,128)(2,1)}, u32[]{:S(2)}) copy-start(bf16[640,128]{1,0:T(8,128)(2,1)} %constant.20.clone.refs_5_) | copy-start | bytes 491524
  3.8 25.8 %copy-start.6 = (bf16[128,640]{1,0:T(8,128)(2,1)S(1)}, bf16[128,640]{1,0:T(8,128)(2,1)}, u32[]{:S(2)}) copy-start(bf16[128,640]{1,0:T(8,128)(2,1)} %constant.19.clone.refs_4_) | copy-start | bytes 491524
  3.8 8.2 %collective-permute-start = (f32[152,128]{1,0:T(8,128)}, f32[152,128]{1,0:T(8,128)S(1)}, u32[]{:S(2)}, u32[]{:S(2)}) collective-permute-start(f32[152,128]{1,0:T(8,128)} %get-tuple-element.26), channel_id=1, source_target_pairs={{0,8},{16,24},{24,16},{8,0},{1,9},{17,25},{25,17},{9,1},{2,10},{18... | collective-permute-start | bytes 233480 | tf_op jit(solution)/shard_map/ppermute | solution.py:787
  6.9 6.9 %collective-permute-start.1 = (f32[152,128]{1,0:T(8,128)}, f32[152,128]{1,0:T(8,128)S(1)}, u32[]{:S(2)}, u32[]{:S(2)}) collective-permute-start(f32[152,128]{1,0:T(8,128)} %get-tuple-element.27), channel_id=1, source_target_pairs={{0,24},{16,8},{24,0},{8,16},{1,25},{17,9},{25,1},{9,17},{2,26},{18... | collective-permute-start | bytes 233480 | tf_op jit(solution)/shard_map/ppermute | solution.py:788
  9.3 4.9 %collective-permute-start.2 = (f32[24,128]{1,0:T(8,128)}, f32[24,128]{1,0:T(8,128)S(1)}, u32[]{:S(2)}, u32[]{:S(2)}) collective-permute-start(f32[24,128]{1,0:T(8,128)} %get-tuple-element.31.refs_0_), channel_id=1, source_target_pairs={{0,16},{16,0},{24,8},{8,24},{1,17},{17,1},{25,9},{9,25},{2,18},{18... | collective-permute-start | bytes 36872 | tf_op jit(solution)/shard_map/ppermute | solution.py:789
  17.2 14.5 %collective-permute-start.5 = (f32[7,4,32,128]{3,2,1,0:T(8,128)}, f32[7,4,32,128]{3,2,1,0:T(8,128)S(1)}, u32[]{:S(2)}, u32[]{:S(2)}) collective-permute-start(f32[7,4,32,128]{3,2,1,0:T(8,128)} %get-tuple-element.38), channel_id=1, source_target_pairs={{0,8},{8,0},{16,24},{24,16},{1,9},{9,1},{17,25},{25,17},{2,10},{10... | collective-permute-start | bytes 1376264 | tf_op jit(solution)/shard_map/ppermute | solution.py:735
  17.7 14.0 %collective-permute-start.6 = (f32[7,4,32,128]{3,2,1,0:T(8,128)}, f32[7,4,32,128]{3,2,1,0:T(8,128)S(1)}, u32[]{:S(2)}, u32[]{:S(2)}) collective-permute-start(f32[7,4,32,128]{3,2,1,0:T(8,128)} %get-tuple-element.39), channel_id=1, source_target_pairs={{0,0},{8,16},{16,8},{24,24},{1,1},{9,17},{17,9},{25,25},{2,2},{10,... | collective-permute-start | bytes 1376264 | tf_op jit(solution)/shard_map/ppermute | solution.py:739
  19.4 10.2 %all-to-all-start = ((f32[8,24,128]{2,1,0:T(8,128)}), f32[8,24,128]{2,1,0:T(8,128)S(1)}, u32[]{:S(2)}, u32[]{:S(2)}) async-start(f32[8,24,128]{2,1,0:T(8,128)} %shard_map.178), calls=%async_computation | async-start | bytes 196608 | tf_op jit(solution)/shard_map/all_to_all | solution.py:806
  23.1 3.0 %collective-permute-start.3 = (f32[160,128]{1,0:T(8,128)S(1)}, f32[160,128]{1,0:T(8,128)S(1)}, u32[]{:S(2)}, u32[]{:S(2)}) collective-permute-start(f32[160,128]{1,0:T(8,128)S(1)} %get-tuple-element.35), channel_id=1, source_target_pairs={{0,1},{1,0},{2,3},{3,2},{4,5},{5,4},{6,7},{7,6},{8,9},{9,8},{10,11... | collective-permute-start | bytes 245768 | tf_op jit(solution)/shard_map/ppermute | solution.py:735
  23.6 6.0 %collective-permute-start.4 = (f32[160,128]{1,0:T(8,128)S(1)}, f32[160,128]{1,0:T(8,128)S(1)}, u32[]{:S(2)}, u32[]{:S(2)}) collective-permute-start(f32[160,128]{1,0:T(8,128)S(1)} %get-tuple-element.36), channel_id=1, source_target_pairs={{0,7},{1,2},{2,1},{3,4},{4,3},{5,6},{6,5},{7,0},{8,15},{9,10},{10,... | collective-permute-start | bytes 245768 | tf_op jit(solution)/shard_map/ppermute | solution.py:739
  29.6 22.1 %copy-start.1 = (bf16[2,512,256]{2,1,0:T(8,128)(2,1)S(1)}, bf16[2,512,256]{2,1,0:T(8,128)(2,1)}, u32[]{:S(2)}) copy-start(bf16[2,512,256]{2,1,0:T(8,128)(2,1)} %constant.21.clone.refs_1_) | copy-start | bytes 1572868
  29.6 22.1 %copy-start.2 = (f32[256,256]{1,0:T(8,128)S(1)}, f32[256,256]{1,0:T(8,128)}, u32[]{:S(2)}) copy-start(f32[256,256]{1,0:T(8,128)} %refs_7_.1) | copy-start | bytes 786436
  31.7 20.0 %copy-start.3 = (bf16[128,640]{1,0:T(8,128)(2,1)S(1)}, bf16[128,640]{1,0:T(8,128)(2,1)}, u32[]{:S(2)}) copy-start(bf16[128,640]{1,0:T(8,128)(2,1)} %constant.26.clone.refs_6_) | copy-start | bytes 491524
  31.7 20.0 %copy-start.4 = (bf16[640,128]{1,0:T(8,128)(2,1)S(1)}, bf16[640,128]{1,0:T(8,128)(2,1)}, u32[]{:S(2)}) copy-start(bf16[640,128]{1,0:T(8,128)(2,1)} %constant.25.clone.refs_5_) | copy-start | bytes 491524
  31.7 19.9 %all-to-all-start.1 = ((f32[32,32,128]{2,1,0:T(8,128)}), f32[32,32,128]{2,1,0:T(8,128)S(1)}, u32[]{:S(2)}, u32[]{:S(2)}) async-start(f32[32,32,128]{2,1,0:T(8,128)} %get-tuple-element.45), calls=%async_computation.1 | async-start | bytes 1048576 | tf_op jit(solution)/shard_map/all_to_all | solution.py:743
  38.7 22.5 %collective-permute-start.7 = (f32[7,20,8,128]{3,2,1,0:T(8,128)}, f32[7,20,8,128]{3,2,1,0:T(8,128)}, u32[]{:S(2)}, u32[]{:S(2)}) collective-permute-start(f32[7,20,8,128]{3,2,1,0:T(8,128)} %get-tuple-element.43), channel_id=1, source_target_pairs={{0,1},{1,0},{2,3},{3,2},{4,5},{5,4},{6,7},{7,6},{8,9},{9,8},{10,11... | collective-permute-start | bytes 1720328 | tf_op jit(solution)/shard_map/ppermute | solution.py:735
  39.0 22.2 %collective-permute-start.8 = (f32[7,20,8,128]{3,2,1,0:T(8,128)}, f32[7,20,8,128]{3,2,1,0:T(8,128)}, u32[]{:S(2)}, u32[]{:S(2)}) collective-permute-start(f32[7,20,8,128]{3,2,1,0:T(8,128)} %get-tuple-element.44), channel_id=1, source_target_pairs={{0,0},{1,2},{2,1},{3,4},{4,3},{5,6},{6,5},{7,7},{8,8},{9,10},{10,9... | collective-permute-start | bytes 1720328 | tf_op jit(solution)/shard_map/ppermute | solution.py:739
  58.1 13.9 %all-to-all-start.2 = ((f32[32,8,128]{2,1,0:T(8,128)}), f32[32,8,128]{2,1,0:T(8,128)S(1)}, u32[]{:S(2)}, u32[]{:S(2)}) async-start(f32[32,8,128]{2,1,0:T(8,128)} %get-tuple-element.48), calls=%async_computation.2 | async-start | bytes 262144 | tf_op jit(solution)/shard_map/all_to_all | solution.py:743
  61.1 10.9 %copy-start.8 = (f32[128,16]{0,1:T(8,128)S(1)}, f32[128,16]{0,1:T(8,128)}, u32[]{:S(2)}) copy-start(f32[128,16]{0,1:T(8,128)} %param.20) | copy-start | bytes 24580
  61.1 10.9 %copy-start.10 = (s32[128,2]{0,1:T(2,128)S(1)}, s32[128,2]{0,1:T(2,128)}, u32[]{:S(2)}) copy-start(s32[128,2]{0,1:T(2,128)} %param.22) | copy-start | bytes 3076
  61.1 10.9 %copy-start.11 = (s32[128,1]{0,1:T(1,128)S(1)}, s32[128,1]{0,1:T(1,128)}, u32[]{:S(2)}) copy-start(s32[128,1]{0,1:T(1,128)} %param.21) | copy-start | bytes 1540

commit v4 on v3

--- a/solution.py
+++ b/solution.py
@@ -157,14 +157,17 @@
     return copies
 
 
+def edges_to_partners():
+    even = my_place()[0] % 2 == 0
+    return jnp.where(even, TILE - HALO, 0), jnp.where(even, 0, TILE - HALO)
+
+
 def edges_kernel(
     span_y, fields, eps, intersection, widths, tile, anchors,
-    pay_a, pay_b, features, strip_a, strip_b,
-    held_a, held_b, held_intersection, held_widths, held_tile, held_anchors, arriving, leaving,
+    pay_a, pay_b, features,
+    held_a, held_b, held_intersection, held_widths, held_tile, held_anchors, arriving,
 ):
-    even = my_place()[0] % 2 == 0
-    edge_a = jnp.where(even, TILE - HALO, 0)
-    edge_b = jnp.where(even, 0, TILE - HALO)
+    edge_a, edge_b = edges_to_partners()
     small = ((intersection, held_intersection), (widths, held_widths), (tile, held_tile), (anchors, held_anchors))
     pairs = []
     for array in range(ARRAYS):
@@ -185,7 +188,6 @@
         ref[offset + 16 : offset + FEATURES] = corner
     for arrival in arrivals[4:]:
         arrival.wait()
-    departures = start_copies([(held_a, strip_a), (held_b, strip_b)], leaving)
     group = lanes_of((TILE, 128)) // BAND
     for pay, held in ((pay_a, held_a), (pay_b, held_b)):
         for block in range(4):
@@ -196,16 +198,20 @@
                     moved = pltpu.roll(held[array, at % 4], (BAND * at - BAND_START) % 128, 1)
                     built = jnp.where(group == at, moved, built)
             pay[block * TILE : (block + 1) * TILE] = built
-    for copy in departures:
-        copy.wait()
-
-
-def pack_kernel(fields, eps, packed, held, arriving):
+
+
+def pack_kernel(fields, eps, packed, strip_a, strip_b, held, arriving, leaving):
+    edge_a, edge_b = edges_to_partners()
+    departures = []
     pairs = [(eps if at == 6 else fields.at[at], held.at[at]) for at in range(ARRAYS)]
     arrivals = start_copies(pairs, arriving)
     group = lanes_of((TILE, 128)) // BAND
     for array in range(ARRAYS):
         arrivals[array].wait()
+        for at, (strip, edge) in enumerate(((strip_a, edge_a), (strip_b, edge_b))):
+            source = held.at[array, pl.ds(edge, HALO)]
+            departures.append(pltpu.make_async_copy(source, strip.at[array], leaving.at[2 * array + at]))
+            departures[-1].start()
         kept = [jnp.zeros((TILE, 128), F32) for _ in range(RUN)]
         for x in range(TILE):
             at = x // RUN
@@ -213,6 +219,8 @@
             kept[x % RUN] = jnp.where(group == at, moved, kept[x % RUN])
         for run in range(RUN):
             packed[array, run] = kept[run]
+    for copy in departures:
+        copy.wait()
 
 
 def paired_low(even, odd):
@@ -755,9 +763,9 @@
     dma = pltpu.SemaphoreType.DMA
     rim_rows = RIM_ROWS + FEATURES
     edges = pltpu.VMEM((ARRAYS, HALO, TILE, 128), F32)
-    pay_a, pay_b, features, strip_a, strip_b = call(
+    pay_a, pay_b, features = call(
         lambda *refs: edges_kernel(span_y, *refs),
-        (shape_of(rim_rows, 128), shape_of(rim_rows, 128), shape_of(FEATURES, P_DEV), strip, strip),
+        (shape_of(rim_rows, 128), shape_of(rim_rows, 128), shape_of(FEATURES, P_DEV)),
         (fields, eps_background, intersection, widths[None], tile, anchors),
         scratch=(
             edges,
@@ -767,21 +775,20 @@
             pltpu.VMEM((1, P_DEV), jnp.int32),
             pltpu.VMEM((2, P_DEV), jnp.int32),
             dma((2 * ARRAYS + 4,)),
-            dma((2,)),
         ),
         micros=2.0,
         room=60,
         anywhere=tuple(range(6)),
-        out_anywhere=(3, 4),
-    )
-    packed = call(
+    )
+    packed, strip_a, strip_b = call(
         pack_kernel,
-        shape_of(ARRAYS, RUN, TILE, 128),
+        (shape_of(ARRAYS, RUN, TILE, 128), strip, strip),
         (fields, eps_background),
-        scratch=(pltpu.VMEM((ARRAYS, TILE, TILE, 128), F32), dma((ARRAYS,))),
+        scratch=(pltpu.VMEM((ARRAYS, TILE, TILE, 128), F32), dma((ARRAYS,)), dma((2 * ARRAYS,))),
         micros=4.0,
         room=52,
         anywhere=(0, 1),
+        out_anywhere=(1, 2),
     )
     pairings = matchings(span_x)
     from_a = lax.ppermute(pay_a, "gx", pairings[0])

time: 73.8 us -> 73.1 us (level)
  waiting for transfers between devices: 12.2 us -> 11.4 us
  transfers between devices with their start and end apart: 12 -> 12, of which waited for: 4 -> 4; matrix products, arithmetic and copies ran while one was open for 0% -> 0% of each run, Pallas kernels for 34% -> 35%
where the time goes in v4:
time: 73.1 us; the launch traced here: 72.2 us
  Pallas kernels  31.6 us (43%)
  starting transfers between devices  28.3 us (39%)
  waiting for transfers between devices  11.4 us (16%)
  between operations  0.87 us (1%)
    pallas_call x9, Pallas kernels, call(): pl.pallas_call(kernel, out_shape=out_shape, in_specs=[hbm if at in anywhe...  31.6 us
    ppermute x3, starting transfers between devices, paired(): return lax.ppermute(value, axis, pairs)  10.1 us
    all_to_all x2, starting transfers between devices, to_all(): lax.all_to_all(value, ('gx', 'gy'), split_axis=0, concat_axis=0, tiled=True)  7.4 us
    all_to_all x2, waiting for transfers between devices, to_all(): lax.all_to_all(value, ('gx', 'gy'), split_axis=0, concat_axis=0, tiled=True)  6.71 us
    all_to_all x1, starting transfers between devices, shards(): lax.all_to_all(windows, 'gy', split_axis=0, concat_axis=0, tiled=True)  3.72 us
    ppermute x3, waiting for transfers between devices, paired(): return lax.ppermute(value, axis, pairs)  3.42 us
    ppermute x1, starting transfers between devices, shards(): from_a = lax.ppermute(pay_a, 'gx', pairings[0])  3.09 us
    ppermute x1, starting transfers between devices, shards(): from_b = lax.ppermute(pay_b, 'gx', pairings[1])  2.47 us
  transfers between devices with their start and end apart: 12, of which 4 were waited for; matrix products, arithmetic and copies ran while one was open for 0% of the time, Pallas kernels for 35%

profile of v4, /device:TPU:0, one launch (start us, length us, event | category | flops | bytes accessed | tf_op | source)
XLA Modules:
  0.0 72.2 jit_solution(10663241330858787146)
XLA Ops:
  0.7 2.4 %shard_map.176 = (f32[152,128]{1,0:T(8,128)}, f32[152,128]{1,0:T(8,128)}, f32[24,128]{1,0:T(8,128)}) custom-call(f32[6,32,32,128]{3,2,1,0:T(8,128)} %refs_0_.5, f32[32,32,128]{2,1,0:T(8,128)} %refs_1_.6, f32[16,128]{1,0:T(8,128)} %bitcast.7, f32[1,128]{1,0:T(1,128)} %bitcast.13, s32[1,128]{1,0:T(1,128)} %bitcast.11, s32[2,128]{1,0:T(2,128)} %bitcast.9), custom_call_target="tpu_custom_call" | custom-call | flops 1000000 | bytes 6000000 | tf_op jit(solution)/shard_map/pallas_call | solution.py:708
  3.1 3.1 %collective-permute-start = (f32[152,128]{1,0:T(8,128)}, f32[152,128]{1,0:T(8,128)S(1)}, u32[]{:S(2)}, u32[]{:S(2)}) collective-permute-start(f32[152,128]{1,0:T(8,128)} %get-tuple-element.28), channel_id=1, source_target_pairs={{0,8},{16,24},{24,16},{8,0},{1,9},{17,25},{25,17},{9,1},{2,10},{18... | collective-permute-start | bytes 233480 | tf_op jit(solution)/shard_map/ppermute | solution.py:794
  6.2 2.5 %collective-permute-start.1 = (f32[152,128]{1,0:T(8,128)}, f32[152,128]{1,0:T(8,128)S(1)}, u32[]{:S(2)}, u32[]{:S(2)}) collective-permute-start(f32[152,128]{1,0:T(8,128)} %get-tuple-element.29), channel_id=1, source_target_pairs={{0,24},{16,8},{24,0},{8,16},{1,25},{17,9},{25,1},{9,17},{2,26},{18... | collective-permute-start | bytes 233480 | tf_op jit(solution)/shard_map/ppermute | solution.py:795
  8.8 3.2 %shard_map.175 = (f32[7,5,32,128]{3,2,1,0:T(8,128)S(1)}, f32[7,4,32,128]{3,2,1,0:T(8,128)}, f32[7,4,32,128]{3,2,1,0:T(8,128)}) custom-call(f32[6,32,32,128]{3,2,1,0:T(8,128)} %refs_0_.5, f32[32,32,128]{2,1,0:T(8,128)S(1)} %copy-done), custom_call_target="tpu_custom_call" | custom-call | flops 1000000 | bytes 12000000 | tf_op jit(solution)/shard_map/pallas_call | solution.py:708
  12.0 1.0 %collective-permute-done.1.refs_2_ = f32[152,128]{1,0:T(8,128)S(1)} collective-permute-done((f32[152,128]{1,0:T(8,128)}, f32[152,128]{1,0:T(8,128)S(1)}, u32[]{:S(2)}, u32[]{:S(2)}) %collective-permute-start.1) | collective-permute-done | bytes 77856 | tf_op jit(solution)/shard_map/ppermute | solution.py:795
  13.1 0.3 shard_map.177
  13.3 0.3 collective-permute-done.2.refs_3_
  13.6 2.9 %shard_map.178 = f32[8,24,128]{2,1,0:T(8,128)} custom-call(f32[24,128]{1,0:T(8,128)S(1)} %copy-done.9, f32[152,128]{1,0:T(8,128)S(1)} %collective-permute-done.refs_1_, f32[152,128]{1,0:T(8,128)S(1)} %collective-permute-done.1.refs_2_, f32[24,128]{1,0:T(8,128)S(1)} %collective-permute-done.2.refs_3_, bf16[4,48,128]{2,1,0:T(8,128)(2,1)S(1)} %copy-done.7), custom_call_target="tpu_custom_call" | custom-call | flops 1000000 | bytes 9000000 | tf_op jit(solution)/shard_map/pallas_call | solution.py:708
  16.5 0.5 collective-permute-start.5
  17.0 1.7 %collective-permute-start.6 = (f32[7,4,32,128]{3,2,1,0:T(8,128)}, f32[7,4,32,128]{3,2,1,0:T(8,128)S(1)}, u32[]{:S(2)}, u32[]{:S(2)}) collective-permute-start(f32[7,4,32,128]{3,2,1,0:T(8,128)} %get-tuple-element.41), channel_id=1, source_target_pairs={{0,0},{8,16},{16,8},{24,24},{1,1},{9,17},{17,9},{25,25},{2,2},{10,... | collective-permute-start | bytes 1376264 | tf_op jit(solution)/shard_map/ppermute | solution.py:747
  18.7 3.7 %all-to-all-start = ((f32[8,24,128]{2,1,0:T(8,128)}), f32[8,24,128]{2,1,0:T(8,128)S(1)}, u32[]{:S(2)}, u32[]{:S(2)}) async-start(f32[8,24,128]{2,1,0:T(8,128)} %shard_map.178), calls=%async_computation | async-start | bytes 196608 | tf_op jit(solution)/shard_map/all_to_all | solution.py:813
  22.4 0.5 collective-permute-start.3
  22.9 2.5 %collective-permute-start.4 = (f32[160,128]{1,0:T(8,128)S(1)}, f32[160,128]{1,0:T(8,128)S(1)}, u32[]{:S(2)}, u32[]{:S(2)}) collective-permute-start(f32[160,128]{1,0:T(8,128)S(1)} %get-tuple-element.38), channel_id=1, source_target_pairs={{0,7},{1,2},{2,1},{3,4},{4,3},{5,6},{6,5},{7,0},{8,15},{9,10},{10,... | collective-permute-start | bytes 245768 | tf_op jit(solution)/shard_map/ppermute | solution.py:747
  25.4 3.4 %collective-permute-done.4.refs_3_ = f32[160,128]{1,0:T(8,128)S(1)} collective-permute-done((f32[160,128]{1,0:T(8,128)S(1)}, f32[160,128]{1,0:T(8,128)S(1)}, u32[]{:S(2)}, u32[]{:S(2)}) %collective-permute-start.4) | collective-permute-done | bytes 81952 | tf_op jit(solution)/shard_map/ppermute | solution.py:747
  28.9 2.1 %shard_map.179 = (f32[32,32,128]{2,1,0:T(8,128)}, f32[4,3,5,32,128]{4,3,2,1,0:T(8,128)}, f32[5,40,128]{2,1,0:T(8,128)S(1)}) custom-call(f32[7,5,32,128]{3,2,1,0:T(8,128)S(1)} %get-tuple-element.30.refs_0_, f32[8,24,128]{2,1,0:T(8,128)S(1)} %all-to-all-done.refs_1_, f32[160,128]{1,0:T(8,128)S(1)} %collective-permute-done.3.refs_2_, ...), custom_call_target="tpu_custom_call" | custom-call | flops 1000000 | bytes 15000000 | tf_op jit(solution)/shard_map/pallas_call | solution.py:708
  31.0 4.3 %all-to-all-start.1 = ((f32[32,32,128]{2,1,0:T(8,128)}), f32[32,32,128]{2,1,0:T(8,128)S(1)}, u32[]{:S(2)}, u32[]{:S(2)}) async-start(f32[32,32,128]{2,1,0:T(8,128)} %get-tuple-element.47), calls=%async_computation.1 | async-start | bytes 1048576 | tf_op jit(solution)/shard_map/all_to_all | solution.py:751
  35.4 2.6 %shard_map.180 = (f32[7,20,8,128]{3,2,1,0:T(8,128)}, f32[7,20,8,128]{3,2,1,0:T(8,128)}) custom-call(f32[6,32,32,128]{3,2,1,0:T(8,128)} %refs_0_.5, f32[32,32,128]{2,1,0:T(8,128)S(1)} %copy-done, f32[7,4,32,128]{3,2,1,0:T(8,128)S(1)} %collective-permute-done.5.refs_2_, f32[7,4,32,128]{3,2,1,0:T(8,128)S(1)} %collective-permute-done.6.refs_3_), custom_call_target="tpu_custom_call" | custom-call | flops 1000000 | bytes 6000000 | tf_op jit(solution)/shard_map/pallas_call | solution.py:708
  38.0 0.3 collective-permute-start.7
  38.3 5.9 %collective-permute-start.8 = (f32[7,20,8,128]{3,2,1,0:T(8,128)}, f32[7,20,8,128]{3,2,1,0:T(8,128)}, u32[]{:S(2)}, u32[]{:S(2)}) collective-permute-start(f32[7,20,8,128]{3,2,1,0:T(8,128)} %get-tuple-element.46), channel_id=1, source_target_pairs={{0,0},{1,2},{2,1},{3,4},{4,3},{5,6},{6,5},{7,7},{8,8},{9,10},{10,9... | collective-permute-start | bytes 1720328 | tf_op jit(solution)/shard_map/ppermute | solution.py:747
  44.2 6.7 %all-to-all-done.1.refs_0_ = f32[32,32,128]{2,1,0:T(8,128)S(1)} async-done(((f32[32,32,128]{2,1,0:T(8,128)}), f32[32,32,128]{2,1,0:T(8,128)S(1)}, u32[]{:S(2)}, u32[]{:S(2)}) %all-to-all-start.1) | async-done | bytes 524320 | tf_op jit(solution)/shard_map/all_to_all | solution.py:751
  51.0 6.4 %shard_map.182 = (f32[8,256]{1,0:T(8,128)}, f32[32,8,128]{2,1,0:T(8,128)}) custom-call(f32[32,32,128]{2,1,0:T(8,128)S(1)} %all-to-all-done.1.refs_0_, bf16[2,512,256]{2,1,0:T(8,128)(2,1)S(1)} %copy-done.1, bf16[2,512,512]{2,1,0:T(8,128)(2,1)} %constant.22.clone.refs_2_, bf16[8,2,128,512]{3,2,1,0:T(8,128)(2,1)} %constant.23.clone.refs_3_, ...), custom_call_target="tpu_custom_call" | custom-call | flops 1000000 | bytes 18000000 | tf_op jit(solution)/shard_map/pallas_call | solution.py:708
  57.4 3.1 %all-to-all-start.2 = ((f32[32,8,128]{2,1,0:T(8,128)}), f32[32,8,128]{2,1,0:T(8,128)S(1)}, u32[]{:S(2)}, u32[]{:S(2)}) async-start(f32[32,8,128]{2,1,0:T(8,128)} %get-tuple-element.50), calls=%async_computation.2 | async-start | bytes 262144 | tf_op jit(solution)/shard_map/all_to_all | solution.py:751
  60.5 10.8 %shard_map.181 = f32[6,32,32,128]{3,2,1,0:T(8,128)} custom-call(f32[6,32,32,128]{3,2,1,0:T(8,128)} %refs_0_.5, f32[32,32,128]{2,1,0:T(8,128)S(1)} %copy-done, f32[7,4,32,128]{3,2,1,0:T(8,128)S(1)} %collective-permute-done.5.refs_2_, f32[7,4,32,128]{3,2,1,0:T(8,128)S(1)} %collective-permute-done.6.refs_3_, ...), custom_call_target="tpu_custom_call" | custom-call | flops 1000000 | bytes 30000000 | tf_op jit(solution)/shard_map/pallas_call | solution.py:708
  71.3 0.9 %shard_map.183 = f32[1,128]{1,0:T(1,128)} custom-call(f32[256,128]{1,0:T(8,128)S(1)} %bitcast.6, f32[16,128]{1,0:T(8,128)S(1)} %bitcast.8, s32[1,128]{1,0:T(1,128)S(1)} %bitcast.12, s32[2,128]{1,0:T(2,128)S(1)} %bitcast.10), custom_call_target="tpu_custom_call" | custom-call | flops 1000000 | bytes 3000000 | tf_op jit(solution)/shard_map/pallas_call | solution.py:708
  (33 shorter events, 0.2 us)
Async XLA Ops:
  0.6 8.1 %copy-start = (f32[32,32,128]{2,1,0:T(8,128)S(1)}, f32[32,32,128]{2,1,0:T(8,128)}, u32[]{:S(2)}) copy-start(f32[32,32,128]{2,1,0:T(8,128)} %refs_1_.6) | copy-start | bytes 1572868
  0.6 13.0 %copy-start.7 = (bf16[4,48,128]{2,1,0:T(8,128)(2,1)S(1)}, bf16[4,48,128]{2,1,0:T(8,128)(2,1)}, u32[]{:S(2)}) copy-start(bf16[4,48,128]{2,1,0:T(8,128)(2,1)} %constant.18.clone.refs_4_) | copy-start | bytes 147460
  3.1 10.5 %copy-start.9 = (f32[24,128]{1,0:T(8,128)S(1)}, f32[24,128]{1,0:T(8,128)}, u32[]{:S(2)}) copy-start(f32[24,128]{1,0:T(8,128)} %get-tuple-element.33.refs_0_) | copy-start | bytes 36868
  3.1 25.8 %copy-start.5 = (bf16[640,128]{1,0:T(8,128)(2,1)S(1)}, bf16[640,128]{1,0:T(8,128)(2,1)}, u32[]{:S(2)}) copy-start(bf16[640,128]{1,0:T(8,128)(2,1)} %constant.20.clone.refs_5_) | copy-start | bytes 491524
  3.1 25.8 %copy-start.6 = (bf16[128,640]{1,0:T(8,128)(2,1)S(1)}, bf16[128,640]{1,0:T(8,128)(2,1)}, u32[]{:S(2)}) copy-start(bf16[128,640]{1,0:T(8,128)(2,1)} %constant.19.clone.refs_4_) | copy-start | bytes 491524
  3.1 8.9 %collective-permute-start = (f32[152,128]{1,0:T(8,128)}, f32[152,128]{1,0:T(8,128)S(1)}, u32[]{:S(2)}, u32[]{:S(2)}) collective-permute-start(f32[152,128]{1,0:T(8,128)} %get-tuple-element.28), channel_id=1, source_target_pairs={{0,8},{16,24},{24,16},{8,0},{1,9},{17,25},{25,17},{9,1},{2,10},{18... | collective-permute-start | bytes 233480 | tf_op jit(solution)/shard_map/ppermute | solution.py:794
  6.2 6.9 %collective-permute-start.1 = (f32[152,128]{1,0:T(8,128)}, f32[152,128]{1,0:T(8,128)S(1)}, u32[]{:S(2)}, u32[]{:S(2)}) collective-permute-start(f32[152,128]{1,0:T(8,128)} %get-tuple-element.29), channel_id=1, source_target_pairs={{0,24},{16,8},{24,0},{8,16},{1,25},{17,9},{25,1},{9,17},{2,26},{18... | collective-permute-start | bytes 233480 | tf_op jit(solution)/shard_map/ppermute | solution.py:795
  8.7 4.9 %collective-permute-start.2 = (f32[24,128]{1,0:T(8,128)}, f32[24,128]{1,0:T(8,128)S(1)}, u32[]{:S(2)}, u32[]{:S(2)}) collective-permute-start(f32[24,128]{1,0:T(8,128)} %get-tuple-element.33.refs_0_), channel_id=1, source_target_pairs={{0,16},{16,0},{24,8},{8,24},{1,17},{17,1},{25,9},{9,25},{2,18},{18... | collective-permute-start | bytes 36872 | tf_op jit(solution)/shard_map/ppermute | solution.py:796
  16.5 14.5 %collective-permute-start.5 = (f32[7,4,32,128]{3,2,1,0:T(8,128)}, f32[7,4,32,128]{3,2,1,0:T(8,128)S(1)}, u32[]{:S(2)}, u32[]{:S(2)}) collective-permute-start(f32[7,4,32,128]{3,2,1,0:T(8,128)} %get-tuple-element.40), channel_id=1, source_target_pairs={{0,8},{8,0},{16,24},{24,16},{1,9},{9,1},{17,25},{25,17},{2,10},{10... | collective-permute-start | bytes 1376264 | tf_op jit(solution)/shard_map/ppermute | solution.py:743
  17.0 14.0 %collective-permute-start.6 = (f32[7,4,32,128]{3,2,1,0:T(8,128)}, f32[7,4,32,128]{3,2,1,0:T(8,128)S(1)}, u32[]{:S(2)}, u32[]{:S(2)}) collective-permute-start(f32[7,4,32,128]{3,2,1,0:T(8,128)} %get-tuple-element.41), channel_id=1, source_target_pairs={{0,0},{8,16},{16,8},{24,24},{1,1},{9,17},{17,9},{25,25},{2,2},{10,... | collective-permute-start | bytes 1376264 | tf_op jit(solution)/shard_map/ppermute | solution.py:747
  18.7 10.2 %all-to-all-start = ((f32[8,24,128]{2,1,0:T(8,128)}), f32[8,24,128]{2,1,0:T(8,128)S(1)}, u32[]{:S(2)}, u32[]{:S(2)}) async-start(f32[8,24,128]{2,1,0:T(8,128)} %shard_map.178), calls=%async_computation | async-start | bytes 196608 | tf_op jit(solution)/shard_map/all_to_all | solution.py:813
  22.4 3.0 %collective-permute-start.3 = (f32[160,128]{1,0:T(8,128)S(1)}, f32[160,128]{1,0:T(8,128)S(1)}, u32[]{:S(2)}, u32[]{:S(2)}) collective-permute-start(f32[160,128]{1,0:T(8,128)S(1)} %get-tuple-element.37), channel_id=1, source_target_pairs={{0,1},{1,0},{2,3},{3,2},{4,5},{5,4},{6,7},{7,6},{8,9},{9,8},{10,11... | collective-permute-start | bytes 245768 | tf_op jit(solution)/shard_map/ppermute | solution.py:743
  22.9 6.0 %collective-permute-start.4 = (f32[160,128]{1,0:T(8,128)S(1)}, f32[160,128]{1,0:T(8,128)S(1)}, u32[]{:S(2)}, u32[]{:S(2)}) collective-permute-start(f32[160,128]{1,0:T(8,128)S(1)} %get-tuple-element.38), channel_id=1, source_target_pairs={{0,7},{1,2},{2,1},{3,4},{4,3},{5,6},{6,5},{7,0},{8,15},{9,10},{10,... | collective-permute-start | bytes 245768 | tf_op jit(solution)/shard_map/ppermute | solution.py:747
  28.9 22.1 %copy-start.1 = (bf16[2,512,256]{2,1,0:T(8,128)(2,1)S(1)}, bf16[2,512,256]{2,1,0:T(8,128)(2,1)}, u32[]{:S(2)}) copy-start(bf16[2,512,256]{2,1,0:T(8,128)(2,1)} %constant.21.clone.refs_1_) | copy-start | bytes 1572868
  28.9 22.1 %copy-start.2 = (f32[256,256]{1,0:T(8,128)S(1)}, f32[256,256]{1,0:T(8,128)}, u32[]{:S(2)}) copy-start(f32[256,256]{1,0:T(8,128)} %refs_7_.1) | copy-start | bytes 786436
  31.0 19.9 %copy-start.3 = (bf16[128,640]{1,0:T(8,128)(2,1)S(1)}, bf16[128,640]{1,0:T(8,128)(2,1)}, u32[]{:S(2)}) copy-start(bf16[128,640]{1,0:T(8,128)(2,1)} %constant.26.clone.refs_6_) | copy-start | bytes 491524
  31.0 20.0 %copy-start.4 = (bf16[640,128]{1,0:T(8,128)(2,1)S(1)}, bf16[640,128]{1,0:T(8,128)(2,1)}, u32[]{:S(2)}) copy-start(bf16[640,128]{1,0:T(8,128)(2,1)} %constant.25.clone.refs_5_) | copy-start | bytes 491524
  31.0 19.9 %all-to-all-start.1 = ((f32[32,32,128]{2,1,0:T(8,128)}), f32[32,32,128]{2,1,0:T(8,128)S(1)}, u32[]{:S(2)}, u32[]{:S(2)}) async-start(f32[32,32,128]{2,1,0:T(8,128)} %get-tuple-element.47), calls=%async_computation.1 | async-start | bytes 1048576 | tf_op jit(solution)/shard_map/all_to_all | solution.py:751
  38.0 22.5 %collective-permute-start.7 = (f32[7,20,8,128]{3,2,1,0:T(8,128)}, f32[7,20,8,128]{3,2,1,0:T(8,128)}, u32[]{:S(2)}, u32[]{:S(2)}) collective-permute-start(f32[7,20,8,128]{3,2,1,0:T(8,128)} %get-tuple-element.45), channel_id=1, source_target_pairs={{0,1},{1,0},{2,3},{3,2},{4,5},{5,4},{6,7},{7,6},{8,9},{9,8},{10,11... | collective-permute-start | bytes 1720328 | tf_op jit(solution)/shard_map/ppermute | solution.py:743
  38.3 22.2 %collective-permute-start.8 = (f32[7,20,8,128]{3,2,1,0:T(8,128)}, f32[7,20,8,128]{3,2,1,0:T(8,128)}, u32[]{:S(2)}, u32[]{:S(2)}) collective-permute-start(f32[7,20,8,128]{3,2,1,0:T(8,128)} %get-tuple-element.46), channel_id=1, source_target_pairs={{0,0},{1,2},{2,1},{3,4},{4,3},{5,6},{6,5},{7,7},{8,8},{9,10},{10,9... | collective-permute-start | bytes 1720328 | tf_op jit(solution)/shard_map/ppermute | solution.py:747
  57.4 13.9 %all-to-all-start.2 = ((f32[32,8,128]{2,1,0:T(8,128)}), f32[32,8,128]{2,1,0:T(8,128)S(1)}, u32[]{:S(2)}, u32[]{:S(2)}) async-start(f32[32,8,128]{2,1,0:T(8,128)} %get-tuple-element.50), calls=%async_computation.2 | async-start | bytes 262144 | tf_op jit(solution)/shard_map/all_to_all | solution.py:751
  60.4 10.9 %copy-start.8 = (f32[128,16]{0,1:T(8,128)S(1)}, f32[128,16]{0,1:T(8,128)}, u32[]{:S(2)}) copy-start(f32[128,16]{0,1:T(8,128)} %param.20) | copy-start | bytes 24580
  60.4 10.9 %copy-start.10 = (s32[128,2]{0,1:T(2,128)S(1)}, s32[128,2]{0,1:T(2,128)}, u32[]{:S(2)}) copy-start(s32[128,2]{0,1:T(2,128)} %param.22) | copy-start | bytes 3076
  60.5 10.9 %copy-start.11 = (s32[128,1]{0,1:T(1,128)S(1)}, s32[128,1]{0,1:T(1,128)}, u32[]{:S(2)}) copy-start(s32[128,1]{0,1:T(1,128)} %param.21) | copy-start | bytes 1540

commit v5 on v4

--- a/solution.py
+++ b/solution.py
@@ -583,7 +583,7 @@
 
 def full_kernel(
     span_x, span_y, fields, eps, rim_a, rim_b, inverse, from_a, from_b,
-    out, one, two, rate_elec, rate_magn, held, arriving, leaving,
+    out, one, two, rate_elec, rate_magn, arriving, leaving,
 ):
     place = my_place()
     even_x, even_y = place[0] % 2 == 0, place[1] % 2 == 0
@@ -603,14 +603,18 @@
     above_bottom = lane > 0
     has_south = place[1] > 0
     has_north = place[1] < span_y - 1
-    for array in range(ARRAYS):
-        dest = rate_elec if array == 6 else one.at[array]
-        for at in range(EXT // 2):
+
+    def rims(at, _):
+        for array in range(ARRAYS):
+            dest = rate_elec if array == 6 else one.at[array]
             first, second = from_a[array, at], from_b[array, at]
             north = jnp.where(has_north, jnp.where(even_y, first, second), 0.0)
             south = jnp.where(has_south, jnp.where(even_y, second, first), 0.0)
             for odd in range(2):
                 dest[2 * at + odd, TILE:] = rim_of(north, south, odd)
+        return 0
+
+    lax.fori_loop(0, EXT // 2, rims, 0)
     for arrival in arrivals:
         arrival.wait()
     for present, offset in ((place[0] > 0, 0), (place[0] < span_x - 1, HALO + TILE)):
@@ -623,14 +627,18 @@
                 for array in range(6):
                     one[array, offset + step] = blank
 
-    for x in range(EXT):
-        cell = (x - HALO) % EXT
-        spread = pltpu.roll(inverse[cell % RUN], (BAND_START - BAND * (cell // RUN)) % 128, 1)
-        value = rate_elec[x]
-        inside = value > 0.0
-        plain = jnp.where(inside, 1.0 / jnp.where(inside, value, 1.0), 0.0)
-        rate_elec[x] = COURANT * jnp.where(in_layers, spread, plain)
-        rate_magn[x] = jnp.where(inside, COURANT, 0.0)
+    def rates(group, _):
+        for run in range(RUN):
+            x = lax.rem(RUN * group + run + HALO, EXT)
+            spread = pltpu.roll(inverse[run], lax.rem(128 + BAND_START - BAND * group, 128), 1)
+            value = rate_elec[x]
+            inside = value > 0.0
+            plain = jnp.where(inside, 1.0 / jnp.where(inside, value, 1.0), 0.0)
+            rate_elec[x] = COURANT * jnp.where(in_layers, spread, plain)
+            rate_magn[x] = jnp.where(inside, COURANT, 0.0)
+        return 0
+
+    lax.fori_loop(0, GROUPS, rates, 0)
 
     def magnetic(rate, magn, ex, ey, ez, ey_next, ez_next):
         hx, hy, hz = magn
@@ -652,7 +660,11 @@
             ez + rate * ((hy - hy_last) - (hx - behind_y(hx))),
         )
 
-    def sweep(source, dest, start, stop, shift, state):
+    def leaving_copy(part, array, x):
+        source = one.at[array, pl.ds(x, UNROLL), :TILE]
+        return pltpu.make_async_copy(source, out.at[array, pl.ds(x - HALO, UNROLL)], leaving.at[6 * part + array])
+
+    def sweep(source, dest, moment, last):
         def read(first, x):
             return tuple(source[first + component, x] for component in range(3))
 
@@ -662,42 +674,43 @@
             magn = magnetic(rate_magn[x], read(3, x), *elec, after[1], after[2])
             new = electric(rate_elec[x], elec, *magn, hy_last, hz_last) + magn
             for array in range(6):
-                dest[array, x - shift] = new[array][:TILE] if shift else new[array]
+                dest[array, x] = new[array]
             return after, magn[1], magn[2]
 
-        if state is None:
-            before, elec = read(0, start - 1), read(0, start)
-            magn = magnetic(rate_magn[start - 1], read(3, start - 1), *before, elec[1], elec[2])
-            state = elec, magn[1], magn[2]
-
-        def cells(at, state):
+        def many(at, state):
+            begin = moment + UNROLL * at
             for step in range(UNROLL):
-                state = advance(start + UNROLL * at + step, state)
+                state = advance(begin + step, state)
+            if last is not None:
+
+                @pl.when(last)
+                def _():
+                    for array in range(6):
+                        leaving_copy(at, array, begin).start()
+
             return state
 
-        whole = (stop - start) // UNROLL
-        state = lax.fori_loop(0, whole, cells, state)
-        for x in range(start + UNROLL * whole, stop):
-            state = advance(x, state)
-        return state
-
-    for moment in range(1, NT):
-        source, dest = (one, two) if moment % 2 == 1 else (two, one)
-        sweep(source, dest, moment, EXT - moment, 0, None)
-    state = None
-    departures = []
-    source = one if NT % 2 == 1 else two
-    for part in range(2):
-        begin, end = part * TILE // 2, (part + 1) * TILE // 2
-        state = sweep(source, held, HALO + begin, HALO + end, HALO, state)
+        count = EXT - 2 * moment
+        whole = lax.div(count, UNROLL)
+
+        def two_cells(at, state):
+            begin = moment + UNROLL * whole + 2 * at
+            return advance(begin + 1, advance(begin, state))
+
+        before, elec = read(0, moment - 1), read(0, moment)
+        magn = magnetic(rate_magn[moment - 1], read(3, moment - 1), *before, elec[1], elec[2])
+        state = lax.fori_loop(0, whole, many, (elec, magn[1], magn[2]))
+        lax.fori_loop(0, lax.div(count - UNROLL * whole, 2), two_cells, state)
+
+    def two_leaps(turn, _):
+        sweep(one, two, 2 * turn + 1, None)
+        sweep(two, one, 2 * turn + 2, turn == NT // 2 - 1)
+        return 0
+
+    lax.fori_loop(0, NT // 2, two_leaps, 0)
+    for part in range(TILE // UNROLL):
         for array in range(6):
-            copy = pltpu.make_async_copy(
-                held.at[array, begin:end], out.at[array, begin:end], leaving.at[6 * part + array]
-            )
-            copy.start()
-            departures.append(copy)
-    for copy in departures:
-        copy.wait()
+            leaving_copy(part, array, HALO + UNROLL * part).wait()
 
 
 def call(kernel, out_shape, operands, scratch=(), micros=1.0, room=52, anywhere=(), out_anywhere=()):
@@ -852,9 +865,8 @@
             pltpu.VMEM((6, EXT, EXT, 128), F32),
             pltpu.VMEM((EXT, EXT, 128), F32),
             pltpu.VMEM((EXT, EXT, 128), F32),
-            pltpu.VMEM((6, TILE, TILE, 128), F32),
             dma((3 * ARRAYS,)),
-            dma((12,)),
+            dma((24,)),
         ),
         micros=10.0,
         anywhere=(0, 1, 2, 3),

time: 73.1 us -> 74.5 us (1.019)
  Pallas kernels: 31.6 us -> 33 us
    pallas_call x9, Pallas kernels: 31.6 us -> 33 us  [call(): pl.pallas_call(kernel, out_shape=out_shape, in_specs=[hbm if at in anywhe...]
  transfers between devices with their start and end apart: 12 -> 12, of which waited for: 4 -> 4; matrix products, arithmetic and copies ran while one was open for 0% -> 0% of each run, Pallas kernels for 35% -> 36%
where the time goes in v5:
time: 74.5 us; the launch traced here: 73.6 us
  Pallas kernels  33 us (44%)
  starting transfers between devices  28.3 us (38%)
  waiting for transfers between devices  11.4 us (15%)
  between operations  0.87 us (1%)
    pallas_call x9, Pallas kernels, call(): pl.pallas_call(kernel, out_shape=out_shape, in_specs=[hbm if at in anywhe...  33 us
    ppermute x3, starting transfers between devices, paired(): return lax.ppermute(value, axis, pairs)  10.1 us
    all_to_all x2, starting transfers between devices, to_all(): lax.all_to_all(value, ('gx', 'gy'), split_axis=0, concat_axis=0, tiled=True)  7.4 us
    all_to_all x2, waiting for transfers between devices, to_all(): lax.all_to_all(value, ('gx', 'gy'), split_axis=0, concat_axis=0, tiled=True)  6.71 us
    all_to_all x1, starting transfers between devices, shards(): lax.all_to_all(windows, 'gy', split_axis=0, concat_axis=0, tiled=True)  3.73 us
    ppermute x3, waiting for transfers between devices, paired(): return lax.ppermute(value, axis, pairs)  3.42 us
    ppermute x1, starting transfers between devices, shards(): from_a = lax.ppermute(pay_a, 'gx', pairings[0])  3.09 us
    ppermute x1, starting transfers between devices, shards(): from_b = lax.ppermute(pay_b, 'gx', pairings[1])  2.47 us
  transfers between devices with their start and end apart: 12, of which 4 were waited for; matrix products, arithmetic and copies ran while one was open for 0% of the time, Pallas kernels for 36%

profile of v5, /device:TPU:0, one launch (start us, length us, event | category | flops | bytes accessed | tf_op | source)
XLA Modules:
  0.0 73.6 jit_solution(1892022107597760903)
XLA Ops:
  0.7 2.4 %shard_map.176 = (f32[152,128]{1,0:T(8,128)}, f32[152,128]{1,0:T(8,128)}, f32[24,128]{1,0:T(8,128)}) custom-call(f32[6,32,32,128]{3,2,1,0:T(8,128)} %refs_0_.5, f32[32,32,128]{2,1,0:T(8,128)} %refs_1_.6, f32[16,128]{1,0:T(8,128)} %bitcast.7, f32[1,128]{1,0:T(1,128)} %bitcast.13, s32[1,128]{1,0:T(1,128)} %bitcast.11, s32[2,128]{1,0:T(2,128)} %bitcast.9), custom_call_target="tpu_custom_call" | custom-call | flops 1000000 | bytes 6000000 | tf_op jit(solution)/shard_map/pallas_call | solution.py:721
  3.1 3.1 %collective-permute-start = (f32[152,128]{1,0:T(8,128)}, f32[152,128]{1,0:T(8,128)S(1)}, u32[]{:S(2)}, u32[]{:S(2)}) collective-permute-start(f32[152,128]{1,0:T(8,128)} %get-tuple-element.28), channel_id=1, source_target_pairs={{0,8},{16,24},{24,16},{8,0},{1,9},{17,25},{25,17},{9,1},{2,10},{18... | collective-permute-start | bytes 233480 | tf_op jit(solution)/shard_map/ppermute | solution.py:807
  6.2 2.5 %collective-permute-start.1 = (f32[152,128]{1,0:T(8,128)}, f32[152,128]{1,0:T(8,128)S(1)}, u32[]{:S(2)}, u32[]{:S(2)}) collective-permute-start(f32[152,128]{1,0:T(8,128)} %get-tuple-element.29), channel_id=1, source_target_pairs={{0,24},{16,8},{24,0},{8,16},{1,25},{17,9},{25,1},{9,17},{2,26},{18... | collective-permute-start | bytes 233480 | tf_op jit(solution)/shard_map/ppermute | solution.py:808
  8.8 3.2 %shard_map.175 = (f32[7,5,32,128]{3,2,1,0:T(8,128)S(1)}, f32[7,4,32,128]{3,2,1,0:T(8,128)}, f32[7,4,32,128]{3,2,1,0:T(8,128)}) custom-call(f32[6,32,32,128]{3,2,1,0:T(8,128)} %refs_0_.5, f32[32,32,128]{2,1,0:T(8,128)S(1)} %copy-done), custom_call_target="tpu_custom_call" | custom-call | flops 1000000 | bytes 12000000 | tf_op jit(solution)/shard_map/pallas_call | solution.py:721
  12.0 1.0 %collective-permute-done.1.refs_2_ = f32[152,128]{1,0:T(8,128)S(1)} collective-permute-done((f32[152,128]{1,0:T(8,128)}, f32[152,128]{1,0:T(8,128)S(1)}, u32[]{:S(2)}, u32[]{:S(2)}) %collective-permute-start.1) | collective-permute-done | bytes 77856 | tf_op jit(solution)/shard_map/ppermute | solution.py:808
  13.1 0.3 shard_map.177
  13.3 0.3 collective-permute-done.2.refs_3_
  13.6 2.9 %shard_map.178 = f32[8,24,128]{2,1,0:T(8,128)} custom-call(f32[24,128]{1,0:T(8,128)S(1)} %copy-done.9, f32[152,128]{1,0:T(8,128)S(1)} %collective-permute-done.refs_1_, f32[152,128]{1,0:T(8,128)S(1)} %collective-permute-done.1.refs_2_, f32[24,128]{1,0:T(8,128)S(1)} %collective-permute-done.2.refs_3_, bf16[4,48,128]{2,1,0:T(8,128)(2,1)S(1)} %copy-done.7), custom_call_target="tpu_custom_call" | custom-call | flops 1000000 | bytes 9000000 | tf_op jit(solution)/shard_map/pallas_call | solution.py:721
  16.5 0.5 collective-permute-start.5
  17.0 1.7 %collective-permute-start.6 = (f32[7,4,32,128]{3,2,1,0:T(8,128)}, f32[7,4,32,128]{3,2,1,0:T(8,128)S(1)}, u32[]{:S(2)}, u32[]{:S(2)}) collective-permute-start(f32[7,4,32,128]{3,2,1,0:T(8,128)} %get-tuple-element.41), channel_id=1, source_target_pairs={{0,0},{8,16},{16,8},{24,24},{1,1},{9,17},{17,9},{25,25},{2,2},{10,... | collective-permute-start | bytes 1376264 | tf_op jit(solution)/shard_map/ppermute | solution.py:760
  18.7 3.7 %all-to-all-start = ((f32[8,24,128]{2,1,0:T(8,128)}), f32[8,24,128]{2,1,0:T(8,128)S(1)}, u32[]{:S(2)}, u32[]{:S(2)}) async-start(f32[8,24,128]{2,1,0:T(8,128)} %shard_map.178), calls=%async_computation | async-start | bytes 196608 | tf_op jit(solution)/shard_map/all_to_all | solution.py:826
  22.4 0.5 collective-permute-start.3
  22.9 2.5 %collective-permute-start.4 = (f32[160,128]{1,0:T(8,128)S(1)}, f32[160,128]{1,0:T(8,128)S(1)}, u32[]{:S(2)}, u32[]{:S(2)}) collective-permute-start(f32[160,128]{1,0:T(8,128)S(1)} %get-tuple-element.38), channel_id=1, source_target_pairs={{0,7},{1,2},{2,1},{3,4},{4,3},{5,6},{6,5},{7,0},{8,15},{9,10},{10,... | collective-permute-start | bytes 245768 | tf_op jit(solution)/shard_map/ppermute | solution.py:760
  25.4 3.4 %collective-permute-done.4.refs_3_ = f32[160,128]{1,0:T(8,128)S(1)} collective-permute-done((f32[160,128]{1,0:T(8,128)S(1)}, f32[160,128]{1,0:T(8,128)S(1)}, u32[]{:S(2)}, u32[]{:S(2)}) %collective-permute-start.4) | collective-permute-done | bytes 81952 | tf_op jit(solution)/shard_map/ppermute | solution.py:760
  28.9 2.1 %shard_map.179 = (f32[32,32,128]{2,1,0:T(8,128)}, f32[4,3,5,32,128]{4,3,2,1,0:T(8,128)}, f32[5,40,128]{2,1,0:T(8,128)S(1)}) custom-call(f32[7,5,32,128]{3,2,1,0:T(8,128)S(1)} %get-tuple-element.30.refs_0_, f32[8,24,128]{2,1,0:T(8,128)S(1)} %all-to-all-done.refs_1_, f32[160,128]{1,0:T(8,128)S(1)} %collective-permute-done.3.refs_2_, ...), custom_call_target="tpu_custom_call" | custom-call | flops 1000000 | bytes 15000000 | tf_op jit(solution)/shard_map/pallas_call | solution.py:721
  31.0 4.3 %all-to-all-start.1 = ((f32[32,32,128]{2,1,0:T(8,128)}), f32[32,32,128]{2,1,0:T(8,128)S(1)}, u32[]{:S(2)}, u32[]{:S(2)}) async-start(f32[32,32,128]{2,1,0:T(8,128)} %get-tuple-element.47), calls=%async_computation.1 | async-start | bytes 1048576 | tf_op jit(solution)/shard_map/all_to_all | solution.py:764
  35.4 2.6 %shard_map.180 = (f32[7,20,8,128]{3,2,1,0:T(8,128)}, f32[7,20,8,128]{3,2,1,0:T(8,128)}) custom-call(f32[6,32,32,128]{3,2,1,0:T(8,128)} %refs_0_.5, f32[32,32,128]{2,1,0:T(8,128)S(1)} %copy-done, f32[7,4,32,128]{3,2,1,0:T(8,128)S(1)} %collective-permute-done.5.refs_2_, f32[7,4,32,128]{3,2,1,0:T(8,128)S(1)} %collective-permute-done.6.refs_3_), custom_call_target="tpu_custom_call" | custom-call | flops 1000000 | bytes 6000000 | tf_op jit(solution)/shard_map/pallas_call | solution.py:721
  38.0 0.3 collective-permute-start.7
  38.3 5.9 %collective-permute-start.8 = (f32[7,20,8,128]{3,2,1,0:T(8,128)}, f32[7,20,8,128]{3,2,1,0:T(8,128)}, u32[]{:S(2)}, u32[]{:S(2)}) collective-permute-start(f32[7,20,8,128]{3,2,1,0:T(8,128)} %get-tuple-element.46), channel_id=1, source_target_pairs={{0,0},{1,2},{2,1},{3,4},{4,3},{5,6},{6,5},{7,7},{8,8},{9,10},{10,9... | collective-permute-start | bytes 1720328 | tf_op jit(solution)/shard_map/ppermute | solution.py:760
  44.2 6.7 %all-to-all-done.1.refs_0_ = f32[32,32,128]{2,1,0:T(8,128)S(1)} async-done(((f32[32,32,128]{2,1,0:T(8,128)}), f32[32,32,128]{2,1,0:T(8,128)S(1)}, u32[]{:S(2)}, u32[]{:S(2)}) %all-to-all-start.1) | async-done | bytes 524320 | tf_op jit(solution)/shard_map/all_to_all | solution.py:764
  51.0 6.4 %shard_map.182 = (f32[8,256]{1,0:T(8,128)}, f32[32,8,128]{2,1,0:T(8,128)}) custom-call(f32[32,32,128]{2,1,0:T(8,128)S(1)} %all-to-all-done.1.refs_0_, bf16[2,512,256]{2,1,0:T(8,128)(2,1)S(1)} %copy-done.1, bf16[2,512,512]{2,1,0:T(8,128)(2,1)} %constant.22.clone.refs_2_, bf16[8,2,128,512]{3,2,1,0:T(8,128)(2,1)} %constant.23.clone.refs_3_, ...), custom_call_target="tpu_custom_call" | custom-call | flops 1000000 | bytes 18000000 | tf_op jit(solution)/shard_map/pallas_call | solution.py:721
  57.4 3.1 %all-to-all-start.2 = ((f32[32,8,128]{2,1,0:T(8,128)}), f32[32,8,128]{2,1,0:T(8,128)S(1)}, u32[]{:S(2)}, u32[]{:S(2)}) async-start(f32[32,8,128]{2,1,0:T(8,128)} %get-tuple-element.50), calls=%async_computation.2 | async-start | bytes 262144 | tf_op jit(solution)/shard_map/all_to_all | solution.py:764
  60.5 12.2 %shard_map.181 = f32[6,32,32,128]{3,2,1,0:T(8,128)} custom-call(f32[6,32,32,128]{3,2,1,0:T(8,128)} %refs_0_.5, f32[32,32,128]{2,1,0:T(8,128)S(1)} %copy-done, f32[7,4,32,128]{3,2,1,0:T(8,128)S(1)} %collective-permute-done.5.refs_2_, f32[7,4,32,128]{3,2,1,0:T(8,128)S(1)} %collective-permute-done.6.refs_3_, ...), custom_call_target="tpu_custom_call" | custom-call | flops 1000000 | bytes 30000000 | tf_op jit(solution)/shard_map/pallas_call | solution.py:721
  72.7 0.9 %shard_map.183 = f32[1,128]{1,0:T(1,128)} custom-call(f32[256,128]{1,0:T(8,128)S(1)} %bitcast.6, f32[16,128]{1,0:T(8,128)S(1)} %bitcast.8, s32[1,128]{1,0:T(1,128)S(1)} %bitcast.12, s32[2,128]{1,0:T(2,128)S(1)} %bitcast.10), custom_call_target="tpu_custom_call" | custom-call | flops 1000000 | bytes 3000000 | tf_op jit(solution)/shard_map/pallas_call | solution.py:721
  (33 shorter events, 0.2 us)
Async XLA Ops:
  0.6 8.1 %copy-start = (f32[32,32,128]{2,1,0:T(8,128)S(1)}, f32[32,32,128]{2,1,0:T(8,128)}, u32[]{:S(2)}) copy-start(f32[32,32,128]{2,1,0:T(8,128)} %refs_1_.6) | copy-start | bytes 1572868
  0.6 13.0 %copy-start.7 = (bf16[4,48,128]{2,1,0:T(8,128)(2,1)S(1)}, bf16[4,48,128]{2,1,0:T(8,128)(2,1)}, u32[]{:S(2)}) copy-start(bf16[4,48,128]{2,1,0:T(8,128)(2,1)} %constant.18.clone.refs_4_) | copy-start | bytes 147460
  3.1 10.5 %copy-start.9 = (f32[24,128]{1,0:T(8,128)S(1)}, f32[24,128]{1,0:T(8,128)}, u32[]{:S(2)}) copy-start(f32[24,128]{1,0:T(8,128)} %get-tuple-element.33.refs_0_) | copy-start | bytes 36868
  3.1 25.8 %copy-start.5 = (bf16[640,128]{1,0:T(8,128)(2,1)S(1)}, bf16[640,128]{1,0:T(8,128)(2,1)}, u32[]{:S(2)}) copy-start(bf16[640,128]{1,0:T(8,128)(2,1)} %constant.20.clone.refs_5_) | copy-start | bytes 491524
  3.1 25.8 %copy-start.6 = (bf16[128,640]{1,0:T(8,128)(2,1)S(1)}, bf16[128,640]{1,0:T(8,128)(2,1)}, u32[]{:S(2)}) copy-start(bf16[128,640]{1,0:T(8,128)(2,1)} %constant.19.clone.refs_4_) | copy-start | bytes 491524
  3.1 8.9 %collective-permute-start = (f32[152,128]{1,0:T(8,128)}, f32[152,128]{1,0:T(8,128)S(1)}, u32[]{:S(2)}, u32[]{:S(2)}) collective-permute-start(f32[152,128]{1,0:T(8,128)} %get-tuple-element.28), channel_id=1, source_target_pairs={{0,8},{16,24},{24,16},{8,0},{1,9},{17,25},{25,17},{9,1},{2,10},{18... | collective-permute-start | bytes 233480 | tf_op jit(solution)/shard_map/ppermute | solution.py:807
  6.2 6.9 %collective-permute-start.1 = (f32[152,128]{1,0:T(8,128)}, f32[152,128]{1,0:T(8,128)S(1)}, u32[]{:S(2)}, u32[]{:S(2)}) collective-permute-start(f32[152,128]{1,0:T(8,128)} %get-tuple-element.29), channel_id=1, source_target_pairs={{0,24},{16,8},{24,0},{8,16},{1,25},{17,9},{25,1},{9,17},{2,26},{18... | collective-permute-start | bytes 233480 | tf_op jit(solution)/shard_map/ppermute | solution.py:808
  8.7 4.9 %collective-permute-start.2 = (f32[24,128]{1,0:T(8,128)}, f32[24,128]{1,0:T(8,128)S(1)}, u32[]{:S(2)}, u32[]{:S(2)}) collective-permute-start(f32[24,128]{1,0:T(8,128)} %get-tuple-element.33.refs_0_), channel_id=1, source_target_pairs={{0,16},{16,0},{24,8},{8,24},{1,17},{17,1},{25,9},{9,25},{2,18},{18... | collective-permute-start | bytes 36872 | tf_op jit(solution)/shard_map/ppermute | solution.py:809
  16.5 14.5 %collective-permute-start.5 = (f32[7,4,32,128]{3,2,1,0:T(8,128)}, f32[7,4,32,128]{3,2,1,0:T(8,128)S(1)}, u32[]{:S(2)}, u32[]{:S(2)}) collective-permute-start(f32[7,4,32,128]{3,2,1,0:T(8,128)} %get-tuple-element.40), channel_id=1, source_target_pairs={{0,8},{8,0},{16,24},{24,16},{1,9},{9,1},{17,25},{25,17},{2,10},{10... | collective-permute-start | bytes 1376264 | tf_op jit(solution)/shard_map/ppermute | solution.py:756
  17.0 14.0 %collective-permute-start.6 = (f32[7,4,32,128]{3,2,1,0:T(8,128)}, f32[7,4,32,128]{3,2,1,0:T(8,128)S(1)}, u32[]{:S(2)}, u32[]{:S(2)}) collective-permute-start(f32[7,4,32,128]{3,2,1,0:T(8,128)} %get-tuple-element.41), channel_id=1, source_target_pairs={{0,0},{8,16},{16,8},{24,24},{1,1},{9,17},{17,9},{25,25},{2,2},{10,... | collective-permute-start | bytes 1376264 | tf_op jit(solution)/shard_map/ppermute | solution.py:760
  18.7 10.2 %all-to-all-start = ((f32[8,24,128]{2,1,0:T(8,128)}), f32[8,24,128]{2,1,0:T(8,128)S(1)}, u32[]{:S(2)}, u32[]{:S(2)}) async-start(f32[8,24,128]{2,1,0:T(8,128)} %shard_map.178), calls=%async_computation | async-start | bytes 196608 | tf_op jit(solution)/shard_map/all_to_all | solution.py:826
  22.4 3.0 %collective-permute-start.3 = (f32[160,128]{1,0:T(8,128)S(1)}, f32[160,128]{1,0:T(8,128)S(1)}, u32[]{:S(2)}, u32[]{:S(2)}) collective-permute-start(f32[160,128]{1,0:T(8,128)S(1)} %get-tuple-element.37), channel_id=1, source_target_pairs={{0,1},{1,0},{2,3},{3,2},{4,5},{5,4},{6,7},{7,6},{8,9},{9,8},{10,11... | collective-permute-start | bytes 245768 | tf_op jit(solution)/shard_map/ppermute | solution.py:756
  22.9 6.0 %collective-permute-start.4 = (f32[160,128]{1,0:T(8,128)S(1)}, f32[160,128]{1,0:T(8,128)S(1)}, u32[]{:S(2)}, u32[]{:S(2)}) collective-permute-start(f32[160,128]{1,0:T(8,128)S(1)} %get-tuple-element.38), channel_id=1, source_target_pairs={{0,7},{1,2},{2,1},{3,4},{4,3},{5,6},{6,5},{7,0},{8,15},{9,10},{10,... | collective-permute-start | bytes 245768 | tf_op jit(solution)/shard_map/ppermute | solution.py:760
  28.9 22.1 %copy-start.1 = (bf16[2,512,256]{2,1,0:T(8,128)(2,1)S(1)}, bf16[2,512,256]{2,1,0:T(8,128)(2,1)}, u32[]{:S(2)}) copy-start(bf16[2,512,256]{2,1,0:T(8,128)(2,1)} %constant.21.clone.refs_1_) | copy-start | bytes 1572868
  28.9 22.1 %copy-start.2 = (f32[256,256]{1,0:T(8,128)S(1)}, f32[256,256]{1,0:T(8,128)}, u32[]{:S(2)}) copy-start(f32[256,256]{1,0:T(8,128)} %refs_7_.1) | copy-start | bytes 786436
  31.0 19.9 %copy-start.3 = (bf16[128,640]{1,0:T(8,128)(2,1)S(1)}, bf16[128,640]{1,0:T(8,128)(2,1)}, u32[]{:S(2)}) copy-start(bf16[128,640]{1,0:T(8,128)(2,1)} %constant.26.clone.refs_6_) | copy-start | bytes 491524
  31.0 20.0 %copy-start.4 = (bf16[640,128]{1,0:T(8,128)(2,1)S(1)}, bf16[640,128]{1,0:T(8,128)(2,1)}, u32[]{:S(2)}) copy-start(bf16[640,128]{1,0:T(8,128)(2,1)} %constant.25.clone.refs_5_) | copy-start | bytes 491524
  31.0 19.9 %all-to-all-start.1 = ((f32[32,32,128]{2,1,0:T(8,128)}), f32[32,32,128]{2,1,0:T(8,128)S(1)}, u32[]{:S(2)}, u32[]{:S(2)}) async-start(f32[32,32,128]{2,1,0:T(8,128)} %get-tuple-element.47), calls=%async_computation.1 | async-start | bytes 1048576 | tf_op jit(solution)/shard_map/all_to_all | solution.py:764
  38.0 22.5 %collective-permute-start.7 = (f32[7,20,8,128]{3,2,1,0:T(8,128)}, f32[7,20,8,128]{3,2,1,0:T(8,128)}, u32[]{:S(2)}, u32[]{:S(2)}) collective-permute-start(f32[7,20,8,128]{3,2,1,0:T(8,128)} %get-tuple-element.45), channel_id=1, source_target_pairs={{0,1},{1,0},{2,3},{3,2},{4,5},{5,4},{6,7},{7,6},{8,9},{9,8},{10,11... | collective-permute-start | bytes 1720328 | tf_op jit(solution)/shard_map/ppermute | solution.py:756
  38.3 22.2 %collective-permute-start.8 = (f32[7,20,8,128]{3,2,1,0:T(8,128)}, f32[7,20,8,128]{3,2,1,0:T(8,128)}, u32[]{:S(2)}, u32[]{:S(2)}) collective-permute-start(f32[7,20,8,128]{3,2,1,0:T(8,128)} %get-tuple-element.46), channel_id=1, source_target_pairs={{0,0},{1,2},{2,1},{3,4},{4,3},{5,6},{6,5},{7,7},{8,8},{9,10},{10,9... | collective-permute-start | bytes 1720328 | tf_op jit(solution)/shard_map/ppermute | solution.py:760
  57.4 15.3 %all-to-all-start.2 = ((f32[32,8,128]{2,1,0:T(8,128)}), f32[32,8,128]{2,1,0:T(8,128)S(1)}, u32[]{:S(2)}, u32[]{:S(2)}) async-start(f32[32,8,128]{2,1,0:T(8,128)} %get-tuple-element.50), calls=%async_computation.2 | async-start | bytes 262144 | tf_op jit(solution)/shard_map/all_to_all | solution.py:764
  60.4 12.2 %copy-start.8 = (f32[128,16]{0,1:T(8,128)S(1)}, f32[128,16]{0,1:T(8,128)}, u32[]{:S(2)}) copy-start(f32[128,16]{0,1:T(8,128)} %param.20) | copy-start | bytes 24580
  60.4 12.2 %copy-start.10 = (s32[128,2]{0,1:T(2,128)S(1)}, s32[128,2]{0,1:T(2,128)}, u32[]{:S(2)}) copy-start(s32[128,2]{0,1:T(2,128)} %param.22) | copy-start | bytes 3076
  60.5 12.2 %copy-start.11 = (s32[128,1]{0,1:T(1,128)S(1)}, s32[128,1]{0,1:T(1,128)}, u32[]{:S(2)}) copy-start(s32[128,1]{0,1:T(1,128)} %param.21) | copy-start | bytes 1540
